TPU v7x, 128 devices: a whole 4x4x4 slice. The times are simulated.
128 devices in a mesh: task: 4 (over y_hi, core), row: 32 (over x, y_lo, z).
Axes of the slice: x: 4, y: 4 (y_hi: 2, y_lo: 2; y = y_hi * 2 + y_lo), z: 4, core: 2. Of those that a mesh axis runs over, the one named last changes fastest.
Arguments:
- deltas: bfloat16 [8, 25600, 5120], P('task', 'row'), may hold values from -20 to 20, as said below
- sketch: bfloat16 [25600, 128], P('row'), may hold values from -0.0390625 to 0.0390625
Outputs:
- merged: bfloat16 [25600, 5120], P('row', 'task')
Inputs may be any that keep to these rules, and one draw needn't show every extreme that they name: Real-valued deltas; the tasks share part of their structure.
All inputs are finite; a program needn't handle non-finite values.
Results may differ from a plain program's by a relative error of at most 0.04.
Values may be sent and summed in bfloat16 or wider, within the bound.
No kernel may reach another device: no remote copies, remote signals or barrier semaphores. Data moves between devices by JAX's collectives and lax.ppermute only.
A program may use at most 128 MiB of HBM per device.

v0:
```python
import functools

import jax
import jax.numpy as jnp
from jax import lax
from jax.experimental import pallas as pl
from jax.experimental.pallas import tpu as pltpu
from jax.sharding import Mesh
from jax.sharding import PartitionSpec as P

NS_STEPS = 5
BF = jnp.bfloat16
F32 = jnp.float32
NS_BLOCK = 256
GRAM_BLOCK = 256
MIB = 1024 * 1024
RING_Y = ("yh", "yl")


def params(mib=24):
    return pltpu.CompilerParams(vmem_limit_bytes=mib * MIB)


def whole():
    return pl.BlockSpec(memory_space=pltpu.VMEM)


def shift(value, axis, step):
    size = lax.axis_size(axis)
    return lax.ppermute(value, axis, [(i, (i + step) % size) for i in range(size)])


def sketch_kernel(at_ref, deltas_ref, sketch_ref, *rest):
    outs, keep_ref, give_ref, rows_ref = rest[:10], rest[10], rest[11], rest[12]
    quarter = pl.program_id(0)
    rank = sketch_ref.shape[1]
    piece = rows_ref.shape[2]
    x, z = at_ref[0], at_ref[1]
    for task in range(2):
        part = lax.dot_general(
            sketch_ref[...], deltas_ref[task], (((0,), (0,)), ((), ())), preferred_element_type=F32
        )
        rows_ref[...] = part.astype(BF).T.reshape(4, 4, piece, rank)
        own, up, down, low, high = outs[5 * task : 5 * task + 5]
        for d in range(4):
            for e in range(4):
                over_x, over_z = (d, e) if task == 0 else (e, d)
                value = rows_ref[lax.rem(x + over_x, 4), lax.rem(z + over_z, 4)]
                if d == 2:
                    (low if e < 2 else high)[e % 2, quarter] = value
                else:
                    (own, up, None, down)[d][e, quarter] = value

    total = deltas_ref[0] + deltas_ref[1]
    mine = quarter % 2 == at_ref[3]

    @pl.when(mine)
    def _():
        keep_ref[0] = total

    @pl.when(jnp.logical_not(mine))
    def _():
        give_ref[0] = total


def sketch_call(at, deltas, sketch):
    tasks, rows, width = deltas.shape
    rank = sketch.shape[1]
    quarter = width // 4
    full, half = (4, 4, quarter // 16, rank), (2, 4, quarter // 16, rank)
    shapes = [full, full, full, half, half] * 2
    return pl.pallas_call(
        sketch_kernel,
        grid_spec=pltpu.PrefetchScalarGridSpec(
            num_scalar_prefetch=1,
            grid=(4,),
            in_specs=[
                pl.BlockSpec((tasks, rows, quarter), lambda i, at: (0, 0, i)),
                pl.BlockSpec((rows, rank), lambda i, at: (0, 0)),
            ],
            out_specs=[pl.BlockSpec(shape, lambda i, at: (0, 0, 0, 0)) for shape in shapes]
            + [pl.BlockSpec((1, rows, quarter), lambda i, at: (i // 2, 0, 0))] * 2,
            scratch_shapes=[pltpu.VMEM(full, BF)],
        ),
        out_shape=[jax.ShapeDtypeStruct(shape, BF) for shape in shapes]
        + [jax.ShapeDtypeStruct((2, rows, quarter), BF)] * 2,
        compiler_params=params(48),
        name="sketch",
    )(at, deltas, sketch)


def upper_blocks(size, block):
    return [(slice(i, i + block), slice(i, size)) for i in range(0, size, block)]


def mirror(out, rows, value, block):
    first = rows.start
    out[rows, first:] = value
    for j in range(block, value.shape[1], block):
        out[first + j : first + j + block, rows] = value[:, j : j + block].T


def pack_rows(refs, packed_ref):
    at = 0
    for ref in refs:
        count, rows, width = ref.shape
        packed_ref[at : at + count * rows, :] = ref[...].reshape(count * rows, width)
        at += count * rows


def place_rows(at_ref, blocks, basis_ref):
    x, z = at_ref[0], at_ref[1]
    for ref, chunk, outer, first in blocks:
        for j in range(ref.shape[0]):
            inner = (0, -1, 1, 2)[first + j]
            over_x, over_z = (inner, outer) if chunk == 0 else (outer, inner)
            basis_ref[chunk, lax.rem(x + over_x + 4, 4), lax.rem(z + over_z + 4, 4)] = ref[j]


def gram_first_kernel(at_ref, a0, a1, a2, b0, b1, b2, acc_ref, basis_ref, packed_ref):
    pack_rows([a0, a1, a2, b0, b1, b2], packed_ref)
    for rows, columns in upper_blocks(acc_ref.shape[0], GRAM_BLOCK):
        acc_ref[rows, columns] = lax.dot_general(
            packed_ref[:, rows], packed_ref[:, columns], (((0,), (0,)), ((), ())), preferred_element_type=F32
        )
    near = [(a0, 0, 0, 0), (a1, 0, -1, 0), (a2, 0, 1, 0), (b0, 1, 0, 0), (b1, 1, -1, 0), (b2, 1, 1, 0)]
    place_rows(at_ref, near, basis_ref)


def gram_first_call(at, parts):
    count, rows, width = parts[0].shape
    return pl.pallas_call(
        gram_first_kernel,
        in_specs=[pl.BlockSpec(memory_space=pltpu.SMEM)] + [whole()] * 6,
        out_specs=[whole()] * 2,
        out_shape=[
            jax.ShapeDtypeStruct((width, width), F32),
            jax.ShapeDtypeStruct((2, 4, 4, rows, width), BF),
        ],
        scratch_shapes=[pltpu.VMEM((6 * count * rows, width), BF)],
        cost_estimate=pl.CostEstimate(
            flops=8 * count * rows * width * width, bytes_accessed=8 * count * rows * width, transcendentals=0
        ),
        compiler_params=params(24),
        name="gram_first",
    )(at, *parts)


def gram_last_kernel(at_ref, a3, a4, b3, b4, acc_ref, near_ref, gram_ref, basis_ref, packed_ref):
    pack_rows([a3, a4, b3, b4], packed_ref)
    for rows, columns in upper_blocks(acc_ref.shape[0], GRAM_BLOCK):
        value = lax.dot_general(
            packed_ref[:, rows], packed_ref[:, columns], (((0,), (0,)), ((), ())), preferred_element_type=F32
        )
        mirror(gram_ref, rows, (acc_ref[rows, columns] + value).astype(BF), GRAM_BLOCK)
    basis_ref[...] = near_ref[...]
    place_rows(at_ref, [(a3, 0, 2, 0), (a4, 0, 2, 2), (b3, 1, 2, 0), (b4, 1, 2, 2)], basis_ref)


def gram_last_call(at, parts, acc, near):
    count, rows, width = parts[0].shape
    return pl.pallas_call(
        gram_last_kernel,
        in_specs=[pl.BlockSpec(memory_space=pltpu.SMEM)] + [whole()] * 6,
        out_specs=[whole()] * 2,
        out_shape=[
            jax.ShapeDtypeStruct((width, width), BF),
            jax.ShapeDtypeStruct(near.shape, BF),
        ],
        scratch_shapes=[pltpu.VMEM((4 * count * rows, width), BF)],
        compiler_params=params(24),
        name="gram_last",
    )(at, *parts, acc, near)


def coeff_kernel(at_ref, basis_ref, pool0_ref, pool1_ref, keep_ref, give_ref, chunk_ref):
    chunk_ref[...] = basis_ref[at_ref[2]]
    half, width = keep_ref.shape
    block = 256
    for out_ref, which in ((give_ref, 1 - at_ref[3]), (keep_ref, at_ref[3])):
        rows = pl.ds(pl.multiple_of(which * half, 16), half)
        for i in range(0, width, block):
            columns = slice(i, i + block)
            value = jnp.dot(pool0_ref[rows, :], basis_ref[0, :, columns], preferred_element_type=F32)
            value = value + jnp.dot(pool1_ref[rows, :], basis_ref[1, :, columns], preferred_element_type=F32)
            out_ref[:, columns] = value.astype(BF)


def coeff_call(at, basis, pooled):
    _, depth, width = basis.shape
    rows = pooled[0].shape[0]
    half = jax.ShapeDtypeStruct((rows // 2, width), BF)
    return pl.pallas_call(
        coeff_kernel,
        in_specs=[pl.BlockSpec(memory_space=pltpu.SMEM)] + [whole()] * 3,
        out_specs=[whole()] * 3,
        out_shape=[half, half, jax.ShapeDtypeStruct((depth, width), BF)],
        cost_estimate=pl.CostEstimate(
            flops=4 * rows * depth * width, bytes_accessed=4 * rows * depth, transcendentals=0
        ),
        compiler_params=params(20),
        name="coeff",
    )(at, basis, *pooled)


def diagonal(shape, first_row, first_col):
    row = lax.broadcasted_iota(jnp.int32, shape, 0) + first_row
    col = lax.broadcasted_iota(jnp.int32, shape, 1) + first_col
    return jnp.where(row == col, 3.0, 0.0)


def product(left, right, out, turn):
    for rows, columns in upper_blocks(left.shape[0], NS_BLOCK):
        value = jnp.dot(left[rows, :], right[:, columns], preferred_element_type=F32)
        if turn:
            value = (diagonal(value.shape, rows.start, columns.start) - value) * 0.5
        mirror(out, rows, value.astype(BF), NS_BLOCK)


def schulz_kernel(own_ref, other_ref, chunk_ref, z_ref, frob_ref, turned_ref, gram_ref, y_ref, t_ref, y2_ref, z2_ref):
    size = own_ref.shape[0]
    total = jnp.zeros((8, size), F32)
    for i in range(0, size, NS_BLOCK):
        rows = slice(i, i + NS_BLOCK)
        gram = own_ref[rows, :].astype(F32) + other_ref[rows, :].astype(F32)
        gram_ref[rows, :] = gram
        total = total + jnp.sum((gram * gram).reshape(NS_BLOCK // 8, 8, size), axis=0)
    frob = jnp.sqrt(jnp.sum(total, keepdims=True))
    frob_ref[...] = jnp.broadcast_to(frob, frob_ref.shape)
    scale = 1.0 / frob
    for i in range(0, size, NS_BLOCK):
        rows = slice(i, i + NS_BLOCK)
        y = (gram_ref[rows, :] * scale).astype(BF)
        y2_ref[rows, :] = y
        z_ref[rows, :] = ((diagonal(y.shape, i, 0) - y.astype(F32)) * 0.5).astype(BF)

    product(y2_ref, z_ref, y_ref, False)

    @pl.loop(1, NS_STEPS)
    def _(iteration):
        product(z_ref, y_ref, t_ref, True)
        product(t_ref, z_ref, z2_ref, False)
        z_ref[...] = z2_ref[...]

        @pl.when(iteration + 1 < NS_STEPS)
        def _():
            product(t_ref, y_ref, y2_ref, False)
            y_ref[...] = y2_ref[...]

    for i in range(0, chunk_ref.shape[0], NS_BLOCK):
        turned_ref[:, i : i + NS_BLOCK] = chunk_ref[i : i + NS_BLOCK, :].T


def schulz_call(own, other, chunk):
    size = own.shape[0]
    return pl.pallas_call(
        schulz_kernel,
        in_specs=[whole()] * 3,
        out_specs=[whole()] * 3,
        out_shape=[
            jax.ShapeDtypeStruct((size, size), BF),
            jax.ShapeDtypeStruct((8, 128), F32),
            jax.ShapeDtypeStruct(chunk.shape[::-1], BF),
        ],
        scratch_shapes=[pltpu.VMEM((size, size), F32)] + [pltpu.VMEM((size, size), BF)] * 4,
        cost_estimate=pl.CostEstimate(
            flops=24 * size**3, bytes_accessed=8 * size**2, transcendentals=0
        ),
        compiler_params=params(32),
        name="schulz",
    )(own, other, chunk)


def third_kernel(coeff_ref, z_ref, frob_ref, out_ref):
    second = jnp.dot(coeff_ref[...], z_ref[...], preferred_element_type=F32).astype(BF)
    third = jnp.dot(second, z_ref[...], preferred_element_type=F32)
    out_ref[...] = (third / frob_ref[0:1, 0:1]).astype(BF)


def third_call(coeff, z, frob):
    return pl.pallas_call(
        third_kernel,
        in_specs=[whole()] * 3,
        out_specs=whole(),
        out_shape=jax.ShapeDtypeStruct(coeff.shape, BF),
        compiler_params=params(),
        name="third",
    )(coeff, z, frob)


def merge_kernel(at_ref, third_ref, chunk_ref, *rest):
    out_ref = rest[-1]
    out_ref[...] = jnp.dot(third_ref[...], chunk_ref[...], preferred_element_type=F32).astype(BF)


def merge_call(at, third, chunk, so_far):
    rows, width = third.shape
    columns = chunk.shape[1]
    in_specs = [
        pl.BlockSpec((rows, width), lambda i, at: (0, 0)),
        pl.BlockSpec((width, columns), lambda i, at: (0, 0)),
    ]
    operands = [at, third, chunk]
    if so_far is None:
        place = lambda i, at: (at[3], 0)
    else:
        place = lambda i, at: (1 - at[3], 0)
        in_specs.append(pl.BlockSpec(memory_space=pl.ANY))
        operands.append(so_far)
    return pl.pallas_call(
        merge_kernel,
        grid_spec=pltpu.PrefetchScalarGridSpec(
            num_scalar_prefetch=1,
            grid=(1,),
            in_specs=in_specs,
            out_specs=pl.BlockSpec((rows, columns), place),
        ),
        out_shape=jax.ShapeDtypeStruct((2 * rows, columns), BF),
        input_output_aliases={3: 0} if so_far is not None else {},
        cost_estimate=pl.CostEstimate(
            flops=2 * rows * columns * width, bytes_accessed=2 * columns * width, transcendentals=0
        ),
        compiler_params=params(),
        name="merge",
    )(*operands)


def add(*values):
    return sum(value.astype(F32) for value in values).astype(BF)


def ring_reduce(pieces, axis):
    own, up, down, low, high = pieces
    low, high = shift(low, axis, 1), shift(high, axis, -1)
    cut = low.shape[0]
    up = lax.dynamic_update_slice(up, add(up[:cut], low), (0,) * up.ndim)
    down = lax.dynamic_update_slice(down, add(down[cut:], high), (cut,) + (0,) * (up.ndim - 1))
    from_below, from_above = shift(up, axis, 1), shift(down, axis, -1)
    return [add(own[e], from_below[e], from_above[e]) for e in range(own.shape[0])]


def direct_reduce(pieces, axis):
    return add(pieces[0], *[shift(piece, axis, step) for step, piece in enumerate(pieces) if step])


def ring_gather(items):
    near = [[a, shift(a, axis, 1), shift(a, axis, -1)] for a, axis in items]

    def second(near):
        out = []
        for (_, axis), (_, before, after) in zip(items, near):
            cut = before.shape[0] // 2
            out.append([shift(before[:cut], axis, 1), shift(after[cut:], axis, -1)])
        return out

    return near, second


def body(deltas, sketch):
    tasks, rows, width = deltas.shape
    core, yh, yl = lax.axis_index("core"), lax.axis_index("yh"), lax.axis_index("yl")
    x, z = lax.axis_index("x"), lax.axis_index("z")
    at, core0, yh0 = lax.optimization_barrier(
        (jnp.stack([x, z, yh, core]).astype(jnp.int32), core == 0, yh == 0)
    )

    *terms, pool_keep, pool_give = sketch_call(at, deltas, sketch)
    sum0 = ring_reduce(terms[:5], "x")
    sum1 = ring_reduce(terms[5:], "z")
    pool_got = shift(pool_give, "core", 1)
    sum0 = direct_reduce(sum0, "z")
    sum1 = direct_reduce(sum1, "x")

    piece, rank = sum0.shape[1:]
    both = jnp.concatenate([sum0, sum1], axis=2).reshape(2, 2, piece, 2 * rank)
    keep = jnp.where(core0, both[:, 0], both[:, 1])
    give = jnp.where(core0, both[:, 1], both[:, 0])
    got = shift(give, "core", 1)
    chip = jnp.concatenate(
        [jnp.where(core0, keep, got), jnp.where(core0, got, keep)], axis=2
    )
    pair = add(chip, shift(chip, "yl", 1))
    across = lax.ppermute(pair, RING_Y, [(0, 3), (3, 0), (1, 2), (2, 1)])
    local = jnp.concatenate(
        [jnp.where(yh0, pair, across), jnp.where(yh0, across, pair)], axis=2
    )

    near, _ = ring_gather([(local[0][None], "x"), (local[1][None], "z")])
    half = local.shape[2] // 2
    far = [
        jnp.concatenate([shift(n[1][..., :half], axis, 1), shift(n[2][..., half:], axis, -1)], axis=2)
        for n, axis in zip(near, ("x", "z"))
    ]
    items = [(jnp.concatenate([*n, f]), axis) for n, f, axis in zip(near, far, ("z", "x"))]
    near, second = ring_gather(items)
    pooled = [add(pool_keep[i], pool_got[i]) for i in range(2)]
    near, pooled = lax.optimization_barrier((near, pooled))
    far = second(near)
    acc, basis = gram_first_call(at, near[0] + near[1])
    far, acc, basis = lax.optimization_barrier((far, acc, basis))
    gram_own, basis = gram_last_call(at, far[0] + far[1], acc, basis)
    gram_other = shift(gram_own, "core", 1)
    mine, give, chunk = coeff_call(at, basis.reshape(2, width // 4, basis.shape[-1]), pooled)
    give, gram_own, gram_other = lax.optimization_barrier((give, gram_own, gram_other))
    twin = shift(give, "core", 1)
    chip_sum, gram_own, gram_other = lax.optimization_barrier((add(mine, twin), gram_own, gram_other))
    over = shift(chip_sum, "yh", 1)
    inverse_root, frob, chunk = schulz_call(gram_own, gram_other, chunk)
    over, inverse_root = lax.optimization_barrier((over, inverse_root))
    total_tasks = tasks * lax.axis_size("yh") * lax.axis_size("core")
    coeff = ((chip_sum.astype(F32) + over.astype(F32)) / total_tasks).astype(BF)

    third = third_call(coeff, inverse_root, frob)
    third_twin = shift(third, "core", 1)
    return merge_call(at, third_twin, chunk, merge_call(at, third, chunk, None))


def solution(mesh):
    fine = Mesh(mesh.devices.reshape(2, 2, 4, 2, 4), ("yh", "core", "x", "yl", "z"))
    task, row = ("yh", "core"), ("x", "yl", "z")
    return jax.shard_map(
        body,
        mesh=fine,
        in_specs=(P(task, row, None), P(row, None)),
        out_specs=P(row, task),
        check_vma=False,
    )
```

profile of v0, /device:TPU:1, one launch (start us, length us, event | category | flops | bytes accessed | tf_op | source)
XLA Modules:
  0.0 150.9 jit_solution(18083413135485246135)
XLA Ops:
  0.1 0.9 copy-done
  1.0 12.5 %sketch.1 = (bf16[4,4,80,128]{3,2,1,0:T(8,128)(2,1)S(1)}, bf16[4,4,80,128]{3,2,1,0:T(8,128)(2,1)S(1)}, bf16[4,4,80,128]{3,2,1,0:T(8,128)(2,1)S(1)}, bf16[2,4,80,...) custom-call(s32[4]{0:T(128)S(1)} %pad_add_fusion.at_ref, ...), custom_call_target="tpu_custom_call" | custom-call | tf_op jit(solution)/shard_map/sketch/pallas_call | solution.py:72
  13.6 4.6 %collective-permute-start.9 = (bf16[2,4,80,128]{3,2,1,0:T(8,128)(2,1)S(1)}, bf16[2,4,80,128]{3,2,1,0:T(8,128)(2,1)S(1)}, u32[]{:S(2)}, u32[]{:S(2)}) collective-permute-start(bf16[2,4,80,128]{3,2,1,0:T(8,128)(2,1)S(1)} %get-tuple-element.64), channel_id=1, source_target_pairs={{0,3},{1,0},{2,1},{3,2},{4,7},{5,4},{6,5},{7,6},{8,11},{9,8},{10,9... | collective-permute-start | bytes 491528 | tf_op jit(solution)/shard_map/ppermute | solution.py:30
  18.2 1.2 collective-permute-start
  19.4 1.5 collective-permute-start.2
  20.9 1.5 collective-permute-start.29
  22.4 3.0 %collective-permute-start.10 = (bf16[4,4,80,128]{3,2,1,0:T(8,128)(2,1)S(1)}, bf16[4,4,80,128]{3,2,1,0:T(8,128)(2,1)S(1)}, u32[]{:S(2)}, u32[]{:S(2)}) collective-permute-start(bf16[4,4,80,128]{3,2,1,0:T(8,128)(2,1)S(1)} %fusion.5), channel_id=1, source_target_pairs={{0,3},{1,0},{2,1},{3,2},{4,7},{5,4},{6,5},{7,6},{8,11},{9,8},{10,9... | collective-permute-start | bytes 983048 | tf_op jit(solution)/shard_map/ppermute | solution.py:30
  25.4 0.8 collective-permute-done.7
  26.4 0.1 fusion.3
  26.5 1.6 %collective-permute-start.3 = (bf16[4,4,80,128]{3,2,1,0:T(8,128)(2,1)S(1)}, bf16[4,4,80,128]{3,2,1,0:T(8,128)(2,1)S(1)}, u32[]{:S(2)}, u32[]{:S(2)}) collective-permute-start(bf16[4,4,80,128]{3,2,1,0:T(8,128)(2,1)S(1)} %fusion.3), channel_id=1, source_target_pairs={{0,24},{8,0},{16,8},{24,16},{1,25},{9,1},{17,9},{25,17},{2,26},{10... | collective-permute-start | bytes 983048 | tf_op jit(solution)/shard_map/ppermute | solution.py:30
  28.3 3.5 %collective-permute-done.10 = bf16[4,4,80,128]{3,2,1,0:T(8,128)(2,1)S(1)} collective-permute-done((bf16[4,4,80,128]{3,2,1,0:T(8,128)(2,1)S(1)}, bf16[4,4,80,128]{3,2,1,0:T(8,128)(2,1)S(1)}, u32[]{:S(2)}, u32[]{:S(2)}) %collective-permute-start.10) | collective-permute-done | bytes 327712 | tf_op jit(solution)/shard_map/ppermute | solution.py:30
  31.8 2.4 %collective-permute-done.8 = bf16[4,4,80,128]{3,2,1,0:T(8,128)(2,1)S(1)} collective-permute-done((bf16[4,4,80,128]{3,2,1,0:T(8,128)(2,1)S(1)}, bf16[4,4,80,128]{3,2,1,0:T(8,128)(2,1)S(1)}, u32[]{:S(2)}, u32[]{:S(2)}) %collective-permute-start.8) | collective-permute-done | bytes 327712 | tf_op jit(solution)/shard_map/ppermute | solution.py:30
  34.2 0.1 fusion.18
  34.3 2.7 %collective-permute-start.13 = (bf16[4,80,128]{2,1,0:T(8,128)(2,1)S(1)}, bf16[4,80,128]{2,1,0:T(8,128)(2,1)S(1)}, u32[]{:S(2)}, u32[]{:S(2)}) collective-permute-start(bf16[4,80,128]{2,1,0:T(8,128)(2,1)S(1)} %get-tuple-element.105), channel_id=1, source_target_pairs={{0,24},{8,0},{16,8},{24,16},{1,25},{9,1},{17,9},{25,17},{2,26},{10... | collective-permute-start | bytes 245768 | tf_op jit(solution)/shard_map/ppermute | solution.py:30
  37.0 0.4 collective-permute-start.12
  37.4 0.1 fusion.14
  37.6 2.5 %collective-permute-done.11 = bf16[4,80,128]{2,1,0:T(8,128)(2,1)S(1)} collective-permute-done((bf16[4,80,128]{2,1,0:T(8,128)(2,1)S(1)}, bf16[4,80,128]{2,1,0:T(8,128)(2,1)S(1)}, u32[]{:S(2)}, u32[]{:S(2)}) %collective-permute-start.11) | collective-permute-done | bytes 81952 | tf_op jit(solution)/shard_map/ppermute | solution.py:30
  40.1 1.0 collective-permute-start.6
  41.1 0.7 collective-permute-done.12
  41.9 0.5 collective-permute-done.4
  42.3 1.0 collective-permute-done.6
  43.4 2.8 %collective-permute-done.5 = bf16[4,80,128]{2,1,0:T(8,128)(2,1)S(1)} collective-permute-done((bf16[4,80,128]{2,1,0:T(8,128)(2,1)S(1)}, bf16[4,80,128]{2,1,0:T(8,128)(2,1)S(1)}, u32[]{:S(2)}, u32[]{:S(2)}) %collective-permute-start.5) | collective-permute-done | bytes 81952 | tf_op jit(solution)/shard_map/ppermute | solution.py:30
  46.3 5.1 %collective-permute-start.14 = (bf16[2,80,256]{2,1,0:T(8,128)(2,1)S(1)}, bf16[2,80,256]{2,1,0:T(8,128)(2,1)S(1)}, u32[]{:S(2)}, u32[]{:S(2)}) collective-permute-start(bf16[2,80,256]{2,1,0:T(8,128)(2,1)S(1)} %select_bitcast_fusion), channel_id=1, source_target_pairs={{0,32},{32,0},{1,33},{33,1},{2,34},{34,2},{3,35},{35,3},{4,36},{36... | collective-permute-start | bytes 245768 | tf_op jit(solution)/shard_map/ppermute | solution.py:30
  51.3 0.9 collective-permute-done.14
  52.3 1.4 collective-permute-start.15
  53.7 4.1 %collective-permute-done.15 = bf16[2,80,512]{2,1,0:T(8,128)(2,1)S(1)} collective-permute-done((bf16[2,80,512]{2,1,0:T(8,128)(2,1)S(1)}, bf16[2,80,512]{2,1,0:T(8,128)(2,1)S(1)}, u32[]{:S(2)}, u32[]{:S(2)}) %collective-permute-start.15) | collective-permute-done | bytes 163872 | tf_op jit(solution)/shard_map/ppermute | solution.py:30
  57.9 2.8 %collective-permute-start.16 = (bf16[2,80,512]{2,1,0:T(8,128)(2,1)S(1)}, bf16[2,80,512]{2,1,0:T(8,128)(2,1)S(1)}, u32[]{:S(2)}, u32[]{:S(2)}) collective-permute-start(bf16[2,80,512]{2,1,0:T(8,128)(2,1)S(1)} %add_convert_fusion.3), channel_id=1, source_target_pairs={{0,68},{68,0},{4,64},{64,4},{1,69},{69,1},{5,65},{65,5},{2,70},{70... | collective-permute-start | bytes 491528 | tf_op jit(solution)/shard_map/ppermute | solution.py:383
  60.7 3.1 %collective-permute-done.16 = bf16[2,80,512]{2,1,0:T(8,128)(2,1)S(1)} collective-permute-done((bf16[2,80,512]{2,1,0:T(8,128)(2,1)S(1)}, bf16[2,80,512]{2,1,0:T(8,128)(2,1)S(1)}, u32[]{:S(2)}, u32[]{:S(2)}) %collective-permute-start.16) | collective-permute-done | bytes 163872 | tf_op jit(solution)/shard_map/ppermute | solution.py:383
  63.9 1.4 collective-permute-start.18
  65.2 0.1 collective-permute-start.17
  65.4 1.0 collective-permute-start.24
  66.4 0.4 collective-permute-start.23
  66.9 1.2 collective-permute-done.18
  68.1 2.5 %collective-permute-start.20 = (bf16[1,80,512]{2,1,0:T(8,128)(2,1)S(1)}, bf16[1,80,512]{2,1,0:T(8,128)(2,1)S(1)}, u32[]{:S(2)}, u32[]{:S(2)}) collective-permute-start(bf16[1,80,512]{2,1,0:T(8,128)(2,1)S(1)} %slice.199), channel_id=1, source_target_pairs={{0,24},{8,0},{16,8},{24,16},{1,25},{9,1},{17,9},{25,17},{2,26},{10... | collective-permute-start | bytes 245768 | tf_op jit(solution)/shard_map/ppermute | solution.py:30
  70.8 1.4 collective-permute-start.26
  72.1 0.2 collective-permute-start.25
  72.4 3.1 %collective-permute-done.19 = bf16[1,80,512]{2,1,0:T(8,128)(2,1)S(1)} collective-permute-done((bf16[1,80,512]{2,1,0:T(8,128)(2,1)S(1)}, bf16[1,80,512]{2,1,0:T(8,128)(2,1)S(1)}, u32[]{:S(2)}, u32[]{:S(2)}) %collective-permute-start.19) | collective-permute-done | bytes 81952 | tf_op jit(solution)/shard_map/ppermute | solution.py:30
  75.5 0.3 collective-permute-start.22
  75.8 1.5 collective-permute-start.21
  77.3 1.2 collective-permute-start.28
  78.5 0.3 collective-permute-start.27
  78.8 1.1 fusion.1
  80.0 7.6 %collective-permute-done.22.a2 = bf16[4,80,1024]{2,1,0:T(8,128)(2,1)S(1)} collective-permute-done((bf16[4,80,1024]{2,1,0:T(8,128)(2,1)S(1)}, bf16[4,80,1024]{2,1,0:T(8,128)(2,1)S(1)}, u32[]{:S(2)}, u32[]{:S(2)}) %collective-permute-start.22) | collective-permute-done | bytes 655392 | tf_op jit(solution)/shard_map/ppermute | solution.py:30
  87.6 3.0 %collective-permute-done.21.a1 = bf16[4,80,1024]{2,1,0:T(8,128)(2,1)S(1)} collective-permute-done((bf16[4,80,1024]{2,1,0:T(8,128)(2,1)S(1)}, bf16[4,80,1024]{2,1,0:T(8,128)(2,1)S(1)}, u32[]{:S(2)}, u32[]{:S(2)}) %collective-permute-start.21) | collective-permute-done | bytes 655392 | tf_op jit(solution)/shard_map/ppermute | solution.py:30
  90.8 0.8 collective-permute-start.33
  91.6 0.7 collective-permute-start.32
  92.3 1.3 collective-permute-start.31
  93.6 0.2 collective-permute-start.30
  93.8 3.6 %gram_first.1 = (f32[1024,1024]{1,0:T(8,128)S(1)}, bf16[2,4,4,80,1024]{4,3,2,1,0:T(8,128)(2,1)S(1)}) custom-call(s32[4]{0:T(128)S(1)} %pad_add_fusion.at_ref, bf16[4,80,1024]{2,1,0:T(8,128)(2,1)S(1)} %maximum_maximum_fusion.a0, bf16[4,80,1024]{2,1,0:T(8,128)(2,1)S(1)} %collective-permute-done.21.a1, bf16[4,80,1024]{2,1,0:T(8,128)(2,1)S(1)} %collective-permute-done.22.a2, ...), custom_call_target="tpu_custom_call" | custom-call | flops 2684354560 | bytes 2621440 | tf_op jit(solution)/shard_map/gram_first/pallas_call | solution.py:132
  97.4 2.3 %collective-permute-done.32.b3 = bf16[2,80,1024]{2,1,0:T(8,128)(2,1)S(1)} collective-permute-done((bf16[2,80,1024]{2,1,0:T(8,128)(2,1)S(1)}, bf16[2,80,1024]{2,1,0:T(8,128)(2,1)S(1)}, u32[]{:S(2)}, u32[]{:S(2)}) %collective-permute-start.32) | collective-permute-done | bytes 327712 | tf_op jit(solution)/shard_map/ppermute | solution.py:30
  99.7 1.0 collective-permute-done.30.a3
  100.7 2.2 %gram_last.1 = (bf16[1024,1024]{1,0:T(8,128)(2,1)S(1)}, bf16[2,4,4,80,1024]{4,3,2,1,0:T(8,128)(2,1)S(1)}) custom-call(s32[4]{0:T(128)S(1)} %pad_add_fusion.at_ref, bf16[2,80,1024]{2,1,0:T(8,128)(2,1)S(1)} %collective-permute-done.30.a3, bf16[2,80,1024]{2,1,0:T(8,128)(2,1)S(1)} %collective-permute-done.31.a4, ...), custom_call_target="tpu_custom_call" | custom-call | tf_op jit(solution)/shard_map/gram_last/pallas_call | solution.py:162
  102.9 8.9 %collective-permute-start.34 = (bf16[1024,1024]{1,0:T(8,128)(2,1)S(1)}, bf16[1024,1024]{1,0:T(8,128)(2,1)S(1)}, u32[]{:S(2)}, u32[]{:S(2)}) collective-permute-start(bf16[1024,1024]{1,0:T(8,128)(2,1)S(1)} %get-tuple-element.91.own_ref), channel_id=1, source_target_pairs={{0,32},{32,0},{1,33},{33,1},{2,34},{34,2},{3,35},{35,3},{4,36},{36... | collective-permute-start | bytes 6291464 | tf_op jit(solution)/shard_map/ppermute | solution.py:30
  111.9 5.1 %coeff.1 = (bf16[400,1024]{1,0:T(8,128)(2,1)S(1)}, bf16[400,1024]{1,0:T(8,128)(2,1)S(1)}, bf16[1280,1024]{1,0:T(8,128)(2,1)S(1)}) custom-call(s32[4]{0:T(128)S(1)} %pad_add_fusion.at_ref, bf16[2,1280,1024]{2,1,0:T(8,128)(2,1)S(1)} %bitcast.57, bf16[800,1280]{1,0:T(8,128)(2,1)S(1)} %get-tuple-element.82.pool0_ref, ...), custom_call_target="tpu_custom_call" | custom-call | flops 4194304000 | bytes 4096000 | tf_op jit(solution)/shard_map/coeff/pallas_call | solution.py:193
  117.0 0.3 collective-permute-start.35
  117.3 2.3 %collective-permute-done.35 = bf16[400,1024]{1,0:T(8,128)(2,1)S(1)} collective-permute-done((bf16[400,1024]{1,0:T(8,128)(2,1)S(1)}, bf16[400,1024]{1,0:T(8,128)(2,1)S(1)}, u32[]{:S(2)}, u32[]{:S(2)}) %collective-permute-start.35) | collective-permute-done | bytes 819232 | tf_op jit(solution)/shard_map/ppermute | solution.py:30
  119.6 0.3 add_convert_fusion.2
  120.0 1.7 %collective-permute-start.36 = (bf16[400,1024]{1,0:T(8,128)(2,1)S(1)}, bf16[400,1024]{1,0:T(8,128)(2,1)S(1)}, u32[]{:S(2)}, u32[]{:S(2)}) collective-permute-start(bf16[400,1024]{1,0:T(8,128)(2,1)S(1)} %add_convert_fusion.2), channel_id=1, source_target_pairs={{0,64},{64,0},{1,65},{65,1},{2,66},{66,2},{3,67},{67,3},{4,68},{68... | collective-permute-start | bytes 2457608 | tf_op jit(solution)/shard_map/ppermute | solution.py:30
  121.7 21.1 %schulz.1 = (bf16[1024,1024]{1,0:T(8,128)(2,1)S(1)}, f32[8,128]{1,0:T(8,128)S(1)}, bf16[1024,1280]{1,0:T(8,128)(2,1)S(1)}) custom-call(bf16[1024,1024]{1,0:T(8,128)(2,1)S(1)} %get-tuple-element.91.own_ref, bf16[1024,1024]{1,0:T(8,128)(2,1)S(1)} %collective-permute-done.34.other_ref, bf16[1280,1024]{1,0:T(8,128)(2,1)S(1)} %get-tuple-element.93.chunk_ref), custom_call_target="tpu_custom_call" | custom-call | flops 25769803776 | bytes 8388608 | tf_op jit(solution)/shard_map/schulz/pallas_call | solution.py:256
  142.7 0.3 multiply_convert_fusion.coeff_ref
  143.1 1.9 %third.1.third_ref = bf16[400,1024]{1,0:T(8,128)(2,1)S(1)} custom-call(bf16[400,1024]{1,0:T(8,128)(2,1)S(1)} %multiply_convert_fusion.coeff_ref, bf16[1024,1024]{1,0:T(8,128)(2,1)S(1)} %get-tuple-element.96.z_ref, f32[8,128]{1,0:T(8,128)S(1)} %get-tuple-element.97.frob_ref), custom_call_target="tpu_custom_call" | custom-call | tf_op jit(solution)/shard_map/third/pallas_call | solution.py:281
  144.9 0.5 collective-permute-start.37
  145.4 2.7 %merge.2.rest_0_ = bf16[800,1280]{1,0:T(8,128)(2,1)} custom-call(s32[4]{0:T(128)S(1)} %pad_add_fusion.at_ref, bf16[400,1024]{1,0:T(8,128)(2,1)S(1)} %third.1.third_ref, bf16[1024,1280]{1,0:T(8,128)(2,1)S(1)} %get-tuple-element.98.chunk_ref), custom_call_target="tpu_custom_call" | custom-call | flops 1048576000 | bytes 2621440 | tf_op jit(solution)/shard_map/merge/pallas_call | solution.py:310
  148.2 2.7 %merge.3 = bf16[800,1280]{1,0:T(8,128)(2,1)} custom-call(s32[4]{0:T(128)S(1)} %pad_add_fusion.at_ref, bf16[400,1024]{1,0:T(8,128)(2,1)S(1)} %collective-permute-done.37.third_ref, bf16[1024,1280]{1,0:T(8,128)(2,1)S(1)} %get-tuple-element.98.chunk_ref, bf16[800,1280]{1,0:T(8,128)(2,1)} %merge.2.rest_0_), custom_call_target="tpu_custom_call", output_to_operand_aliasing={{}: (3, {})} | custom-call | flops 1048576000 | bytes 2621440 | tf_op jit(solution)/shard_map/merge/pallas_call | solution.py:310
  (53 shorter events, 1.3 us)
Async XLA Ops:
  0.1 0.9 copy-start
  13.6 8.8 %collective-permute-start.9 = (bf16[2,4,80,128]{3,2,1,0:T(8,128)(2,1)S(1)}, bf16[2,4,80,128]{3,2,1,0:T(8,128)(2,1)S(1)}, u32[]{:S(2)}, u32[]{:S(2)}) collective-permute-start(bf16[2,4,80,128]{3,2,1,0:T(8,128)(2,1)S(1)} %get-tuple-element.64), channel_id=1, source_target_pairs={{0,3},{1,0},{2,1},{3,2},{4,7},{5,4},{6,5},{7,6},{8,11},{9,8},{10,9... | collective-permute-start | bytes 491528 | tf_op jit(solution)/shard_map/ppermute | solution.py:30
  18.2 10.0 %collective-permute-start = (bf16[2,4,80,128]{3,2,1,0:T(8,128)(2,1)S(1)}, bf16[2,4,80,128]{3,2,1,0:T(8,128)(2,1)S(1)}, u32[]{:S(2)}, u32[]{:S(2)}) collective-permute-start(bf16[2,4,80,128]{3,2,1,0:T(8,128)(2,1)S(1)} %get-tuple-element.57), channel_id=1, source_target_pairs={{0,8},{8,16},{16,24},{24,0},{1,9},{9,17},{17,25},{25,1},{2,10},{10... | collective-permute-start | bytes 491528 | tf_op jit(solution)/shard_map/ppermute | solution.py:30
  19.4 7.0 %collective-permute-start.2 = (bf16[2,4,80,128]{3,2,1,0:T(8,128)(2,1)S(1)}, bf16[2,4,80,128]{3,2,1,0:T(8,128)(2,1)S(1)}, u32[]{:S(2)}, u32[]{:S(2)}) collective-permute-start(bf16[2,4,80,128]{3,2,1,0:T(8,128)(2,1)S(1)} %get-tuple-element.59), channel_id=1, source_target_pairs={{0,24},{8,0},{16,8},{24,16},{1,25},{9,1},{17,9},{25,17},{2,26},{10... | collective-permute-start | bytes 491528 | tf_op jit(solution)/shard_map/ppermute | solution.py:30
  20.9 5.4 %collective-permute-start.7 = (bf16[2,4,80,128]{3,2,1,0:T(8,128)(2,1)S(1)}, bf16[2,4,80,128]{3,2,1,0:T(8,128)(2,1)S(1)}, u32[]{:S(2)}, u32[]{:S(2)}) collective-permute-start(bf16[2,4,80,128]{3,2,1,0:T(8,128)(2,1)S(1)} %get-tuple-element.62), channel_id=1, source_target_pairs={{0,1},{1,2},{2,3},{3,0},{4,5},{5,6},{6,7},{7,4},{8,9},{9,10},{10,1... | collective-permute-start | bytes 491528 | tf_op jit(solution)/shard_map/ppermute | solution.py:30
  20.9 58.0 %collective-permute-start.29 = (bf16[2,800,1280]{2,1,0:T(8,128)(2,1)}, bf16[2,800,1280]{2,1,0:T(8,128)(2,1)S(1)}, u32[]{:S(2)}, u32[]{:S(2)}) collective-permute-start(bf16[2,800,1280]{2,1,0:T(8,128)(2,1)} %get-tuple-element.66), channel_id=1, source_target_pairs={{0,32},{32,0},{1,33},{33,1},{2,34},{34,2},{3,35},{35,3},{4,36},{36... | collective-permute-start | bytes 12288008 | tf_op jit(solution)/shard_map/ppermute | solution.py:30
  22.4 9.4 %collective-permute-start.10 = (bf16[4,4,80,128]{3,2,1,0:T(8,128)(2,1)S(1)}, bf16[4,4,80,128]{3,2,1,0:T(8,128)(2,1)S(1)}, u32[]{:S(2)}, u32[]{:S(2)}) collective-permute-start(bf16[4,4,80,128]{3,2,1,0:T(8,128)(2,1)S(1)} %fusion.5), channel_id=1, source_target_pairs={{0,3},{1,0},{2,1},{3,2},{4,7},{5,4},{6,5},{7,6},{8,11},{9,8},{10,9... | collective-permute-start | bytes 983048 | tf_op jit(solution)/shard_map/ppermute | solution.py:30
  26.3 7.8 %collective-permute-start.8 = (bf16[4,4,80,128]{3,2,1,0:T(8,128)(2,1)S(1)}, bf16[4,4,80,128]{3,2,1,0:T(8,128)(2,1)S(1)}, u32[]{:S(2)}, u32[]{:S(2)}) collective-permute-start(bf16[4,4,80,128]{3,2,1,0:T(8,128)(2,1)S(1)} %fusion.4), channel_id=1, source_target_pairs={{0,1},{1,2},{2,3},{3,0},{4,5},{5,6},{6,7},{7,4},{8,9},{9,10},{10,1... | collective-permute-start | bytes 983048 | tf_op jit(solution)/shard_map/ppermute | solution.py:30
  26.5 10.5 %collective-permute-start.3 = (bf16[4,4,80,128]{3,2,1,0:T(8,128)(2,1)S(1)}, bf16[4,4,80,128]{3,2,1,0:T(8,128)(2,1)S(1)}, u32[]{:S(2)}, u32[]{:S(2)}) collective-permute-start(bf16[4,4,80,128]{3,2,1,0:T(8,128)(2,1)S(1)} %fusion.3), channel_id=1, source_target_pairs={{0,24},{8,0},{16,8},{24,16},{1,25},{9,1},{17,9},{25,17},{2,26},{10... | collective-permute-start | bytes 983048 | tf_op jit(solution)/shard_map/ppermute | solution.py:30
  28.2 9.2 %collective-permute-start.1 = (bf16[4,4,80,128]{3,2,1,0:T(8,128)(2,1)S(1)}, bf16[4,4,80,128]{3,2,1,0:T(8,128)(2,1)S(1)}, u32[]{:S(2)}, u32[]{:S(2)}) collective-permute-start(bf16[4,4,80,128]{3,2,1,0:T(8,128)(2,1)S(1)} %fusion.2), channel_id=1, source_target_pairs={{0,8},{8,16},{16,24},{24,0},{1,9},{9,17},{17,25},{25,1},{2,10},{10... | collective-permute-start | bytes 983048 | tf_op jit(solution)/shard_map/ppermute | solution.py:30
  34.3 5.8 %collective-permute-start.11 = (bf16[4,80,128]{2,1,0:T(8,128)(2,1)S(1)}, bf16[4,80,128]{2,1,0:T(8,128)(2,1)S(1)}, u32[]{:S(2)}, u32[]{:S(2)}) collective-permute-start(bf16[4,80,128]{2,1,0:T(8,128)(2,1)S(1)} %get-tuple-element.104), channel_id=1, source_target_pairs={{0,8},{8,16},{16,24},{24,0},{1,9},{9,17},{17,25},{25,1},{2,10},{10... | collective-permute-start | bytes 245768 | tf_op jit(solution)/shard_map/ppermute | solution.py:30
  34.3 6.7 %collective-permute-start.13 = (bf16[4,80,128]{2,1,0:T(8,128)(2,1)S(1)}, bf16[4,80,128]{2,1,0:T(8,128)(2,1)S(1)}, u32[]{:S(2)}, u32[]{:S(2)}) collective-permute-start(bf16[4,80,128]{2,1,0:T(8,128)(2,1)S(1)} %get-tuple-element.105), channel_id=1, source_target_pairs={{0,24},{8,0},{16,8},{24,16},{1,25},{9,1},{17,9},{25,17},{2,26},{10... | collective-permute-start | bytes 245768 | tf_op jit(solution)/shard_map/ppermute | solution.py:30
  37.0 4.8 %collective-permute-start.12 = (bf16[4,80,128]{2,1,0:T(8,128)(2,1)S(1)}, bf16[4,80,128]{2,1,0:T(8,128)(2,1)S(1)}, u32[]{:S(2)}, u32[]{:S(2)}) collective-permute-start(bf16[4,80,128]{2,1,0:T(8,128)(2,1)S(1)} %get-tuple-element.106), channel_id=1, source_target_pairs={{0,16},{8,24},{16,0},{24,8},{1,17},{9,25},{17,1},{25,9},{2,18},{10... | collective-permute-start | bytes 245768 | tf_op jit(solution)/shard_map/ppermute | solution.py:30
  37.5 4.9 %collective-permute-start.4 = (bf16[4,80,128]{2,1,0:T(8,128)(2,1)S(1)}, bf16[4,80,128]{2,1,0:T(8,128)(2,1)S(1)}, u32[]{:S(2)}, u32[]{:S(2)}) collective-permute-start(bf16[4,80,128]{2,1,0:T(8,128)(2,1)S(1)} %get-tuple-element.101), channel_id=1, source_target_pairs={{0,1},{1,2},{2,3},{3,0},{4,5},{5,6},{6,7},{7,4},{8,9},{9,10},{10,1... | collective-permute-start | bytes 245768 | tf_op jit(solution)/shard_map/ppermute | solution.py:30
  40.1 3.3 %collective-permute-start.6 = (bf16[4,80,128]{2,1,0:T(8,128)(2,1)S(1)}, bf16[4,80,128]{2,1,0:T(8,128)(2,1)S(1)}, u32[]{:S(2)}, u32[]{:S(2)}) collective-permute-start(bf16[4,80,128]{2,1,0:T(8,128)(2,1)S(1)} %get-tuple-element.102), channel_id=1, source_target_pairs={{0,3},{1,0},{2,1},{3,2},{4,7},{5,4},{6,5},{7,6},{8,11},{9,8},{10,9... | collective-permute-start | bytes 245768 | tf_op jit(solution)/shard_map/ppermute | solution.py:30
  41.1 5.1 %collective-permute-start.5 = (bf16[4,80,128]{2,1,0:T(8,128)(2,1)S(1)}, bf16[4,80,128]{2,1,0:T(8,128)(2,1)S(1)}, u32[]{:S(2)}, u32[]{:S(2)}) collective-permute-start(bf16[4,80,128]{2,1,0:T(8,128)(2,1)S(1)} %get-tuple-element.103), channel_id=1, source_target_pairs={{0,2},{1,3},{2,0},{3,1},{4,6},{5,7},{6,4},{7,5},{8,10},{9,11},{10,... | collective-permute-start | bytes 245768 | tf_op jit(solution)/shard_map/ppermute | solution.py:30
  46.3 6.0 %collective-permute-start.14 = (bf16[2,80,256]{2,1,0:T(8,128)(2,1)S(1)}, bf16[2,80,256]{2,1,0:T(8,128)(2,1)S(1)}, u32[]{:S(2)}, u32[]{:S(2)}) collective-permute-start(bf16[2,80,256]{2,1,0:T(8,128)(2,1)S(1)} %select_bitcast_fusion), channel_id=1, source_target_pairs={{0,32},{32,0},{1,33},{33,1},{2,34},{34,2},{3,35},{35,3},{4,36},{36... | collective-permute-start | bytes 245768 | tf_op jit(solution)/shard_map/ppermute | solution.py:30
  52.3 5.5 %collective-permute-start.15 = (bf16[2,80,512]{2,1,0:T(8,128)(2,1)S(1)}, bf16[2,80,512]{2,1,0:T(8,128)(2,1)S(1)}, u32[]{:S(2)}, u32[]{:S(2)}) collective-permute-start(bf16[2,80,512]{2,1,0:T(8,128)(2,1)S(1)} %pad_maximum_fusion.2), channel_id=1, source_target_pairs={{0,4},{4,0},{1,5},{5,1},{2,6},{6,2},{3,7},{7,3},{8,12},{12,8},{9,1... | collective-permute-start | bytes 491528 | tf_op jit(solution)/shard_map/ppermute | solution.py:30
  57.9 5.9 %collective-permute-start.16 = (bf16[2,80,512]{2,1,0:T(8,128)(2,1)S(1)}, bf16[2,80,512]{2,1,0:T(8,128)(2,1)S(1)}, u32[]{:S(2)}, u32[]{:S(2)}) collective-permute-start(bf16[2,80,512]{2,1,0:T(8,128)(2,1)S(1)} %add_convert_fusion.3), channel_id=1, source_target_pairs={{0,68},{68,0},{4,64},{64,4},{1,69},{69,1},{5,65},{65,5},{2,70},{70... | collective-permute-start | bytes 491528 | tf_op jit(solution)/shard_map/ppermute | solution.py:383
  63.8 15.1 %copy-start.1 = (bf16[2,800,1280]{2,1,0:T(8,128)(2,1)S(1)}, bf16[2,800,1280]{2,1,0:T(8,128)(2,1)}, u32[]{:S(2)}) copy-start(bf16[2,800,1280]{2,1,0:T(8,128)(2,1)} %get-tuple-element.65) | copy-start | bytes 12288004
  63.9 4.2 %collective-permute-start.18 = (bf16[1,80,1024]{2,1,0:T(8,128)(2,1)S(1)}, bf16[1,80,1024]{2,1,0:T(8,128)(2,1)S(1)}, u32[]{:S(2)}, u32[]{:S(2)}) collective-permute-start(bf16[1,80,1024]{2,1,0:T(8,128)(2,1)S(1)} %get-tuple-element.108), channel_id=1, source_target_pairs={{0,24},{8,0},{16,8},{24,16},{1,25},{9,1},{17,9},{25,17},{2,26},{10... | collective-permute-start | bytes 491528 | tf_op jit(solution)/shard_map/ppermute | solution.py:30
  65.2 5.4 %collective-permute-start.17 = (bf16[1,80,1024]{2,1,0:T(8,128)(2,1)S(1)}, bf16[1,80,1024]{2,1,0:T(8,128)(2,1)S(1)}, u32[]{:S(2)}, u32[]{:S(2)}) collective-permute-start(bf16[1,80,1024]{2,1,0:T(8,128)(2,1)S(1)} %get-tuple-element.108), channel_id=1, source_target_pairs={{0,8},{8,16},{16,24},{24,0},{1,9},{9,17},{17,25},{25,1},{2,10},{10... | collective-permute-start | bytes 491528 | tf_op jit(solution)/shard_map/ppermute | solution.py:30
  65.4 5.3 %collective-permute-start.24 = (bf16[1,80,1024]{2,1,0:T(8,128)(2,1)S(1)}, bf16[1,80,1024]{2,1,0:T(8,128)(2,1)S(1)}, u32[]{:S(2)}, u32[]{:S(2)}) collective-permute-start(bf16[1,80,1024]{2,1,0:T(8,128)(2,1)S(1)} %get-tuple-element.107), channel_id=1, source_target_pairs={{0,3},{1,0},{2,1},{3,2},{4,7},{5,4},{6,5},{7,6},{8,11},{9,8},{10,9... | collective-permute-start | bytes 491528 | tf_op jit(solution)/shard_map/ppermute | solution.py:30
  66.4 5.7 %collective-permute-start.23 = (bf16[1,80,1024]{2,1,0:T(8,128)(2,1)S(1)}, bf16[1,80,1024]{2,1,0:T(8,128)(2,1)S(1)}, u32[]{:S(2)}, u32[]{:S(2)}) collective-permute-start(bf16[1,80,1024]{2,1,0:T(8,128)(2,1)S(1)} %get-tuple-element.107), channel_id=1, source_target_pairs={{0,1},{1,2},{2,3},{3,0},{4,5},{5,6},{6,7},{7,4},{8,9},{9,10},{10,1... | collective-permute-start | bytes 491528 | tf_op jit(solution)/shard_map/ppermute | solution.py:30
  68.1 4.3 %collective-permute-start.20 = (bf16[1,80,512]{2,1,0:T(8,128)(2,1)S(1)}, bf16[1,80,512]{2,1,0:T(8,128)(2,1)S(1)}, u32[]{:S(2)}, u32[]{:S(2)}) collective-permute-start(bf16[1,80,512]{2,1,0:T(8,128)(2,1)S(1)} %slice.199), channel_id=1, source_target_pairs={{0,24},{8,0},{16,8},{24,16},{1,25},{9,1},{17,9},{25,17},{2,26},{10... | collective-permute-start | bytes 245768 | tf_op jit(solution)/shard_map/ppermute | solution.py:30
  70.7 4.8 %collective-permute-start.19 = (bf16[1,80,512]{2,1,0:T(8,128)(2,1)S(1)}, bf16[1,80,512]{2,1,0:T(8,128)(2,1)S(1)}, u32[]{:S(2)}, u32[]{:S(2)}) collective-permute-start(bf16[1,80,512]{2,1,0:T(8,128)(2,1)S(1)} %slice.198), channel_id=1, source_target_pairs={{0,8},{8,16},{16,24},{24,0},{1,9},{9,17},{17,25},{25,1},{2,10},{10... | collective-permute-start | bytes 245768 | tf_op jit(solution)/shard_map/ppermute | solution.py:30
  70.8 6.5 %collective-permute-start.26 = (bf16[1,80,512]{2,1,0:T(8,128)(2,1)S(1)}, bf16[1,80,512]{2,1,0:T(8,128)(2,1)S(1)}, u32[]{:S(2)}, u32[]{:S(2)}) collective-permute-start(bf16[1,80,512]{2,1,0:T(8,128)(2,1)S(1)} %slice.201), channel_id=1, source_target_pairs={{0,3},{1,0},{2,1},{3,2},{4,7},{5,4},{6,5},{7,6},{8,11},{9,8},{10,9... | collective-permute-start | bytes 245768 | tf_op jit(solution)/shard_map/ppermute | solution.py:30
  72.1 5.1 %collective-permute-start.25 = (bf16[1,80,512]{2,1,0:T(8,128)(2,1)S(1)}, bf16[1,80,512]{2,1,0:T(8,128)(2,1)S(1)}, u32[]{:S(2)}, u32[]{:S(2)}) collective-permute-start(bf16[1,80,512]{2,1,0:T(8,128)(2,1)S(1)} %slice.200), channel_id=1, source_target_pairs={{0,1},{1,2},{2,3},{3,0},{4,5},{5,6},{6,7},{7,4},{8,9},{9,10},{10,1... | collective-permute-start | bytes 245768 | tf_op jit(solution)/shard_map/ppermute | solution.py:30
  75.5 12.1 %collective-permute-start.22 = (bf16[4,80,1024]{2,1,0:T(8,128)(2,1)S(1)}, bf16[4,80,1024]{2,1,0:T(8,128)(2,1)S(1)}, u32[]{:S(2)}, u32[]{:S(2)}) collective-permute-start(bf16[4,80,1024]{2,1,0:T(8,128)(2,1)S(1)} %maximum_maximum_fusion.a0), channel_id=1, source_target_pairs={{0,3},{1,0},{2,1},{3,2},{4,7},{5,4},{6,5},{7,6},{8,11},{9,8},{10,9... | collective-permute-start | bytes 1966088 | tf_op jit(solution)/shard_map/ppermute | solution.py:30
  75.8 14.9 %collective-permute-start.21 = (bf16[4,80,1024]{2,1,0:T(8,128)(2,1)S(1)}, bf16[4,80,1024]{2,1,0:T(8,128)(2,1)S(1)}, u32[]{:S(2)}, u32[]{:S(2)}) collective-permute-start(bf16[4,80,1024]{2,1,0:T(8,128)(2,1)S(1)} %maximum_maximum_fusion.a0), channel_id=1, source_target_pairs={{0,1},{1,2},{2,3},{3,0},{4,5},{5,6},{6,7},{7,4},{8,9},{9,10},{10,1... | collective-permute-start | bytes 1966088 | tf_op jit(solution)/shard_map/ppermute | solution.py:30
  77.3 13.3 %collective-permute-start.28 = (bf16[4,80,1024]{2,1,0:T(8,128)(2,1)S(1)}, bf16[4,80,1024]{2,1,0:T(8,128)(2,1)S(1)}, u32[]{:S(2)}, u32[]{:S(2)}) collective-permute-start(bf16[4,80,1024]{2,1,0:T(8,128)(2,1)S(1)} %maximum_maximum_fusion.1.b0), channel_id=1, source_target_pairs={{0,24},{8,0},{16,8},{24,16},{1,25},{9,1},{17,9},{25,17},{2,26},{10... | collective-permute-start | bytes 1966088 | tf_op jit(solution)/shard_map/ppermute | solution.py:30
  78.5 12.1 %collective-permute-start.27 = (bf16[4,80,1024]{2,1,0:T(8,128)(2,1)S(1)}, bf16[4,80,1024]{2,1,0:T(8,128)(2,1)S(1)}, u32[]{:S(2)}, u32[]{:S(2)}) collective-permute-start(bf16[4,80,1024]{2,1,0:T(8,128)(2,1)S(1)} %maximum_maximum_fusion.1.b0), channel_id=1, source_target_pairs={{0,8},{8,16},{16,24},{24,0},{1,9},{9,17},{17,25},{25,1},{2,10},{10... | collective-permute-start | bytes 1966088 | tf_op jit(solution)/shard_map/ppermute | solution.py:30
  90.8 6.6 %collective-permute-start.33 = (bf16[2,80,1024]{2,1,0:T(8,128)(2,1)S(1)}, bf16[2,80,1024]{2,1,0:T(8,128)(2,1)S(1)}, u32[]{:S(2)}, u32[]{:S(2)}) collective-permute-start(bf16[2,80,1024]{2,1,0:T(8,128)(2,1)S(1)} %slice.177), channel_id=1, source_target_pairs={{0,24},{8,0},{16,8},{24,16},{1,25},{9,1},{17,9},{25,17},{2,26},{10... | collective-permute-start | bytes 983048 | tf_op jit(solution)/shard_map/ppermute | solution.py:30
  91.6 8.1 %collective-permute-start.32 = (bf16[2,80,1024]{2,1,0:T(8,128)(2,1)S(1)}, bf16[2,80,1024]{2,1,0:T(8,128)(2,1)S(1)}, u32[]{:S(2)}, u32[]{:S(2)}) collective-permute-start(bf16[2,80,1024]{2,1,0:T(8,128)(2,1)S(1)} %slice.176), channel_id=1, source_target_pairs={{0,8},{8,16},{16,24},{24,0},{1,9},{9,17},{17,25},{25,1},{2,10},{10... | collective-permute-start | bytes 983048 | tf_op jit(solution)/shard_map/ppermute | solution.py:30
  92.3 7.4 %collective-permute-start.31 = (bf16[2,80,1024]{2,1,0:T(8,128)(2,1)S(1)}, bf16[2,80,1024]{2,1,0:T(8,128)(2,1)S(1)}, u32[]{:S(2)}, u32[]{:S(2)}) collective-permute-start(bf16[2,80,1024]{2,1,0:T(8,128)(2,1)S(1)} %slice.175), channel_id=1, source_target_pairs={{0,3},{1,0},{2,1},{3,2},{4,7},{5,4},{6,5},{7,6},{8,11},{9,8},{10,9... | collective-permute-start | bytes 983048 | tf_op jit(solution)/shard_map/ppermute | solution.py:30
  93.6 7.1 %collective-permute-start.30 = (bf16[2,80,1024]{2,1,0:T(8,128)(2,1)S(1)}, bf16[2,80,1024]{2,1,0:T(8,128)(2,1)S(1)}, u32[]{:S(2)}, u32[]{:S(2)}) collective-permute-start(bf16[2,80,1024]{2,1,0:T(8,128)(2,1)S(1)} %slice.174), channel_id=1, source_target_pairs={{0,1},{1,2},{2,3},{3,0},{4,5},{5,6},{6,7},{7,4},{8,9},{9,10},{10,1... | collective-permute-start | bytes 983048 | tf_op jit(solution)/shard_map/ppermute | solution.py:30
  102.9 14.1 %collective-permute-start.34 = (bf16[1024,1024]{1,0:T(8,128)(2,1)S(1)}, bf16[1024,1024]{1,0:T(8,128)(2,1)S(1)}, u32[]{:S(2)}, u32[]{:S(2)}) collective-permute-start(bf16[1024,1024]{1,0:T(8,128)(2,1)S(1)} %get-tuple-element.91.own_ref), channel_id=1, source_target_pairs={{0,32},{32,0},{1,33},{33,1},{2,34},{34,2},{3,35},{35,3},{4,36},{36... | collective-permute-start | bytes 6291464 | tf_op jit(solution)/shard_map/ppermute | solution.py:30
  117.0 2.6 %collective-permute-start.35 = (bf16[400,1024]{1,0:T(8,128)(2,1)S(1)}, bf16[400,1024]{1,0:T(8,128)(2,1)S(1)}, u32[]{:S(2)}, u32[]{:S(2)}) collective-permute-start(bf16[400,1024]{1,0:T(8,128)(2,1)S(1)} %get-tuple-element.87), channel_id=1, source_target_pairs={{0,32},{32,0},{1,33},{33,1},{2,34},{34,2},{3,35},{35,3},{4,36},{36... | collective-permute-start | bytes 2457608 | tf_op jit(solution)/shard_map/ppermute | solution.py:30
  120.0 22.8 %collective-permute-start.36 = (bf16[400,1024]{1,0:T(8,128)(2,1)S(1)}, bf16[400,1024]{1,0:T(8,128)(2,1)S(1)}, u32[]{:S(2)}, u32[]{:S(2)}) collective-permute-start(bf16[400,1024]{1,0:T(8,128)(2,1)S(1)} %add_convert_fusion.2), channel_id=1, source_target_pairs={{0,64},{64,0},{1,65},{65,1},{2,66},{66,2},{3,67},{67,3},{4,68},{68... | collective-permute-start | bytes 2457608 | tf_op jit(solution)/shard_map/ppermute | solution.py:30
  144.9 3.2 %collective-permute-start.37 = (bf16[400,1024]{1,0:T(8,128)(2,1)S(1)}, bf16[400,1024]{1,0:T(8,128)(2,1)S(1)}, u32[]{:S(2)}, u32[]{:S(2)}) collective-permute-start(bf16[400,1024]{1,0:T(8,128)(2,1)S(1)} %third.1.third_ref), channel_id=1, source_target_pairs={{0,32},{32,0},{1,33},{33,1},{2,34},{34,2},{3,35},{35,3},{4,36},{36... | collective-permute-start | bytes 2457608 | tf_op jit(solution)/shard_map/ppermute | solution.py:30
where the time goes:
time: 151 us
  starting transfers between devices  52 us (34%)
  Pallas kernels  51.9 us (34%)
  waiting for transfers between devices  43 us (28%)
  other arithmetic  2.75 us (2%)
    ppermute x37, starting transfers between devices, shift(): lax.ppermute(value, axis, [(i, (i + step) % size) for i in range(size)])  49.1 us
    ppermute x37, waiting for transfers between devices, shift(): lax.ppermute(value, axis, [(i, (i + step) % size) for i in range(size)])  39.9 us
    pallas_call x1, Pallas kernels, schulz_call(): pl.pallas_call(schulz_kernel, in_specs=[whole()] * 3, out_specs=[whole()]...  21.1 us
    pallas_call x1, Pallas kernels, sketch_call(): pl.pallas_call(sketch_kernel, grid_spec=pltpu.PrefetchScalarGridSpec(num_...  12.5 us
    pallas_call x2, Pallas kernels, merge_call(): pl.pallas_call(merge_kernel, grid_spec=pltpu.PrefetchScalarGridSpec(num_s...  5.46 us
    pallas_call x1, Pallas kernels, coeff_call(): pl.pallas_call(coeff_kernel, in_specs=[pl.BlockSpec(memory_space=pltpu.SM...  5.13 us
    pallas_call x1, Pallas kernels, gram_first_call(): pl.pallas_call(gram_first_kernel, in_specs=[pl.BlockSpec(memory_space=plt...  3.6 us
    ppermute x1, waiting for transfers between devices, body(): across = lax.ppermute(pair, RING_Y, [(0, 3), (3, 0), (1, 2), (2, 1)])  3.11 us
  transfers between devices with their start and end apart: 38, of which 18 were waited for; matrix products, arithmetic and copies ran while one was open for 1% of the time, Pallas kernels for 22%

commit v1 on v0

--- a/solution.py
+++ b/solution.py
@@ -13,6 +13,8 @@
 F32 = jnp.float32
 NS_BLOCK = 256
 GRAM_BLOCK = 256
+MERGE_BLOCK = 256
+FETCH_AHEAD = 2
 MIB = 1024 * 1024
 RING_Y = ("yh", "yl")
 
@@ -30,37 +32,61 @@
     return lax.ppermute(value, axis, [(i, (i + step) % size) for i in range(size)])
 
 
-def sketch_kernel(at_ref, deltas_ref, sketch_ref, *rest):
-    outs, keep_ref, give_ref, rows_ref = rest[:10], rest[10], rest[11], rest[12]
-    quarter = pl.program_id(0)
+def halving_order(at, index):
+    near = at + 1 - 2 * lax.rem(at, 2)
+    return (at, 3 - at, near, 3 - near)[index]
+
+
+def sketch_kernel(at_ref, deltas_any, sketch_ref, *rest):
+    outs, keep_any, give_any = rest[:10], rest[10], rest[11]
+    rows_ref, held_ref, pool_ref, in_sem, out_sem = rest[12:]
+    quarters, tasks, rows, quarter = held_ref.shape
     rank = sketch_ref.shape[1]
     piece = rows_ref.shape[2]
     x, z = at_ref[0], at_ref[1]
-    for task in range(2):
-        part = lax.dot_general(
-            sketch_ref[...], deltas_ref[task], (((0,), (0,)), ((), ())), preferred_element_type=F32
-        )
-        rows_ref[...] = part.astype(BF).T.reshape(4, 4, piece, rank)
-        own, up, down, low, high = outs[5 * task : 5 * task + 5]
-        for d in range(4):
-            for e in range(4):
-                over_x, over_z = (d, e) if task == 0 else (e, d)
-                value = rows_ref[lax.rem(x + over_x, 4), lax.rem(z + over_z, 4)]
-                if d == 2:
-                    (low if e < 2 else high)[e % 2, quarter] = value
-                else:
-                    (own, up, None, down)[d][e, quarter] = value
-
-    total = deltas_ref[0] + deltas_ref[1]
-    mine = quarter % 2 == at_ref[3]
-
-    @pl.when(mine)
-    def _():
-        keep_ref[0] = total
-
-    @pl.when(jnp.logical_not(mine))
-    def _():
-        give_ref[0] = total
+
+    def fetch(q, task):
+        columns = pl.ds(pl.multiple_of(q * quarter, quarter), quarter)
+        return pltpu.make_async_copy(deltas_any.at[task, :, columns], held_ref.at[q, task], in_sem.at[q, task])
+
+    for q in range(FETCH_AHEAD):
+        for task in range(tasks):
+            fetch(q, task).start()
+
+    @pl.loop(0, quarters)
+    def _(q):
+        for task in range(tasks):
+            fetch(q, task).wait()
+
+            @pl.when(q + FETCH_AHEAD < quarters)
+            def _():
+                fetch(q + FETCH_AHEAD, task).start()
+
+            part = lax.dot_general(
+                sketch_ref[...], held_ref[q, task], (((0,), (0,)), ((), ())), preferred_element_type=F32
+            )
+            rows_ref[...] = part.astype(BF).T.reshape(4, 4, piece, rank)
+            own, up, down, low, high = outs[5 * task : 5 * task + 5]
+            for d in range(4):
+                for e in range(4):
+                    if task == 0:
+                        value = rows_ref[lax.rem(x + d, 4), halving_order(z, e)]
+                    else:
+                        value = rows_ref[halving_order(x, e), lax.rem(z + d, 4)]
+                    if d == 2:
+                        (low if e < 2 else high)[e % 2, q] = value
+                    else:
+                        (own, up, None, down)[d][e, q] = value
+        pool_ref[q] = held_ref[q, 0] + held_ref[q, 1]
+        mine = at_ref[3] == lax.rem(q, 2)
+        for target, wanted in ((keep_any, mine), (give_any, jnp.logical_not(mine))):
+
+            @pl.when(wanted)
+            def _(target=target):
+                pltpu.make_async_copy(pool_ref.at[q], target.at[q // 2], out_sem.at[q]).start()
+
+    for q in range(quarters):
+        pltpu.make_async_copy(pool_ref.at[q], keep_any.at[q // 2], out_sem.at[q]).wait()
 
 
 def sketch_call(at, deltas, sketch):
@@ -69,21 +95,20 @@
     quarter = width // 4
     full, half = (4, 4, quarter // 16, rank), (2, 4, quarter // 16, rank)
     shapes = [full, full, full, half, half] * 2
+    anywhere = pl.BlockSpec(memory_space=pl.ANY)
     return pl.pallas_call(
         sketch_kernel,
-        grid_spec=pltpu.PrefetchScalarGridSpec(
-            num_scalar_prefetch=1,
-            grid=(4,),
-            in_specs=[
-                pl.BlockSpec((tasks, rows, quarter), lambda i, at: (0, 0, i)),
-                pl.BlockSpec((rows, rank), lambda i, at: (0, 0)),
-            ],
-            out_specs=[pl.BlockSpec(shape, lambda i, at: (0, 0, 0, 0)) for shape in shapes]
-            + [pl.BlockSpec((1, rows, quarter), lambda i, at: (i // 2, 0, 0))] * 2,
-            scratch_shapes=[pltpu.VMEM(full, BF)],
-        ),
+        in_specs=[pl.BlockSpec(memory_space=pltpu.SMEM), anywhere, whole()],
+        out_specs=[whole()] * len(shapes) + [anywhere] * 2,
         out_shape=[jax.ShapeDtypeStruct(shape, BF) for shape in shapes]
         + [jax.ShapeDtypeStruct((2, rows, quarter), BF)] * 2,
+        scratch_shapes=[
+            pltpu.VMEM(full, BF),
+            pltpu.VMEM((4, tasks, rows, quarter), BF),
+            pltpu.VMEM((4, rows, quarter), BF),
+            pltpu.SemaphoreType.DMA((4, tasks)),
+            pltpu.SemaphoreType.DMA((4,)),
+        ],
         compiler_params=params(48),
         name="sketch",
     )(at, deltas, sketch)
@@ -173,30 +198,28 @@
     )(at, *parts, acc, near)
 
 
-def coeff_kernel(at_ref, basis_ref, pool0_ref, pool1_ref, keep_ref, give_ref, chunk_ref):
-    chunk_ref[...] = basis_ref[at_ref[2]]
-    half, width = keep_ref.shape
+def coeff_kernel(at_ref, basis_ref, pool0_ref, pool1_ref, out_ref, *, own):
+    half, width = out_ref.shape
+    which = at_ref[3] if own else 1 - at_ref[3]
     block = 256
-    for out_ref, which in ((give_ref, 1 - at_ref[3]), (keep_ref, at_ref[3])):
-        rows = pl.ds(pl.multiple_of(which * half, 16), half)
-        for i in range(0, width, block):
-            columns = slice(i, i + block)
-            value = jnp.dot(pool0_ref[rows, :], basis_ref[0, :, columns], preferred_element_type=F32)
-            value = value + jnp.dot(pool1_ref[rows, :], basis_ref[1, :, columns], preferred_element_type=F32)
-            out_ref[:, columns] = value.astype(BF)
-
-
-def coeff_call(at, basis, pooled):
+    rows = pl.ds(pl.multiple_of(which * half, 16), half)
+    for i in range(0, width, block):
+        columns = slice(i, i + block)
+        value = jnp.dot(pool0_ref[rows, :], basis_ref[0, :, columns], preferred_element_type=F32)
+        value = value + jnp.dot(pool1_ref[rows, :], basis_ref[1, :, columns], preferred_element_type=F32)
+        out_ref[:, columns] = value.astype(BF)
+
+
+def coeff_call(at, basis, pooled, own):
     _, depth, width = basis.shape
     rows = pooled[0].shape[0]
-    half = jax.ShapeDtypeStruct((rows // 2, width), BF)
-    return pl.pallas_call(
-        coeff_kernel,
+    return pl.pallas_call(
+        functools.partial(coeff_kernel, own=own),
         in_specs=[pl.BlockSpec(memory_space=pltpu.SMEM)] + [whole()] * 3,
-        out_specs=[whole()] * 3,
-        out_shape=[half, half, jax.ShapeDtypeStruct((depth, width), BF)],
+        out_specs=whole(),
+        out_shape=jax.ShapeDtypeStruct((rows // 2, width), BF),
         cost_estimate=pl.CostEstimate(
-            flops=4 * rows * depth * width, bytes_accessed=4 * rows * depth, transcendentals=0
+            flops=2 * rows * depth * width, bytes_accessed=4 * rows * depth, transcendentals=0
         ),
         compiler_params=params(20),
         name="coeff",
@@ -217,7 +240,7 @@
         mirror(out, rows, value.astype(BF), NS_BLOCK)
 
 
-def schulz_kernel(own_ref, other_ref, chunk_ref, z_ref, frob_ref, turned_ref, gram_ref, y_ref, t_ref, y2_ref, z2_ref):
+def schulz_kernel(own_ref, other_ref, z_ref, frob_ref, gram_ref, y_ref, t_ref, y2_ref, z2_ref):
     size = own_ref.shape[0]
     total = jnp.zeros((8, size), F32)
     for i in range(0, size, NS_BLOCK):
@@ -247,20 +270,16 @@
             product(t_ref, y_ref, y2_ref, False)
             y_ref[...] = y2_ref[...]
 
-    for i in range(0, chunk_ref.shape[0], NS_BLOCK):
-        turned_ref[:, i : i + NS_BLOCK] = chunk_ref[i : i + NS_BLOCK, :].T
-
-
-def schulz_call(own, other, chunk):
+
+def schulz_call(own, other):
     size = own.shape[0]
     return pl.pallas_call(
         schulz_kernel,
-        in_specs=[whole()] * 3,
-        out_specs=[whole()] * 3,
+        in_specs=[whole()] * 2,
+        out_specs=[whole()] * 2,
         out_shape=[
             jax.ShapeDtypeStruct((size, size), BF),
             jax.ShapeDtypeStruct((8, 128), F32),
-            jax.ShapeDtypeStruct(chunk.shape[::-1], BF),
         ],
         scratch_shapes=[pltpu.VMEM((size, size), F32)] + [pltpu.VMEM((size, size), BF)] * 4,
         cost_estimate=pl.CostEstimate(
@@ -268,61 +287,76 @@
         ),
         compiler_params=params(32),
         name="schulz",
-    )(own, other, chunk)
-
-
-def third_kernel(coeff_ref, z_ref, frob_ref, out_ref):
-    second = jnp.dot(coeff_ref[...], z_ref[...], preferred_element_type=F32).astype(BF)
+    )(own, other)
+
+
+def third_kernel(chip_ref, over_ref, z_ref, frob_ref, out_ref, *, tasks):
+    coeff = ((chip_ref[...].astype(F32) + over_ref[...].astype(F32)) / tasks).astype(BF)
+    second = jnp.dot(coeff, z_ref[...], preferred_element_type=F32).astype(BF)
     third = jnp.dot(second, z_ref[...], preferred_element_type=F32)
     out_ref[...] = (third / frob_ref[0:1, 0:1]).astype(BF)
 
 
-def third_call(coeff, z, frob):
-    return pl.pallas_call(
-        third_kernel,
-        in_specs=[whole()] * 3,
+def third_call(chip_sum, over, z, frob, tasks):
+    return pl.pallas_call(
+        functools.partial(third_kernel, tasks=tasks),
+        in_specs=[whole()] * 4,
         out_specs=whole(),
-        out_shape=jax.ShapeDtypeStruct(coeff.shape, BF),
+        out_shape=jax.ShapeDtypeStruct(chip_sum.shape, BF),
         compiler_params=params(),
         name="third",
-    )(coeff, z, frob)
-
-
-def merge_kernel(at_ref, third_ref, chunk_ref, *rest):
-    out_ref = rest[-1]
-    out_ref[...] = jnp.dot(third_ref[...], chunk_ref[...], preferred_element_type=F32).astype(BF)
-
-
-def merge_call(at, third, chunk, so_far):
+    )(chip_sum, over, z, frob)
+
+
+def merge_own_kernel(at_ref, third_ref, chunk_ref, out_any, turned_ref, stage_ref, sem):
+    merge_rows(at_ref, at_ref[3], third_ref, turned_ref, out_any, stage_ref, sem, chunk_ref)
+
+
+def merge_twin_kernel(at_ref, third_ref, turned_ref, so_far_any, out_any, stage_ref, sem):
+    merge_rows(at_ref, 1 - at_ref[3], third_ref, turned_ref, out_any, stage_ref, sem)
+
+
+def merge_rows(at_ref, which, third_ref, turned_ref, out_any, stage_ref, sem, chunk_ref=None):
+    half, width = stage_ref.shape
+    rows = pl.ds(pl.multiple_of(which * half, 16), half)
+    copies = []
+    for i in range(0, width, MERGE_BLOCK):
+        columns = slice(i, i + MERGE_BLOCK)
+        if chunk_ref is not None:
+            turned_ref[:, columns] = chunk_ref[at_ref[2], columns, :].T
+        stage_ref[:, columns] = jnp.dot(
+            third_ref[...], turned_ref[:, columns], preferred_element_type=F32
+        ).astype(BF)
+        target = out_any.at[rows, pl.ds(i, MERGE_BLOCK)]
+        copies.append(pltpu.make_async_copy(stage_ref.at[:, columns], target, sem.at[len(copies)]))
+        copies[-1].start()
+    for copy in copies:
+        copy.wait()
+
+
+def merge_call(at, third, chunk, so_far=None):
     rows, width = third.shape
+    first = so_far is None
     columns = chunk.shape[1]
-    in_specs = [
-        pl.BlockSpec((rows, width), lambda i, at: (0, 0)),
-        pl.BlockSpec((width, columns), lambda i, at: (0, 0)),
-    ]
-    operands = [at, third, chunk]
-    if so_far is None:
-        place = lambda i, at: (at[3], 0)
-    else:
-        place = lambda i, at: (1 - at[3], 0)
-        in_specs.append(pl.BlockSpec(memory_space=pl.ANY))
-        operands.append(so_far)
-    return pl.pallas_call(
-        merge_kernel,
-        grid_spec=pltpu.PrefetchScalarGridSpec(
-            num_scalar_prefetch=1,
-            grid=(1,),
-            in_specs=in_specs,
-            out_specs=pl.BlockSpec((rows, columns), place),
-        ),
-        out_shape=jax.ShapeDtypeStruct((2 * rows, columns), BF),
-        input_output_aliases={3: 0} if so_far is not None else {},
+    anywhere = pl.BlockSpec(memory_space=pl.ANY)
+    merged = jax.ShapeDtypeStruct((2 * rows, columns), BF)
+    turned = jax.ShapeDtypeStruct((width, columns), BF)
+    return pl.pallas_call(
+        merge_own_kernel if first else merge_twin_kernel,
+        in_specs=[pl.BlockSpec(memory_space=pltpu.SMEM), whole(), whole()] + ([] if first else [anywhere]),
+        out_specs=[anywhere, whole()] if first else anywhere,
+        out_shape=[merged, turned] if first else merged,
+        input_output_aliases={} if first else {3: 0},
+        scratch_shapes=[
+            pltpu.VMEM((rows, columns), BF),
+            pltpu.SemaphoreType.DMA((columns // MERGE_BLOCK,)),
+        ],
         cost_estimate=pl.CostEstimate(
             flops=2 * rows * columns * width, bytes_accessed=2 * columns * width, transcendentals=0
         ),
         compiler_params=params(),
         name="merge",
-    )(*operands)
+    )(at, third, chunk, *([] if first else [so_far]))
 
 
 def add(*values):
@@ -336,11 +370,16 @@
     up = lax.dynamic_update_slice(up, add(up[:cut], low), (0,) * up.ndim)
     down = lax.dynamic_update_slice(down, add(down[cut:], high), (cut,) + (0,) * (up.ndim - 1))
     from_below, from_above = shift(up, axis, 1), shift(down, axis, -1)
-    return [add(own[e], from_below[e], from_above[e]) for e in range(own.shape[0])]
-
-
-def direct_reduce(pieces, axis):
-    return add(pieces[0], *[shift(piece, axis, step) for step, piece in enumerate(pieces) if step])
+    half = own.shape[0] // 2
+    keep = [add(own[e], from_below[e], from_above[e]) for e in range(half)]
+    give = add(own[half:], from_below[half:], from_above[half:])
+    return keep, give
+
+
+def halving_reduce(keep, give, axis):
+    got = lax.ppermute(give, axis, [(0, 1), (1, 0), (2, 3), (3, 2)])
+    mine, other = add(keep[0], got[0]), add(keep[1], got[1])
+    return add(mine, lax.ppermute(other, axis, [(0, 3), (3, 0), (1, 2), (2, 1)]))
 
 
 def ring_gather(items):
@@ -360,16 +399,16 @@
     tasks, rows, width = deltas.shape
     core, yh, yl = lax.axis_index("core"), lax.axis_index("yh"), lax.axis_index("yl")
     x, z = lax.axis_index("x"), lax.axis_index("z")
-    at, core0, yh0 = lax.optimization_barrier(
-        (jnp.stack([x, z, yh, core]).astype(jnp.int32), core == 0, yh == 0)
+    at, core0, yh0, yl0 = lax.optimization_barrier(
+        (jnp.stack([x, z, yh, core]).astype(jnp.int32), core == 0, yh == 0, yl == 0)
     )
 
     *terms, pool_keep, pool_give = sketch_call(at, deltas, sketch)
     sum0 = ring_reduce(terms[:5], "x")
     sum1 = ring_reduce(terms[5:], "z")
     pool_got = shift(pool_give, "core", 1)
-    sum0 = direct_reduce(sum0, "z")
-    sum1 = direct_reduce(sum1, "x")
+    sum0 = halving_reduce(*sum0, "z")
+    sum1 = halving_reduce(*sum1, "x")
 
     piece, rank = sum0.shape[1:]
     both = jnp.concatenate([sum0, sum1], axis=2).reshape(2, 2, piece, 2 * rank)
@@ -379,11 +418,10 @@
     chip = jnp.concatenate(
         [jnp.where(core0, keep, got), jnp.where(core0, got, keep)], axis=2
     )
-    pair = add(chip, shift(chip, "yl", 1))
-    across = lax.ppermute(pair, RING_Y, [(0, 3), (3, 0), (1, 2), (2, 1)])
-    local = jnp.concatenate(
-        [jnp.where(yh0, pair, across), jnp.where(yh0, across, pair)], axis=2
-    )
+    below, above, across = [shift(chip, RING_Y, step) for step in (1, -1, 2)]
+    ours = add(chip, jnp.where(yl0, above, below))
+    theirs = add(across, jnp.where(yl0, below, above))
+    local = jnp.concatenate([jnp.where(yh0, ours, theirs), jnp.where(yh0, theirs, ours)], axis=2)
 
     near, _ = ring_gather([(local[0][None], "x"), (local[1][None], "z")])
     half = local.shape[2] // 2
@@ -400,19 +438,21 @@
     far, acc, basis = lax.optimization_barrier((far, acc, basis))
     gram_own, basis = gram_last_call(at, far[0] + far[1], acc, basis)
     gram_other = shift(gram_own, "core", 1)
-    mine, give, chunk = coeff_call(at, basis.reshape(2, width // 4, basis.shape[-1]), pooled)
-    give, gram_own, gram_other = lax.optimization_barrier((give, gram_own, gram_other))
+    basis = basis.reshape(2, width // 4, basis.shape[-1])
+    give = coeff_call(at, basis, pooled, False)
+    give, pooled = lax.optimization_barrier((give, pooled))
     twin = shift(give, "core", 1)
+    mine = coeff_call(at, basis, pooled, True)
+    twin, mine, gram_own, gram_other = lax.optimization_barrier((twin, mine, gram_own, gram_other))
     chip_sum, gram_own, gram_other = lax.optimization_barrier((add(mine, twin), gram_own, gram_other))
     over = shift(chip_sum, "yh", 1)
-    inverse_root, frob, chunk = schulz_call(gram_own, gram_other, chunk)
+    inverse_root, frob = schulz_call(gram_own, gram_other)
     over, inverse_root = lax.optimization_barrier((over, inverse_root))
     total_tasks = tasks * lax.axis_size("yh") * lax.axis_size("core")
-    coeff = ((chip_sum.astype(F32) + over.astype(F32)) / total_tasks).astype(BF)
-
-    third = third_call(coeff, inverse_root, frob)
+    third = third_call(chip_sum, over, inverse_root, frob, total_tasks)
     third_twin = shift(third, "core", 1)
-    return merge_call(at, third_twin, chunk, merge_call(at, third, chunk, None))
+    merged, turned = merge_call(at, third, basis)
+    return merge_call(at, third_twin, turned, merged)
 
 
 def solution(mesh):

time: 151 us -> 147 us (0.974)
  waiting for transfers between devices: 43 us -> 39 us
  Pallas kernels: 51.9 us -> 49.1 us
  starting transfers between devices: 52 us -> 54.7 us
    ppermute x37 -> x33, waiting for transfers between devices: 39.9 us -> 34.1 us  [shift(): lax.ppermute(value, axis, [(i, (i + step) % size) for i in range(size)])]
    pallas_call x6 -> x7, Pallas kernels: 46.1 us -> 43.3 us  [the longest x1 20.3 us: schulz_call(): pl.pallas_call(schulz_kernel, in_specs=[whole()] * 2, out_specs=[whole()]...]
    ppermute x1 -> x4, waiting for transfers between devices: 3.11 us -> 4.92 us  [the longest x2 2.55 us: halving_reduce(): got = lax.ppermute(give, axis, [(0, 1), (1, 0), (2, 3), (3, 2)])]
    ppermute x37 -> x33, starting transfers between devices: 49.1 us -> 50.8 us  [shift(): lax.ppermute(value, axis, [(i, (i + step) % size) for i in range(size)])]
    ppermute x1 -> x4, starting transfers between devices: 2.82 us -> 3.96 us  [the longest x2 3.79 us: halving_reduce(): lax.ppermute(other, axis, [(0, 3), (3, 0), (1, 2), (2, 1)])]
  transfers between devices with their start and end apart: 38 -> 37, of which waited for: 18 -> 19; matrix products, arithmetic and copies ran while one was open for 1% -> 2% of each run, Pallas kernels for 22% -> 22%
where the time goes in v1:
time: 147 us
  starting transfers between devices  54.7 us (37%)
  Pallas kernels  49.1 us (33%)
  waiting for transfers between devices  39 us (27%)
  other arithmetic  2.59 us (2%)
    ppermute x33, starting transfers between devices, shift(): lax.ppermute(value, axis, [(i, (i + step) % size) for i in range(size)])  50.8 us
    ppermute x33, waiting for transfers between devices, shift(): lax.ppermute(value, axis, [(i, (i + step) % size) for i in range(size)])  34.1 us
    pallas_call x1, Pallas kernels, schulz_call(): pl.pallas_call(schulz_kernel, in_specs=[whole()] * 2, out_specs=[whole()]...  20.3 us
    pallas_call x1, Pallas kernels, sketch_call(): pl.pallas_call(sketch_kernel, in_specs=[pl.BlockSpec(memory_space=pltpu.S...  10.2 us
    pallas_call x2, Pallas kernels, coeff_call(): pl.pallas_call(functools.partial(coeff_kernel, own=own), in_specs=[pl.Blo...  5.66 us
    pallas_call x2, Pallas kernels, merge_call(): pl.pallas_call(merge_own_kernel if first else merge_twin_kernel, in_specs...  5.22 us
    ppermute x2, starting transfers between devices, halving_reduce(): lax.ppermute(other, axis, [(0, 3), (3, 0), (1, 2), (2, 1)])  3.79 us
    pallas_call x1, Pallas kernels, gram_first_call(): pl.pallas_call(gram_first_kernel, in_specs=[pl.BlockSpec(memory_space=plt...  3.59 us
  transfers between devices with their start and end apart: 37, of which 19 were waited for; matrix products, arithmetic and copies ran while one was open for 2% of the time, Pallas kernels for 22%

profile of v1, /device:TPU:1, one launch (start us, length us, event | category | flops | bytes accessed | tf_op | source)
XLA Modules:
  0.0 147.0 jit_solution(16012069335054391330)
XLA Ops:
  0.0 0.1 pad_add_fusion.at_ref
  0.1 0.9 copy-done
  1.0 10.2 %sketch.1 = (bf16[4,4,80,128]{3,2,1,0:T(8,128)(2,1)S(1)}, bf16[4,4,80,128]{3,2,1,0:T(8,128)(2,1)S(1)}, bf16[4,4,80,128]{3,2,1,0:T(8,128)(2,1)S(1)}, bf16[2,4,80,...) custom-call(s32[4]{0:T(128)S(1)} %pad_add_fusion.at_ref, ...), custom_call_target="tpu_custom_call" | custom-call | tf_op jit(solution)/shard_map/sketch/pallas_call | solution.py:99
  11.2 4.7 %collective-permute-start.8 = (bf16[2,4,80,128]{3,2,1,0:T(8,128)(2,1)S(1)}, bf16[2,4,80,128]{3,2,1,0:T(8,128)(2,1)S(1)}, u32[]{:S(2)}, u32[]{:S(2)}) collective-permute-start(bf16[2,4,80,128]{3,2,1,0:T(8,128)(2,1)S(1)} %get-tuple-element.67), channel_id=1, source_target_pairs={{0,3},{1,0},{2,1},{3,2},{4,7},{5,4},{6,5},{7,6},{8,11},{9,8},{10,9... | collective-permute-start | bytes 491528 | tf_op jit(solution)/shard_map/ppermute | solution.py:32
  15.9 1.2 collective-permute-start
  17.1 1.5 collective-permute-start.2
  18.6 1.6 %collective-permute-start.28 = (bf16[2,800,1280]{2,1,0:T(8,128)(2,1)}, bf16[2,800,1280]{2,1,0:T(8,128)(2,1)S(1)}, u32[]{:S(2)}, u32[]{:S(2)}) collective-permute-start(bf16[2,800,1280]{2,1,0:T(8,128)(2,1)} %get-tuple-element.70), channel_id=1, source_target_pairs={{0,32},{32,0},{1,33},{33,1},{2,34},{34,2},{3,35},{35,3},{4,36},{36... | collective-permute-start | bytes 12288008 | tf_op jit(solution)/shard_map/ppermute | solution.py:32
  20.1 0.1 fusion.5
  20.2 3.0 %collective-permute-start.9 = (bf16[4,4,80,128]{3,2,1,0:T(8,128)(2,1)S(1)}, bf16[4,4,80,128]{3,2,1,0:T(8,128)(2,1)S(1)}, u32[]{:S(2)}, u32[]{:S(2)}) collective-permute-start(bf16[4,4,80,128]{3,2,1,0:T(8,128)(2,1)S(1)} %fusion.5), channel_id=1, source_target_pairs={{0,3},{1,0},{2,1},{3,2},{4,7},{5,4},{6,5},{7,6},{8,11},{9,8},{10,9... | collective-permute-start | bytes 983048 | tf_op jit(solution)/shard_map/ppermute | solution.py:32
  23.2 0.7 collective-permute-done.6
  23.9 0.1 fusion.4
  24.1 0.1 fusion.3
  24.2 1.6 %collective-permute-start.3 = (bf16[4,4,80,128]{3,2,1,0:T(8,128)(2,1)S(1)}, bf16[4,4,80,128]{3,2,1,0:T(8,128)(2,1)S(1)}, u32[]{:S(2)}, u32[]{:S(2)}) collective-permute-start(bf16[4,4,80,128]{3,2,1,0:T(8,128)(2,1)S(1)} %fusion.3), channel_id=1, source_target_pairs={{0,24},{8,0},{16,8},{24,16},{1,25},{9,1},{17,9},{25,17},{2,26},{10... | collective-permute-start | bytes 983048 | tf_op jit(solution)/shard_map/ppermute | solution.py:32
  25.8 0.1 fusion.2
  26.0 3.7 %collective-permute-done.9 = bf16[4,4,80,128]{3,2,1,0:T(8,128)(2,1)S(1)} collective-permute-done((bf16[4,4,80,128]{3,2,1,0:T(8,128)(2,1)S(1)}, bf16[4,4,80,128]{3,2,1,0:T(8,128)(2,1)S(1)}, u32[]{:S(2)}, u32[]{:S(2)}) %collective-permute-start.9) | collective-permute-done | bytes 327712 | tf_op jit(solution)/shard_map/ppermute | solution.py:32
  29.7 2.1 %collective-permute-done.7 = bf16[4,4,80,128]{3,2,1,0:T(8,128)(2,1)S(1)} collective-permute-done((bf16[4,4,80,128]{3,2,1,0:T(8,128)(2,1)S(1)}, bf16[4,4,80,128]{3,2,1,0:T(8,128)(2,1)S(1)}, u32[]{:S(2)}, u32[]{:S(2)}) %collective-permute-start.7) | collective-permute-done | bytes 327712 | tf_op jit(solution)/shard_map/ppermute | solution.py:32
  31.9 0.1 collective-permute-start.10
  32.0 1.7 %collective-permute-done.1 = bf16[4,4,80,128]{3,2,1,0:T(8,128)(2,1)S(1)} collective-permute-done((bf16[4,4,80,128]{3,2,1,0:T(8,128)(2,1)S(1)}, bf16[4,4,80,128]{3,2,1,0:T(8,128)(2,1)S(1)}, u32[]{:S(2)}, u32[]{:S(2)}) %collective-permute-start.1) | collective-permute-done | bytes 327712 | tf_op jit(solution)/shard_map/ppermute | solution.py:32
  33.8 0.1 collective-permute-start.4
  33.9 2.5 %collective-permute-done.10 = bf16[2,4,80,128]{3,2,1,0:T(8,128)(2,1)S(1)} collective-permute-done((bf16[2,4,80,128]{3,2,1,0:T(8,128)(2,1)S(1)}, bf16[2,4,80,128]{3,2,1,0:T(8,128)(2,1)S(1)}, u32[]{:S(2)}, u32[]{:S(2)}) %collective-permute-start.10) | collective-permute-done | bytes 163872 | tf_op jit(solution)/shard_map/ppermute | solution.py:380
  36.5 1.6 %collective-permute-start.11 = (bf16[4,80,128]{2,1,0:T(8,128)(2,1)S(1)}, bf16[4,80,128]{2,1,0:T(8,128)(2,1)S(1)}, u32[]{:S(2)}, u32[]{:S(2)}) collective-permute-start(bf16[4,80,128]{2,1,0:T(8,128)(2,1)S(1)} %fusion.12), channel_id=1, source_target_pairs={{0,24},{24,0},{8,16},{16,8},{1,25},{25,1},{9,17},{17,9},{2,26},{26... | collective-permute-start | bytes 245768 | tf_op jit(solution)/shard_map/ppermute | solution.py:382
  38.1 2.1 %collective-permute-start.5 = (bf16[4,80,128]{2,1,0:T(8,128)(2,1)S(1)}, bf16[4,80,128]{2,1,0:T(8,128)(2,1)S(1)}, u32[]{:S(2)}, u32[]{:S(2)}) collective-permute-start(bf16[4,80,128]{2,1,0:T(8,128)(2,1)S(1)} %fusion.10), channel_id=1, source_target_pairs={{0,3},{3,0},{1,2},{2,1},{4,7},{7,4},{5,6},{6,5},{8,11},{11,8},{9,1... | collective-permute-start | bytes 245768 | tf_op jit(solution)/shard_map/ppermute | solution.py:382
  40.3 0.7 collective-permute-done.11
  41.1 1.6 %collective-permute-done.5 = bf16[4,80,128]{2,1,0:T(8,128)(2,1)S(1)} collective-permute-done((bf16[4,80,128]{2,1,0:T(8,128)(2,1)S(1)}, bf16[4,80,128]{2,1,0:T(8,128)(2,1)S(1)}, u32[]{:S(2)}, u32[]{:S(2)}) %collective-permute-start.5) | collective-permute-done | bytes 81952 | tf_op jit(solution)/shard_map/ppermute | solution.py:382
  42.8 6.0 %collective-permute-start.12 = (bf16[2,80,256]{2,1,0:T(8,128)(2,1)S(1)}, bf16[2,80,256]{2,1,0:T(8,128)(2,1)S(1)}, u32[]{:S(2)}, u32[]{:S(2)}) collective-permute-start(bf16[2,80,256]{2,1,0:T(8,128)(2,1)S(1)} %select_bitcast_fusion), channel_id=1, source_target_pairs={{0,32},{32,0},{1,33},{33,1},{2,34},{34,2},{3,35},{35,3},{4,36},{36... | collective-permute-start | bytes 245768 | tf_op jit(solution)/shard_map/ppermute | solution.py:32
  48.8 0.9 collective-permute-done.12
  49.8 1.4 collective-permute-start.14
  51.2 1.5 %collective-permute-start.13 = (bf16[2,80,512]{2,1,0:T(8,128)(2,1)S(1)}, bf16[2,80,512]{2,1,0:T(8,128)(2,1)S(1)}, u32[]{:S(2)}, u32[]{:S(2)}) collective-permute-start(bf16[2,80,512]{2,1,0:T(8,128)(2,1)S(1)} %pad_maximum_fusion.2), channel_id=1, source_target_pairs={{0,68},{4,0},{64,4},{68,64},{1,69},{5,1},{65,5},{69,65},{2,70},{6,... | collective-permute-start | bytes 491528 | tf_op jit(solution)/shard_map/ppermute | solution.py:32
  52.7 1.6 %collective-permute-start.15 = (bf16[2,80,512]{2,1,0:T(8,128)(2,1)S(1)}, bf16[2,80,512]{2,1,0:T(8,128)(2,1)S(1)}, u32[]{:S(2)}, u32[]{:S(2)}) collective-permute-start(bf16[2,80,512]{2,1,0:T(8,128)(2,1)S(1)} %pad_maximum_fusion.2), channel_id=1, source_target_pairs={{0,64},{4,68},{64,0},{68,4},{1,65},{5,69},{65,1},{69,5},{2,66},{6,... | collective-permute-start | bytes 491528 | tf_op jit(solution)/shard_map/ppermute | solution.py:32
  54.3 2.4 %collective-permute-done.14 = bf16[2,80,512]{2,1,0:T(8,128)(2,1)S(1)} collective-permute-done((bf16[2,80,512]{2,1,0:T(8,128)(2,1)S(1)}, bf16[2,80,512]{2,1,0:T(8,128)(2,1)S(1)}, u32[]{:S(2)}, u32[]{:S(2)}) %collective-permute-start.14) | collective-permute-done | bytes 163872 | tf_op jit(solution)/shard_map/ppermute | solution.py:32
  56.7 4.6 %collective-permute-done.15 = bf16[2,80,512]{2,1,0:T(8,128)(2,1)S(1)} collective-permute-done((bf16[2,80,512]{2,1,0:T(8,128)(2,1)S(1)}, bf16[2,80,512]{2,1,0:T(8,128)(2,1)S(1)}, u32[]{:S(2)}, u32[]{:S(2)}) %collective-permute-start.15) | collective-permute-done | bytes 163872 | tf_op jit(solution)/shard_map/ppermute | solution.py:32
  61.3 0.1 broadcast_select_fusion
  61.5 1.2 collective-permute-start.17
  62.7 0.4 collective-permute-start.16
  63.0 2.6 %collective-permute-start.23 = (bf16[1,80,1024]{2,1,0:T(8,128)(2,1)S(1)}, bf16[1,80,1024]{2,1,0:T(8,128)(2,1)S(1)}, u32[]{:S(2)}, u32[]{:S(2)}) collective-permute-start(bf16[1,80,1024]{2,1,0:T(8,128)(2,1)S(1)} %get-tuple-element.110), channel_id=1, source_target_pairs={{0,3},{1,0},{2,1},{3,2},{4,7},{5,4},{6,5},{7,6},{8,11},{9,8},{10,9... | collective-permute-start | bytes 491528 | tf_op jit(solution)/shard_map/ppermute | solution.py:32
  65.6 0.5 collective-permute-done.17
  66.1 2.3 %collective-permute-start.19 = (bf16[1,80,512]{2,1,0:T(8,128)(2,1)S(1)}, bf16[1,80,512]{2,1,0:T(8,128)(2,1)S(1)}, u32[]{:S(2)}, u32[]{:S(2)}) collective-permute-start(bf16[1,80,512]{2,1,0:T(8,128)(2,1)S(1)} %slice.191), channel_id=1, source_target_pairs={{0,24},{8,0},{16,8},{24,16},{1,25},{9,1},{17,9},{25,17},{2,26},{10... | collective-permute-start | bytes 245768 | tf_op jit(solution)/shard_map/ppermute | solution.py:32
  68.5 2.8 %collective-permute-start.25 = (bf16[1,80,512]{2,1,0:T(8,128)(2,1)S(1)}, bf16[1,80,512]{2,1,0:T(8,128)(2,1)S(1)}, u32[]{:S(2)}, u32[]{:S(2)}) collective-permute-start(bf16[1,80,512]{2,1,0:T(8,128)(2,1)S(1)} %slice.193), channel_id=1, source_target_pairs={{0,3},{1,0},{2,1},{3,2},{4,7},{5,4},{6,5},{7,6},{8,11},{9,8},{10,9... | collective-permute-start | bytes 245768 | tf_op jit(solution)/shard_map/ppermute | solution.py:32
  71.4 1.9 %collective-permute-done.18 = bf16[1,80,512]{2,1,0:T(8,128)(2,1)S(1)} collective-permute-done((bf16[1,80,512]{2,1,0:T(8,128)(2,1)S(1)}, bf16[1,80,512]{2,1,0:T(8,128)(2,1)S(1)}, u32[]{:S(2)}, u32[]{:S(2)}) %collective-permute-start.18) | collective-permute-done | bytes 81952 | tf_op jit(solution)/shard_map/ppermute | solution.py:32
  73.3 2.3 %collective-permute-start.21 = (bf16[4,80,1024]{2,1,0:T(8,128)(2,1)S(1)}, bf16[4,80,1024]{2,1,0:T(8,128)(2,1)S(1)}, u32[]{:S(2)}, u32[]{:S(2)}) collective-permute-start(bf16[4,80,1024]{2,1,0:T(8,128)(2,1)S(1)} %maximum_maximum_fusion.a0), channel_id=1, source_target_pairs={{0,3},{1,0},{2,1},{3,2},{4,7},{5,4},{6,5},{7,6},{8,11},{9,8},{10,9... | collective-permute-start | bytes 1966088 | tf_op jit(solution)/shard_map/ppermute | solution.py:32
  75.6 0.5 collective-permute-done.24
  76.2 2.2 %collective-permute-start.27 = (bf16[4,80,1024]{2,1,0:T(8,128)(2,1)S(1)}, bf16[4,80,1024]{2,1,0:T(8,128)(2,1)S(1)}, u32[]{:S(2)}, u32[]{:S(2)}) collective-permute-start(bf16[4,80,1024]{2,1,0:T(8,128)(2,1)S(1)} %maximum_maximum_fusion.1.b0), channel_id=1, source_target_pairs={{0,24},{8,0},{16,8},{24,16},{1,25},{9,1},{17,9},{25,17},{2,26},{10... | collective-permute-start | bytes 1966088 | tf_op jit(solution)/shard_map/ppermute | solution.py:32
  78.4 1.2 fusion.1
  79.6 6.7 %collective-permute-done.21.a2 = bf16[4,80,1024]{2,1,0:T(8,128)(2,1)S(1)} collective-permute-done((bf16[4,80,1024]{2,1,0:T(8,128)(2,1)S(1)}, bf16[4,80,1024]{2,1,0:T(8,128)(2,1)S(1)}, u32[]{:S(2)}, u32[]{:S(2)}) %collective-permute-start.21) | collective-permute-done | bytes 655392 | tf_op jit(solution)/shard_map/ppermute | solution.py:32
  86.4 2.8 %collective-permute-done.20.a1 = bf16[4,80,1024]{2,1,0:T(8,128)(2,1)S(1)} collective-permute-done((bf16[4,80,1024]{2,1,0:T(8,128)(2,1)S(1)}, bf16[4,80,1024]{2,1,0:T(8,128)(2,1)S(1)}, u32[]{:S(2)}, u32[]{:S(2)}) %collective-permute-start.20) | collective-permute-done | bytes 655392 | tf_op jit(solution)/shard_map/ppermute | solution.py:32
  89.2 1.5 collective-permute-done.26.b1
  90.7 1.7 %collective-permute-start.32 = (bf16[2,80,1024]{2,1,0:T(8,128)(2,1)S(1)}, bf16[2,80,1024]{2,1,0:T(8,128)(2,1)S(1)}, u32[]{:S(2)}, u32[]{:S(2)}) collective-permute-start(bf16[2,80,1024]{2,1,0:T(8,128)(2,1)S(1)} %slice.169), channel_id=1, source_target_pairs={{0,24},{8,0},{16,8},{24,16},{1,25},{9,1},{17,9},{25,17},{2,26},{10... | collective-permute-start | bytes 983048 | tf_op jit(solution)/shard_map/ppermute | solution.py:32
  92.5 2.0 %collective-permute-start.30 = (bf16[2,80,1024]{2,1,0:T(8,128)(2,1)S(1)}, bf16[2,80,1024]{2,1,0:T(8,128)(2,1)S(1)}, u32[]{:S(2)}, u32[]{:S(2)}) collective-permute-start(bf16[2,80,1024]{2,1,0:T(8,128)(2,1)S(1)} %slice.167), channel_id=1, source_target_pairs={{0,3},{1,0},{2,1},{3,2},{4,7},{5,4},{6,5},{7,6},{8,11},{9,8},{10,9... | collective-permute-start | bytes 983048 | tf_op jit(solution)/shard_map/ppermute | solution.py:32
  94.4 3.6 %gram_first.1 = (f32[1024,1024]{1,0:T(8,128)S(1)}, bf16[2,4,4,80,1024]{4,3,2,1,0:T(8,128)(2,1)S(1)}) custom-call(s32[4]{0:T(128)S(1)} %pad_add_fusion.at_ref, bf16[4,80,1024]{2,1,0:T(8,128)(2,1)S(1)} %maximum_maximum_fusion.a0, bf16[4,80,1024]{2,1,0:T(8,128)(2,1)S(1)} %collective-permute-done.20.a1, bf16[4,80,1024]{2,1,0:T(8,128)(2,1)S(1)} %collective-permute-done.21.a2, ...), custom_call_target="tpu_custom_call" | custom-call | flops 2684354560 | bytes 2621440 | tf_op jit(solution)/shard_map/gram_first/pallas_call | solution.py:157
  98.0 1.6 %collective-permute-done.31.b3 = bf16[2,80,1024]{2,1,0:T(8,128)(2,1)S(1)} collective-permute-done((bf16[2,80,1024]{2,1,0:T(8,128)(2,1)S(1)}, bf16[2,80,1024]{2,1,0:T(8,128)(2,1)S(1)}, u32[]{:S(2)}, u32[]{:S(2)}) %collective-permute-start.31) | collective-permute-done | bytes 327712 | tf_op jit(solution)/shard_map/ppermute | solution.py:32
  99.6 2.2 %collective-permute-done.29.a3 = bf16[2,80,1024]{2,1,0:T(8,128)(2,1)S(1)} collective-permute-done((bf16[2,80,1024]{2,1,0:T(8,128)(2,1)S(1)}, bf16[2,80,1024]{2,1,0:T(8,128)(2,1)S(1)}, u32[]{:S(2)}, u32[]{:S(2)}) %collective-permute-start.29) | collective-permute-done | bytes 327712 | tf_op jit(solution)/shard_map/ppermute | solution.py:32
  101.8 2.2 %gram_last.1 = (bf16[1024,1024]{1,0:T(8,128)(2,1)S(1)}, bf16[2,4,4,80,1024]{4,3,2,1,0:T(8,128)(2,1)S(1)}) custom-call(s32[4]{0:T(128)S(1)} %pad_add_fusion.at_ref, bf16[2,80,1024]{2,1,0:T(8,128)(2,1)S(1)} %collective-permute-done.29.a3, bf16[2,80,1024]{2,1,0:T(8,128)(2,1)S(1)} %collective-permute-done.30.a4, ...), custom_call_target="tpu_custom_call" | custom-call | tf_op jit(solution)/shard_map/gram_last/pallas_call | solution.py:187
  104.0 6.9 %collective-permute-start.34 = (bf16[1024,1024]{1,0:T(8,128)(2,1)S(1)}, bf16[1024,1024]{1,0:T(8,128)(2,1)S(1)}, u32[]{:S(2)}, u32[]{:S(2)}) collective-permute-start(bf16[1024,1024]{1,0:T(8,128)(2,1)S(1)} %get-tuple-element.97.own_ref), channel_id=1, source_target_pairs={{0,32},{32,0},{1,33},{33,1},{2,34},{34,2},{3,35},{35,3},{4,36},{36... | collective-permute-start | bytes 6291464 | tf_op jit(solution)/shard_map/ppermute | solution.py:32
  111.0 2.8 %coeff.2 = bf16[400,1024]{1,0:T(8,128)(2,1)S(1)} custom-call(s32[4]{0:T(128)S(1)} %pad_add_fusion.at_ref, bf16[2,1280,1024]{2,1,0:T(8,128)(2,1)S(1)} %bitcast.49, bf16[800,1280]{1,0:T(8,128)(2,1)S(1)} %get-tuple-element.89.pool0_ref, bf16[800,1280]{1,0:T(8,128)(2,1)S(1)} %get-tuple-element.90.pool1_ref), custom_call_target="tpu_custom_call" | custom-call | flops 2097152000 | bytes 4096000 | tf_op jit(solution)/shard_map/coeff/pallas_call | solution.py:216
  113.8 0.1 collective-permute-start.33
  114.0 2.9 %coeff.3 = bf16[400,1024]{1,0:T(8,128)(2,1)S(1)} custom-call(s32[4]{0:T(128)S(1)} %pad_add_fusion.at_ref, bf16[2,1280,1024]{2,1,0:T(8,128)(2,1)S(1)} %bitcast.50, bf16[800,1280]{1,0:T(8,128)(2,1)S(1)} %get-tuple-element.89.pool0_ref, bf16[800,1280]{1,0:T(8,128)(2,1)S(1)} %get-tuple-element.90.pool1_ref), custom_call_target="tpu_custom_call" | custom-call | flops 2097152000 | bytes 4096000 | tf_op jit(solution)/shard_map/coeff/pallas_call | solution.py:216
  116.8 0.3 add_convert_fusion.2.chip_ref
  117.2 0.7 collective-permute-start.35
  117.8 20.3 %schulz.1 = (bf16[1024,1024]{1,0:T(8,128)(2,1)S(1)}, f32[8,128]{1,0:T(8,128)S(1)}) custom-call(bf16[1024,1024]{1,0:T(8,128)(2,1)S(1)} %get-tuple-element.97.own_ref, bf16[1024,1024]{1,0:T(8,128)(2,1)S(1)} %collective-permute-done.34.other_ref), custom_call_target="tpu_custom_call" | custom-call | flops 25769803776 | bytes 8388608 | tf_op jit(solution)/shard_map/schulz/pallas_call | solution.py:276
  138.2 0.2 collective-permute-done.35.over_ref
  138.4 1.9 %third.1.third_ref = bf16[400,1024]{1,0:T(8,128)(2,1)S(1)} custom-call(bf16[400,1024]{1,0:T(8,128)(2,1)S(1)} %add_convert_fusion.2.chip_ref, bf16[400,1024]{1,0:T(8,128)(2,1)S(1)} %collective-permute-done.35.over_ref, bf16[1024,1024]{1,0:T(8,128)(2,1)S(1)} %get-tuple-element.101.z_ref, f32[8,128]{1,0:T(8,128)S(1)} %get-tuple-element.102.frob_ref), custom_call_target="tpu_custom_call" | custom-call | tf_op jit(solution)/shard_map/third/pallas_call | solution.py:301
  140.3 1.3 collective-permute-start.36
  141.6 2.7 %merge.2 = (bf16[800,1280]{1,0:T(8,128)(2,1)}, bf16[1024,1280]{1,0:T(8,128)(2,1)S(1)}) custom-call(s32[4]{0:T(128)S(1)} %pad_add_fusion.at_ref, bf16[400,1024]{1,0:T(8,128)(2,1)S(1)} %third.1.third_ref, bf16[2,1280,1024]{2,1,0:T(8,128)(2,1)S(1)} %bitcast.51), custom_call_target="tpu_custom_call" | custom-call | flops 1048576000 | bytes 2621440 | tf_op jit(solution)/shard_map/merge/pallas_call | solution.py:344
  144.3 2.6 %merge.3 = bf16[800,1280]{1,0:T(8,128)(2,1)} custom-call(s32[4]{0:T(128)S(1)} %pad_add_fusion.at_ref, bf16[400,1024]{1,0:T(8,128)(2,1)S(1)} %collective-permute-done.36.third_ref, bf16[1024,1280]{1,0:T(8,128)(2,1)S(1)} %get-tuple-element.103.turned_ref, bf16[800,1280]{1,0:T(8,128)(2,1)} %get-tuple-element.104.so_far_any), custom_call_target="tpu_custom_call", output_to_operand_aliasing={{}: (3, {})} | custom-call | flops 1048576000 | bytes 2621440 | tf_op jit(solution)/shard_map/merge/pallas_call | solution.py:344
  (53 shorter events, 1.0 us)
Async XLA Ops:
  0.1 0.9 copy-start
  11.2 8.9 %collective-permute-start.8 = (bf16[2,4,80,128]{3,2,1,0:T(8,128)(2,1)S(1)}, bf16[2,4,80,128]{3,2,1,0:T(8,128)(2,1)S(1)}, u32[]{:S(2)}, u32[]{:S(2)}) collective-permute-start(bf16[2,4,80,128]{3,2,1,0:T(8,128)(2,1)S(1)} %get-tuple-element.67), channel_id=1, source_target_pairs={{0,3},{1,0},{2,1},{3,2},{4,7},{5,4},{6,5},{7,6},{8,11},{9,8},{10,9... | collective-permute-start | bytes 491528 | tf_op jit(solution)/shard_map/ppermute | solution.py:32
  15.9 9.9 %collective-permute-start = (bf16[2,4,80,128]{3,2,1,0:T(8,128)(2,1)S(1)}, bf16[2,4,80,128]{3,2,1,0:T(8,128)(2,1)S(1)}, u32[]{:S(2)}, u32[]{:S(2)}) collective-permute-start(bf16[2,4,80,128]{3,2,1,0:T(8,128)(2,1)S(1)} %get-tuple-element.60), channel_id=1, source_target_pairs={{0,8},{8,16},{16,24},{24,0},{1,9},{9,17},{17,25},{25,1},{2,10},{10... | collective-permute-start | bytes 491528 | tf_op jit(solution)/shard_map/ppermute | solution.py:32
  17.1 7.0 %collective-permute-start.2 = (bf16[2,4,80,128]{3,2,1,0:T(8,128)(2,1)S(1)}, bf16[2,4,80,128]{3,2,1,0:T(8,128)(2,1)S(1)}, u32[]{:S(2)}, u32[]{:S(2)}) collective-permute-start(bf16[2,4,80,128]{3,2,1,0:T(8,128)(2,1)S(1)} %get-tuple-element.62), channel_id=1, source_target_pairs={{0,24},{8,0},{16,8},{24,16},{1,25},{9,1},{17,9},{25,17},{2,26},{10... | collective-permute-start | bytes 491528 | tf_op jit(solution)/shard_map/ppermute | solution.py:32
  18.6 5.4 %collective-permute-start.6 = (bf16[2,4,80,128]{3,2,1,0:T(8,128)(2,1)S(1)}, bf16[2,4,80,128]{3,2,1,0:T(8,128)(2,1)S(1)}, u32[]{:S(2)}, u32[]{:S(2)}) collective-permute-start(bf16[2,4,80,128]{3,2,1,0:T(8,128)(2,1)S(1)} %get-tuple-element.65), channel_id=1, source_target_pairs={{0,1},{1,2},{2,3},{3,0},{4,5},{5,6},{6,7},{7,4},{8,9},{9,10},{10,1... | collective-permute-start | bytes 491528 | tf_op jit(solution)/shard_map/ppermute | solution.py:32
  18.6 59.9 %collective-permute-start.28 = (bf16[2,800,1280]{2,1,0:T(8,128)(2,1)}, bf16[2,800,1280]{2,1,0:T(8,128)(2,1)S(1)}, u32[]{:S(2)}, u32[]{:S(2)}) collective-permute-start(bf16[2,800,1280]{2,1,0:T(8,128)(2,1)} %get-tuple-element.70), channel_id=1, source_target_pairs={{0,32},{32,0},{1,33},{33,1},{2,34},{34,2},{3,35},{35,3},{4,36},{36... | collective-permute-start | bytes 12288008 | tf_op jit(solution)/shard_map/ppermute | solution.py:32
  20.2 9.5 %collective-permute-start.9 = (bf16[4,4,80,128]{3,2,1,0:T(8,128)(2,1)S(1)}, bf16[4,4,80,128]{3,2,1,0:T(8,128)(2,1)S(1)}, u32[]{:S(2)}, u32[]{:S(2)}) collective-permute-start(bf16[4,4,80,128]{3,2,1,0:T(8,128)(2,1)S(1)} %fusion.5), channel_id=1, source_target_pairs={{0,3},{1,0},{2,1},{3,2},{4,7},{5,4},{6,5},{7,6},{8,11},{9,8},{10,9... | collective-permute-start | bytes 983048 | tf_op jit(solution)/shard_map/ppermute | solution.py:32
  24.0 7.8 %collective-permute-start.7 = (bf16[4,4,80,128]{3,2,1,0:T(8,128)(2,1)S(1)}, bf16[4,4,80,128]{3,2,1,0:T(8,128)(2,1)S(1)}, u32[]{:S(2)}, u32[]{:S(2)}) collective-permute-start(bf16[4,4,80,128]{3,2,1,0:T(8,128)(2,1)S(1)} %fusion.4), channel_id=1, source_target_pairs={{0,1},{1,2},{2,3},{3,0},{4,5},{5,6},{6,7},{7,4},{8,9},{9,10},{10,1... | collective-permute-start | bytes 983048 | tf_op jit(solution)/shard_map/ppermute | solution.py:32
  24.2 7.8 %collective-permute-start.3 = (bf16[4,4,80,128]{3,2,1,0:T(8,128)(2,1)S(1)}, bf16[4,4,80,128]{3,2,1,0:T(8,128)(2,1)S(1)}, u32[]{:S(2)}, u32[]{:S(2)}) collective-permute-start(bf16[4,4,80,128]{3,2,1,0:T(8,128)(2,1)S(1)} %fusion.3), channel_id=1, source_target_pairs={{0,24},{8,0},{16,8},{24,16},{1,25},{9,1},{17,9},{25,17},{2,26},{10... | collective-permute-start | bytes 983048 | tf_op jit(solution)/shard_map/ppermute | solution.py:32
  25.9 7.8 %collective-permute-start.1 = (bf16[4,4,80,128]{3,2,1,0:T(8,128)(2,1)S(1)}, bf16[4,4,80,128]{3,2,1,0:T(8,128)(2,1)S(1)}, u32[]{:S(2)}, u32[]{:S(2)}) collective-permute-start(bf16[4,4,80,128]{3,2,1,0:T(8,128)(2,1)S(1)} %fusion.2), channel_id=1, source_target_pairs={{0,8},{8,16},{16,24},{24,0},{1,9},{9,17},{17,25},{25,1},{2,10},{10... | collective-permute-start | bytes 983048 | tf_op jit(solution)/shard_map/ppermute | solution.py:32
  31.9 4.5 %collective-permute-start.10 = (bf16[2,4,80,128]{3,2,1,0:T(8,128)(2,1)S(1)}, bf16[2,4,80,128]{3,2,1,0:T(8,128)(2,1)S(1)}, u32[]{:S(2)}, u32[]{:S(2)}) collective-permute-start(bf16[2,4,80,128]{3,2,1,0:T(8,128)(2,1)S(1)} %add_convert_fusion.5), channel_id=1, source_target_pairs={{0,8},{8,0},{16,24},{24,16},{1,9},{9,1},{17,25},{25,17},{2,10},{10... | collective-permute-start | bytes 491528 | tf_op jit(solution)/shard_map/ppermute | solution.py:380
  33.8 4.3 %collective-permute-start.4 = (bf16[2,4,80,128]{3,2,1,0:T(8,128)(2,1)S(1)}, bf16[2,4,80,128]{3,2,1,0:T(8,128)(2,1)S(1)}, u32[]{:S(2)}, u32[]{:S(2)}) collective-permute-start(bf16[2,4,80,128]{3,2,1,0:T(8,128)(2,1)S(1)} %add_convert_fusion.8), channel_id=1, source_target_pairs={{0,1},{1,0},{2,3},{3,2},{4,5},{5,4},{6,7},{7,6},{8,9},{9,8},{10,11... | collective-permute-start | bytes 491528 | tf_op jit(solution)/shard_map/ppermute | solution.py:380
  36.5 4.6 %collective-permute-start.11 = (bf16[4,80,128]{2,1,0:T(8,128)(2,1)S(1)}, bf16[4,80,128]{2,1,0:T(8,128)(2,1)S(1)}, u32[]{:S(2)}, u32[]{:S(2)}) collective-permute-start(bf16[4,80,128]{2,1,0:T(8,128)(2,1)S(1)} %fusion.12), channel_id=1, source_target_pairs={{0,24},{24,0},{8,16},{16,8},{1,25},{25,1},{9,17},{17,9},{2,26},{26... | collective-permute-start | bytes 245768 | tf_op jit(solution)/shard_map/ppermute | solution.py:382
  38.1 4.6 %collective-permute-start.5 = (bf16[4,80,128]{2,1,0:T(8,128)(2,1)S(1)}, bf16[4,80,128]{2,1,0:T(8,128)(2,1)S(1)}, u32[]{:S(2)}, u32[]{:S(2)}) collective-permute-start(bf16[4,80,128]{2,1,0:T(8,128)(2,1)S(1)} %fusion.10), channel_id=1, source_target_pairs={{0,3},{3,0},{1,2},{2,1},{4,7},{7,4},{5,6},{6,5},{8,11},{11,8},{9,1... | collective-permute-start | bytes 245768 | tf_op jit(solution)/shard_map/ppermute | solution.py:382
  42.8 6.9 %collective-permute-start.12 = (bf16[2,80,256]{2,1,0:T(8,128)(2,1)S(1)}, bf16[2,80,256]{2,1,0:T(8,128)(2,1)S(1)}, u32[]{:S(2)}, u32[]{:S(2)}) collective-permute-start(bf16[2,80,256]{2,1,0:T(8,128)(2,1)S(1)} %select_bitcast_fusion), channel_id=1, source_target_pairs={{0,32},{32,0},{1,33},{33,1},{2,34},{34,2},{3,35},{35,3},{4,36},{36... | collective-permute-start | bytes 245768 | tf_op jit(solution)/shard_map/ppermute | solution.py:32
  49.8 6.8 %collective-permute-start.14 = (bf16[2,80,512]{2,1,0:T(8,128)(2,1)S(1)}, bf16[2,80,512]{2,1,0:T(8,128)(2,1)S(1)}, u32[]{:S(2)}, u32[]{:S(2)}) collective-permute-start(bf16[2,80,512]{2,1,0:T(8,128)(2,1)S(1)} %pad_maximum_fusion.2), channel_id=1, source_target_pairs={{0,4},{4,64},{64,68},{68,0},{1,5},{5,65},{65,69},{69,1},{2,6},{6,6... | collective-permute-start | bytes 491528 | tf_op jit(solution)/shard_map/ppermute | solution.py:32
  51.2 5.5 %collective-permute-start.13 = (bf16[2,80,512]{2,1,0:T(8,128)(2,1)S(1)}, bf16[2,80,512]{2,1,0:T(8,128)(2,1)S(1)}, u32[]{:S(2)}, u32[]{:S(2)}) collective-permute-start(bf16[2,80,512]{2,1,0:T(8,128)(2,1)S(1)} %pad_maximum_fusion.2), channel_id=1, source_target_pairs={{0,68},{4,0},{64,4},{68,64},{1,69},{5,1},{65,5},{69,65},{2,70},{6,... | collective-permute-start | bytes 491528 | tf_op jit(solution)/shard_map/ppermute | solution.py:32
  52.7 8.6 %collective-permute-start.15 = (bf16[2,80,512]{2,1,0:T(8,128)(2,1)S(1)}, bf16[2,80,512]{2,1,0:T(8,128)(2,1)S(1)}, u32[]{:S(2)}, u32[]{:S(2)}) collective-permute-start(bf16[2,80,512]{2,1,0:T(8,128)(2,1)S(1)} %pad_maximum_fusion.2), channel_id=1, source_target_pairs={{0,64},{4,68},{64,0},{68,4},{1,65},{5,69},{65,1},{69,5},{2,66},{6,... | collective-permute-start | bytes 491528 | tf_op jit(solution)/shard_map/ppermute | solution.py:32
  61.4 17.0 %copy-start.1 = (bf16[2,800,1280]{2,1,0:T(8,128)(2,1)S(1)}, bf16[2,800,1280]{2,1,0:T(8,128)(2,1)}, u32[]{:S(2)}) copy-start(bf16[2,800,1280]{2,1,0:T(8,128)(2,1)} %get-tuple-element.69) | copy-start | bytes 12288004
  61.5 4.6 %collective-permute-start.17 = (bf16[1,80,1024]{2,1,0:T(8,128)(2,1)S(1)}, bf16[1,80,1024]{2,1,0:T(8,128)(2,1)S(1)}, u32[]{:S(2)}, u32[]{:S(2)}) collective-permute-start(bf16[1,80,1024]{2,1,0:T(8,128)(2,1)S(1)} %get-tuple-element.111), channel_id=1, source_target_pairs={{0,24},{8,0},{16,8},{24,16},{1,25},{9,1},{17,9},{25,17},{2,26},{10... | collective-permute-start | bytes 491528 | tf_op jit(solution)/shard_map/ppermute | solution.py:32
  62.7 5.7 %collective-permute-start.16 = (bf16[1,80,1024]{2,1,0:T(8,128)(2,1)S(1)}, bf16[1,80,1024]{2,1,0:T(8,128)(2,1)S(1)}, u32[]{:S(2)}, u32[]{:S(2)}) collective-permute-start(bf16[1,80,1024]{2,1,0:T(8,128)(2,1)S(1)} %get-tuple-element.111), channel_id=1, source_target_pairs={{0,8},{8,16},{16,24},{24,0},{1,9},{9,17},{17,25},{25,1},{2,10},{10... | collective-permute-start | bytes 491528 | tf_op jit(solution)/shard_map/ppermute | solution.py:32
  63.0 5.5 %collective-permute-start.23 = (bf16[1,80,1024]{2,1,0:T(8,128)(2,1)S(1)}, bf16[1,80,1024]{2,1,0:T(8,128)(2,1)S(1)}, u32[]{:S(2)}, u32[]{:S(2)}) collective-permute-start(bf16[1,80,1024]{2,1,0:T(8,128)(2,1)S(1)} %get-tuple-element.110), channel_id=1, source_target_pairs={{0,3},{1,0},{2,1},{3,2},{4,7},{5,4},{6,5},{7,6},{8,11},{9,8},{10,9... | collective-permute-start | bytes 491528 | tf_op jit(solution)/shard_map/ppermute | solution.py:32
  65.6 5.7 %collective-permute-start.22 = (bf16[1,80,1024]{2,1,0:T(8,128)(2,1)S(1)}, bf16[1,80,1024]{2,1,0:T(8,128)(2,1)S(1)}, u32[]{:S(2)}, u32[]{:S(2)}) collective-permute-start(bf16[1,80,1024]{2,1,0:T(8,128)(2,1)S(1)} %get-tuple-element.110), channel_id=1, source_target_pairs={{0,1},{1,2},{2,3},{3,0},{4,5},{5,6},{6,7},{7,4},{8,9},{9,10},{10,1... | collective-permute-start | bytes 491528 | tf_op jit(solution)/shard_map/ppermute | solution.py:32
  66.1 5.3 %collective-permute-start.19 = (bf16[1,80,512]{2,1,0:T(8,128)(2,1)S(1)}, bf16[1,80,512]{2,1,0:T(8,128)(2,1)S(1)}, u32[]{:S(2)}, u32[]{:S(2)}) collective-permute-start(bf16[1,80,512]{2,1,0:T(8,128)(2,1)S(1)} %slice.191), channel_id=1, source_target_pairs={{0,24},{8,0},{16,8},{24,16},{1,25},{9,1},{17,9},{25,17},{2,26},{10... | collective-permute-start | bytes 245768 | tf_op jit(solution)/shard_map/ppermute | solution.py:32
  68.4 4.9 %collective-permute-start.18 = (bf16[1,80,512]{2,1,0:T(8,128)(2,1)S(1)}, bf16[1,80,512]{2,1,0:T(8,128)(2,1)S(1)}, u32[]{:S(2)}, u32[]{:S(2)}) collective-permute-start(bf16[1,80,512]{2,1,0:T(8,128)(2,1)S(1)} %slice.190), channel_id=1, source_target_pairs={{0,8},{8,16},{16,24},{24,0},{1,9},{9,17},{17,25},{25,1},{2,10},{10... | collective-permute-start | bytes 245768 | tf_op jit(solution)/shard_map/ppermute | solution.py:32
  68.5 7.1 %collective-permute-start.25 = (bf16[1,80,512]{2,1,0:T(8,128)(2,1)S(1)}, bf16[1,80,512]{2,1,0:T(8,128)(2,1)S(1)}, u32[]{:S(2)}, u32[]{:S(2)}) collective-permute-start(bf16[1,80,512]{2,1,0:T(8,128)(2,1)S(1)} %slice.193), channel_id=1, source_target_pairs={{0,3},{1,0},{2,1},{3,2},{4,7},{5,4},{6,5},{7,6},{8,11},{9,8},{10,9... | collective-permute-start | bytes 245768 | tf_op jit(solution)/shard_map/ppermute | solution.py:32
  71.3 4.8 %collective-permute-start.24 = (bf16[1,80,512]{2,1,0:T(8,128)(2,1)S(1)}, bf16[1,80,512]{2,1,0:T(8,128)(2,1)S(1)}, u32[]{:S(2)}, u32[]{:S(2)}) collective-permute-start(bf16[1,80,512]{2,1,0:T(8,128)(2,1)S(1)} %slice.192), channel_id=1, source_target_pairs={{0,1},{1,2},{2,3},{3,0},{4,5},{5,6},{6,7},{7,4},{8,9},{9,10},{10,1... | collective-permute-start | bytes 245768 | tf_op jit(solution)/shard_map/ppermute | solution.py:32
  73.3 13.1 %collective-permute-start.21 = (bf16[4,80,1024]{2,1,0:T(8,128)(2,1)S(1)}, bf16[4,80,1024]{2,1,0:T(8,128)(2,1)S(1)}, u32[]{:S(2)}, u32[]{:S(2)}) collective-permute-start(bf16[4,80,1024]{2,1,0:T(8,128)(2,1)S(1)} %maximum_maximum_fusion.a0), channel_id=1, source_target_pairs={{0,3},{1,0},{2,1},{3,2},{4,7},{5,4},{6,5},{7,6},{8,11},{9,8},{10,9... | collective-permute-start | bytes 1966088 | tf_op jit(solution)/shard_map/ppermute | solution.py:32
  75.6 13.6 %collective-permute-start.20 = (bf16[4,80,1024]{2,1,0:T(8,128)(2,1)S(1)}, bf16[4,80,1024]{2,1,0:T(8,128)(2,1)S(1)}, u32[]{:S(2)}, u32[]{:S(2)}) collective-permute-start(bf16[4,80,1024]{2,1,0:T(8,128)(2,1)S(1)} %maximum_maximum_fusion.a0), channel_id=1, source_target_pairs={{0,1},{1,2},{2,3},{3,0},{4,5},{5,6},{6,7},{7,4},{8,9},{9,10},{10,1... | collective-permute-start | bytes 1966088 | tf_op jit(solution)/shard_map/ppermute | solution.py:32
  76.2 13.0 %collective-permute-start.27 = (bf16[4,80,1024]{2,1,0:T(8,128)(2,1)S(1)}, bf16[4,80,1024]{2,1,0:T(8,128)(2,1)S(1)}, u32[]{:S(2)}, u32[]{:S(2)}) collective-permute-start(bf16[4,80,1024]{2,1,0:T(8,128)(2,1)S(1)} %maximum_maximum_fusion.1.b0), channel_id=1, source_target_pairs={{0,24},{8,0},{16,8},{24,16},{1,25},{9,1},{17,9},{25,17},{2,26},{10... | collective-permute-start | bytes 1966088 | tf_op jit(solution)/shard_map/ppermute | solution.py:32
  78.4 12.2 %collective-permute-start.26 = (bf16[4,80,1024]{2,1,0:T(8,128)(2,1)S(1)}, bf16[4,80,1024]{2,1,0:T(8,128)(2,1)S(1)}, u32[]{:S(2)}, u32[]{:S(2)}) collective-permute-start(bf16[4,80,1024]{2,1,0:T(8,128)(2,1)S(1)} %maximum_maximum_fusion.1.b0), channel_id=1, source_target_pairs={{0,8},{8,16},{16,24},{24,0},{1,9},{9,17},{17,25},{25,1},{2,10},{10... | collective-permute-start | bytes 1966088 | tf_op jit(solution)/shard_map/ppermute | solution.py:32
  90.7 7.3 %collective-permute-start.32 = (bf16[2,80,1024]{2,1,0:T(8,128)(2,1)S(1)}, bf16[2,80,1024]{2,1,0:T(8,128)(2,1)S(1)}, u32[]{:S(2)}, u32[]{:S(2)}) collective-permute-start(bf16[2,80,1024]{2,1,0:T(8,128)(2,1)S(1)} %slice.169), channel_id=1, source_target_pairs={{0,24},{8,0},{16,8},{24,16},{1,25},{9,1},{17,9},{25,17},{2,26},{10... | collective-permute-start | bytes 983048 | tf_op jit(solution)/shard_map/ppermute | solution.py:32
  92.4 7.1 %collective-permute-start.31 = (bf16[2,80,1024]{2,1,0:T(8,128)(2,1)S(1)}, bf16[2,80,1024]{2,1,0:T(8,128)(2,1)S(1)}, u32[]{:S(2)}, u32[]{:S(2)}) collective-permute-start(bf16[2,80,1024]{2,1,0:T(8,128)(2,1)S(1)} %slice.168), channel_id=1, source_target_pairs={{0,8},{8,16},{16,24},{24,0},{1,9},{9,17},{17,25},{25,1},{2,10},{10... | collective-permute-start | bytes 983048 | tf_op jit(solution)/shard_map/ppermute | solution.py:32
  92.5 7.1 %collective-permute-start.30 = (bf16[2,80,1024]{2,1,0:T(8,128)(2,1)S(1)}, bf16[2,80,1024]{2,1,0:T(8,128)(2,1)S(1)}, u32[]{:S(2)}, u32[]{:S(2)}) collective-permute-start(bf16[2,80,1024]{2,1,0:T(8,128)(2,1)S(1)} %slice.167), channel_id=1, source_target_pairs={{0,3},{1,0},{2,1},{3,2},{4,7},{5,4},{6,5},{7,6},{8,11},{9,8},{10,9... | collective-permute-start | bytes 983048 | tf_op jit(solution)/shard_map/ppermute | solution.py:32
  94.4 7.4 %collective-permute-start.29 = (bf16[2,80,1024]{2,1,0:T(8,128)(2,1)S(1)}, bf16[2,80,1024]{2,1,0:T(8,128)(2,1)S(1)}, u32[]{:S(2)}, u32[]{:S(2)}) collective-permute-start(bf16[2,80,1024]{2,1,0:T(8,128)(2,1)S(1)} %slice.166), channel_id=1, source_target_pairs={{0,1},{1,2},{2,3},{3,0},{4,5},{5,6},{6,7},{7,4},{8,9},{9,10},{10,1... | collective-permute-start | bytes 983048 | tf_op jit(solution)/shard_map/ppermute | solution.py:32
  104.0 12.8 %collective-permute-start.34 = (bf16[1024,1024]{1,0:T(8,128)(2,1)S(1)}, bf16[1024,1024]{1,0:T(8,128)(2,1)S(1)}, u32[]{:S(2)}, u32[]{:S(2)}) collective-permute-start(bf16[1024,1024]{1,0:T(8,128)(2,1)S(1)} %get-tuple-element.97.own_ref), channel_id=1, source_target_pairs={{0,32},{32,0},{1,33},{33,1},{2,34},{34,2},{3,35},{35,3},{4,36},{36... | collective-permute-start | bytes 6291464 | tf_op jit(solution)/shard_map/ppermute | solution.py:32
  113.8 3.0 %collective-permute-start.33 = (bf16[400,1024]{1,0:T(8,128)(2,1)S(1)}, bf16[400,1024]{1,0:T(8,128)(2,1)S(1)}, u32[]{:S(2)}, u32[]{:S(2)}) collective-permute-start(bf16[400,1024]{1,0:T(8,128)(2,1)S(1)} %coeff.2), channel_id=1, source_target_pairs={{0,32},{32,0},{1,33},{33,1},{2,34},{34,2},{3,35},{35,3},{4,36},{36... | collective-permute-start | bytes 2457608 | tf_op jit(solution)/shard_map/ppermute | solution.py:32
  117.2 21.2 %collective-permute-start.35 = (bf16[400,1024]{1,0:T(8,128)(2,1)S(1)}, bf16[400,1024]{1,0:T(8,128)(2,1)S(1)}, u32[]{:S(2)}, u32[]{:S(2)}) collective-permute-start(bf16[400,1024]{1,0:T(8,128)(2,1)S(1)} %add_convert_fusion.2.chip_ref), channel_id=1, source_target_pairs={{0,64},{64,0},{1,65},{65,1},{2,66},{66,2},{3,67},{67,3},{4,68},{68... | collective-permute-start | bytes 2457608 | tf_op jit(solution)/shard_map/ppermute | solution.py:32
  140.3 4.0 %collective-permute-start.36 = (bf16[400,1024]{1,0:T(8,128)(2,1)S(1)}, bf16[400,1024]{1,0:T(8,128)(2,1)S(1)}, u32[]{:S(2)}, u32[]{:S(2)}) collective-permute-start(bf16[400,1024]{1,0:T(8,128)(2,1)S(1)} %third.1.third_ref), channel_id=1, source_target_pairs={{0,32},{32,0},{1,33},{33,1},{2,34},{34,2},{3,35},{35,3},{4,36},{36... | collective-permute-start | bytes 2457608 | tf_op jit(solution)/shard_map/ppermute | solution.py:32

commit v2 on v1

--- a/solution.py
+++ b/solution.py
@@ -308,55 +308,63 @@
     )(chip_sum, over, z, frob)
 
 
-def merge_own_kernel(at_ref, third_ref, chunk_ref, out_any, turned_ref, stage_ref, sem):
-    merge_rows(at_ref, at_ref[3], third_ref, turned_ref, out_any, stage_ref, sem, chunk_ref)
-
-
-def merge_twin_kernel(at_ref, third_ref, turned_ref, so_far_any, out_any, stage_ref, sem):
-    merge_rows(at_ref, 1 - at_ref[3], third_ref, turned_ref, out_any, stage_ref, sem)
-
-
-def merge_rows(at_ref, which, third_ref, turned_ref, out_any, stage_ref, sem, chunk_ref=None):
-    half, width = stage_ref.shape
-    rows = pl.ds(pl.multiple_of(which * half, 16), half)
-    copies = []
-    for i in range(0, width, MERGE_BLOCK):
+def merge_own_kernel(at_ref, third_ref, basis_ref, out_ref, turned_ref):
+    for i in range(0, out_ref.shape[1], MERGE_BLOCK):
         columns = slice(i, i + MERGE_BLOCK)
-        if chunk_ref is not None:
-            turned_ref[:, columns] = chunk_ref[at_ref[2], columns, :].T
-        stage_ref[:, columns] = jnp.dot(
+        turned_ref[:, columns] = basis_ref[at_ref[2], columns, :].T
+        out_ref[:, columns] = jnp.dot(
             third_ref[...], turned_ref[:, columns], preferred_element_type=F32
         ).astype(BF)
-        target = out_any.at[rows, pl.ds(i, MERGE_BLOCK)]
-        copies.append(pltpu.make_async_copy(stage_ref.at[:, columns], target, sem.at[len(copies)]))
-        copies[-1].start()
-    for copy in copies:
-        copy.wait()
-
-
-def merge_call(at, third, chunk, so_far=None):
+
+
+def merge_own_call(at, third, basis):
     rows, width = third.shape
-    first = so_far is None
-    columns = chunk.shape[1]
-    anywhere = pl.BlockSpec(memory_space=pl.ANY)
-    merged = jax.ShapeDtypeStruct((2 * rows, columns), BF)
-    turned = jax.ShapeDtypeStruct((width, columns), BF)
-    return pl.pallas_call(
-        merge_own_kernel if first else merge_twin_kernel,
-        in_specs=[pl.BlockSpec(memory_space=pltpu.SMEM), whole(), whole()] + ([] if first else [anywhere]),
-        out_specs=[anywhere, whole()] if first else anywhere,
-        out_shape=[merged, turned] if first else merged,
-        input_output_aliases={} if first else {3: 0},
-        scratch_shapes=[
-            pltpu.VMEM((rows, columns), BF),
-            pltpu.SemaphoreType.DMA((columns // MERGE_BLOCK,)),
-        ],
+    columns = basis.shape[1]
+    return pl.pallas_call(
+        merge_own_kernel,
+        in_specs=[pl.BlockSpec(memory_space=pltpu.SMEM), whole(), whole()],
+        out_specs=[whole(), whole()],
+        out_shape=[jax.ShapeDtypeStruct((rows, columns), BF), jax.ShapeDtypeStruct((width, columns), BF)],
         cost_estimate=pl.CostEstimate(
             flops=2 * rows * columns * width, bytes_accessed=2 * columns * width, transcendentals=0
         ),
         compiler_params=params(),
+        name="merge_own",
+    )(at, third, basis)
+
+
+def merge_kernel(at_ref, third_ref, turned_ref, own_ref, out_any, twin_ref, sem):
+    half, width = own_ref.shape
+    own_rows = pl.ds(pl.multiple_of(at_ref[3] * half, 16), half)
+    twin_rows = pl.ds(pl.multiple_of((1 - at_ref[3]) * half, 16), half)
+    copies = [pltpu.make_async_copy(own_ref, out_any.at[own_rows, :], sem.at[0])]
+    copies[0].start()
+    for i in range(0, width, MERGE_BLOCK):
+        columns = slice(i, i + MERGE_BLOCK)
+        twin_ref[:, columns] = jnp.dot(
+            third_ref[...], turned_ref[:, columns], preferred_element_type=F32
+        ).astype(BF)
+        target = out_any.at[twin_rows, pl.ds(i, MERGE_BLOCK)]
+        copies.append(pltpu.make_async_copy(twin_ref.at[:, columns], target, sem.at[len(copies)]))
+        copies[-1].start()
+    for copy in copies:
+        copy.wait()
+
+
+def merge_call(at, third, turned, own):
+    rows, columns = own.shape
+    return pl.pallas_call(
+        merge_kernel,
+        in_specs=[pl.BlockSpec(memory_space=pltpu.SMEM)] + [whole()] * 3,
+        out_specs=pl.BlockSpec(memory_space=pl.ANY),
+        out_shape=jax.ShapeDtypeStruct((2 * rows, columns), BF),
+        scratch_shapes=[
+            pltpu.VMEM((rows, columns), BF),
+            pltpu.SemaphoreType.DMA((1 + columns // MERGE_BLOCK,)),
+        ],
+        compiler_params=params(),
         name="merge",
-    )(at, third, chunk, *([] if first else [so_far]))
+    )(at, third, turned, own)
 
 
 def add(*values):
@@ -418,7 +426,10 @@
     chip = jnp.concatenate(
         [jnp.where(core0, keep, got), jnp.where(core0, got, keep)], axis=2
     )
-    below, above, across = [shift(chip, RING_Y, step) for step in (1, -1, 2)]
+    pooled = [add(pool_keep[i], pool_got[i]) for i in range(2)]
+    (below, above, across), pooled = lax.optimization_barrier(
+        ([shift(chip, RING_Y, step) for step in (1, -1, 2)], pooled)
+    )
     ours = add(chip, jnp.where(yl0, above, below))
     theirs = add(across, jnp.where(yl0, below, above))
     local = jnp.concatenate([jnp.where(yh0, ours, theirs), jnp.where(yh0, theirs, ours)], axis=2)
@@ -431,8 +442,6 @@
     ]
     items = [(jnp.concatenate([*n, f]), axis) for n, f, axis in zip(near, far, ("z", "x"))]
     near, second = ring_gather(items)
-    pooled = [add(pool_keep[i], pool_got[i]) for i in range(2)]
-    near, pooled = lax.optimization_barrier((near, pooled))
     far = second(near)
     acc, basis = gram_first_call(at, near[0] + near[1])
     far, acc, basis = lax.optimization_barrier((far, acc, basis))
@@ -451,7 +460,7 @@
     total_tasks = tasks * lax.axis_size("yh") * lax.axis_size("core")
     third = third_call(chip_sum, over, inverse_root, frob, total_tasks)
     third_twin = shift(third, "core", 1)
-    merged, turned = merge_call(at, third, basis)
+    merged, turned = merge_own_call(at, third, basis)
     return merge_call(at, third_twin, turned, merged)
 
 

time: 147 us -> 145 us (0.986)
  transfers between devices with their start and end apart: 37 -> 37, of which waited for: 19 -> 20; matrix products, arithmetic and copies ran while one was open for 2% -> 1% of each run, Pallas kernels for 22% -> 22%
where the time goes in v2:
time: 145 us
  starting transfers between devices  54.8 us (38%)
  Pallas kernels  48.4 us (33%)
  waiting for transfers between devices  37.7 us (26%)
  other arithmetic  2.53 us (2%)
    ppermute x33, starting transfers between devices, shift(): lax.ppermute(value, axis, [(i, (i + step) % size) for i in range(size)])  50.6 us
    ppermute x33, waiting for transfers between devices, shift(): lax.ppermute(value, axis, [(i, (i + step) % size) for i in range(size)])  33 us
    pallas_call x1, Pallas kernels, schulz_call(): pl.pallas_call(schulz_kernel, in_specs=[whole()] * 2, out_specs=[whole()]...  20.3 us
    pallas_call x1, Pallas kernels, sketch_call(): pl.pallas_call(sketch_kernel, in_specs=[pl.BlockSpec(memory_space=pltpu.S...  10.2 us
    pallas_call x2, Pallas kernels, coeff_call(): pl.pallas_call(functools.partial(coeff_kernel, own=own), in_specs=[pl.Blo...  5.66 us
    ppermute x2, starting transfers between devices, halving_reduce(): lax.ppermute(other, axis, [(0, 3), (3, 0), (1, 2), (2, 1)])  4.01 us
    pallas_call x1, Pallas kernels, gram_first_call(): pl.pallas_call(gram_first_kernel, in_specs=[pl.BlockSpec(memory_space=plt...  3.62 us
  transfers between devices with their start and end apart: 37, of which 20 were waited for; matrix products, arithmetic and copies ran while one was open for 1% of the time, Pallas kernels for 22%

profile of v2, /device:TPU:1, one launch (start us, length us, event | category | flops | bytes accessed | tf_op | source)
XLA Modules:
  0.0 145.0 jit_solution(9670958754315353044)
XLA Ops:
  0.1 0.9 copy-done
  1.0 10.2 %sketch.1 = (bf16[4,4,80,128]{3,2,1,0:T(8,128)(2,1)S(1)}, bf16[4,4,80,128]{3,2,1,0:T(8,128)(2,1)S(1)}, bf16[4,4,80,128]{3,2,1,0:T(8,128)(2,1)S(1)}, bf16[2,4,80,...) custom-call(s32[4]{0:T(128)S(1)} %pad_add_fusion.at_ref, ...), custom_call_target="tpu_custom_call" | custom-call | tf_op jit(solution)/shard_map/sketch/pallas_call | solution.py:99
  11.2 1.6 %collective-permute-start.16 = (bf16[2,800,1280]{2,1,0:T(8,128)(2,1)}, bf16[2,800,1280]{2,1,0:T(8,128)(2,1)S(1)}, u32[]{:S(2)}, u32[]{:S(2)}) collective-permute-start(bf16[2,800,1280]{2,1,0:T(8,128)(2,1)} %get-tuple-element.67), channel_id=1, source_target_pairs={{0,32},{32,0},{1,33},{33,1},{2,34},{34,2},{3,35},{35,3},{4,36},{36... | collective-permute-start | bytes 12288008 | tf_op jit(solution)/shard_map/ppermute | solution.py:32
  12.8 3.9 %collective-permute-start.8 = (bf16[2,4,80,128]{3,2,1,0:T(8,128)(2,1)S(1)}, bf16[2,4,80,128]{3,2,1,0:T(8,128)(2,1)S(1)}, u32[]{:S(2)}, u32[]{:S(2)}) collective-permute-start(bf16[2,4,80,128]{3,2,1,0:T(8,128)(2,1)S(1)} %get-tuple-element.64), channel_id=1, source_target_pairs={{0,3},{1,0},{2,1},{3,2},{4,7},{5,4},{6,5},{7,6},{8,11},{9,8},{10,9... | collective-permute-start | bytes 491528 | tf_op jit(solution)/shard_map/ppermute | solution.py:32
  16.6 1.2 collective-permute-start
  17.9 1.5 %collective-permute-start.2 = (bf16[2,4,80,128]{3,2,1,0:T(8,128)(2,1)S(1)}, bf16[2,4,80,128]{3,2,1,0:T(8,128)(2,1)S(1)}, u32[]{:S(2)}, u32[]{:S(2)}) collective-permute-start(bf16[2,4,80,128]{3,2,1,0:T(8,128)(2,1)S(1)} %get-tuple-element.59), channel_id=1, source_target_pairs={{0,24},{8,0},{16,8},{24,16},{1,25},{9,1},{17,9},{25,17},{2,26},{10... | collective-permute-start | bytes 491528 | tf_op jit(solution)/shard_map/ppermute | solution.py:32
  19.3 0.9 collective-permute-done.8
  20.2 0.1 fusion.5
  20.3 3.5 %collective-permute-start.9 = (bf16[4,4,80,128]{3,2,1,0:T(8,128)(2,1)S(1)}, bf16[4,4,80,128]{3,2,1,0:T(8,128)(2,1)S(1)}, u32[]{:S(2)}, u32[]{:S(2)}) collective-permute-start(bf16[4,4,80,128]{3,2,1,0:T(8,128)(2,1)S(1)} %fusion.5), channel_id=1, source_target_pairs={{0,3},{1,0},{2,1},{3,2},{4,7},{5,4},{6,5},{7,6},{8,11},{9,8},{10,9... | collective-permute-start | bytes 983048 | tf_op jit(solution)/shard_map/ppermute | solution.py:32
  23.8 1.6 %collective-permute-done.6 = bf16[2,4,80,128]{3,2,1,0:T(8,128)(2,1)S(1)} collective-permute-done((bf16[2,4,80,128]{3,2,1,0:T(8,128)(2,1)S(1)}, bf16[2,4,80,128]{3,2,1,0:T(8,128)(2,1)S(1)}, u32[]{:S(2)}, u32[]{:S(2)}) %collective-permute-start.6) | collective-permute-done | bytes 163872 | tf_op jit(solution)/shard_map/ppermute | solution.py:32
  25.3 0.1 fusion.4
  25.5 0.1 fusion.3
  25.6 1.3 collective-permute-start.3
  26.9 0.1 fusion.2
  27.0 0.3 collective-permute-start.1
  27.3 2.6 %collective-permute-done.9 = bf16[4,4,80,128]{3,2,1,0:T(8,128)(2,1)S(1)} collective-permute-done((bf16[4,4,80,128]{3,2,1,0:T(8,128)(2,1)S(1)}, bf16[4,4,80,128]{3,2,1,0:T(8,128)(2,1)S(1)}, u32[]{:S(2)}, u32[]{:S(2)}) %collective-permute-start.9) | collective-permute-done | bytes 327712 | tf_op jit(solution)/shard_map/ppermute | solution.py:32
  29.9 4.2 %collective-permute-done.7 = bf16[4,4,80,128]{3,2,1,0:T(8,128)(2,1)S(1)} collective-permute-done((bf16[4,4,80,128]{3,2,1,0:T(8,128)(2,1)S(1)}, bf16[4,4,80,128]{3,2,1,0:T(8,128)(2,1)S(1)}, u32[]{:S(2)}, u32[]{:S(2)}) %collective-permute-start.7) | collective-permute-done | bytes 327712 | tf_op jit(solution)/shard_map/ppermute | solution.py:32
  34.1 0.1 collective-permute-start.10
  34.3 1.1 collective-permute-done.1
  35.5 0.1 collective-permute-start.4
  35.6 2.8 %collective-permute-done.10 = bf16[2,4,80,128]{3,2,1,0:T(8,128)(2,1)S(1)} collective-permute-done((bf16[2,4,80,128]{3,2,1,0:T(8,128)(2,1)S(1)}, bf16[2,4,80,128]{3,2,1,0:T(8,128)(2,1)S(1)}, u32[]{:S(2)}, u32[]{:S(2)}) %collective-permute-start.10) | collective-permute-done | bytes 163872 | tf_op jit(solution)/shard_map/ppermute | solution.py:388
  38.4 1.3 collective-permute-start.11
  39.8 2.7 %collective-permute-start.5 = (bf16[4,80,128]{2,1,0:T(8,128)(2,1)S(1)}, bf16[4,80,128]{2,1,0:T(8,128)(2,1)S(1)}, u32[]{:S(2)}, u32[]{:S(2)}) collective-permute-start(bf16[4,80,128]{2,1,0:T(8,128)(2,1)S(1)} %fusion.10), channel_id=1, source_target_pairs={{0,3},{3,0},{1,2},{2,1},{4,7},{7,4},{5,6},{6,5},{8,11},{11,8},{9,1... | collective-permute-start | bytes 245768 | tf_op jit(solution)/shard_map/ppermute | solution.py:390
  42.5 0.5 collective-permute-done.11
  43.1 1.3 collective-permute-done.5
  44.5 5.4 %collective-permute-start.12 = (bf16[2,80,256]{2,1,0:T(8,128)(2,1)S(1)}, bf16[2,80,256]{2,1,0:T(8,128)(2,1)S(1)}, u32[]{:S(2)}, u32[]{:S(2)}) collective-permute-start(bf16[2,80,256]{2,1,0:T(8,128)(2,1)S(1)} %select_bitcast_fusion), channel_id=1, source_target_pairs={{0,32},{32,0},{1,33},{33,1},{2,34},{34,2},{3,35},{35,3},{4,36},{36... | collective-permute-start | bytes 245768 | tf_op jit(solution)/shard_map/ppermute | solution.py:32
  49.9 0.9 collective-permute-done.12
  50.9 2.8 %collective-permute-start.14 = (bf16[2,80,512]{2,1,0:T(8,128)(2,1)S(1)}, bf16[2,80,512]{2,1,0:T(8,128)(2,1)S(1)}, u32[]{:S(2)}, u32[]{:S(2)}) collective-permute-start(bf16[2,80,512]{2,1,0:T(8,128)(2,1)S(1)} %pad_maximum_fusion.2), channel_id=1, source_target_pairs={{0,68},{4,0},{64,4},{68,64},{1,69},{5,1},{65,5},{69,65},{2,70},{6,... | collective-permute-start | bytes 491528 | tf_op jit(solution)/shard_map/ppermute | solution.py:32
  53.7 1.6 %collective-permute-start.15 = (bf16[2,80,512]{2,1,0:T(8,128)(2,1)S(1)}, bf16[2,80,512]{2,1,0:T(8,128)(2,1)S(1)}, u32[]{:S(2)}, u32[]{:S(2)}) collective-permute-start(bf16[2,80,512]{2,1,0:T(8,128)(2,1)S(1)} %pad_maximum_fusion.2), channel_id=1, source_target_pairs={{0,64},{4,68},{64,0},{68,4},{1,65},{5,69},{65,1},{69,5},{2,66},{6,... | collective-permute-start | bytes 491528 | tf_op jit(solution)/shard_map/ppermute | solution.py:32
  55.4 1.1 fusion.1
  56.5 0.4 collective-permute-done.14
  56.9 4.1 %collective-permute-done.13 = bf16[2,80,512]{2,1,0:T(8,128)(2,1)S(1)} collective-permute-done((bf16[2,80,512]{2,1,0:T(8,128)(2,1)S(1)}, bf16[2,80,512]{2,1,0:T(8,128)(2,1)S(1)}, u32[]{:S(2)}, u32[]{:S(2)}) %collective-permute-start.13) | collective-permute-done | bytes 163872 | tf_op jit(solution)/shard_map/ppermute | solution.py:32
  61.0 1.5 %collective-permute-done.15 = bf16[2,80,512]{2,1,0:T(8,128)(2,1)S(1)} collective-permute-done((bf16[2,80,512]{2,1,0:T(8,128)(2,1)S(1)}, bf16[2,80,512]{2,1,0:T(8,128)(2,1)S(1)}, u32[]{:S(2)}, u32[]{:S(2)}) %collective-permute-start.15) | collective-permute-done | bytes 163872 | tf_op jit(solution)/shard_map/ppermute | solution.py:32
  62.6 0.1 broadcast_select_fusion
  62.7 1.5 %collective-permute-start.18 = (bf16[1,80,1024]{2,1,0:T(8,128)(2,1)S(1)}, bf16[1,80,1024]{2,1,0:T(8,128)(2,1)S(1)}, u32[]{:S(2)}, u32[]{:S(2)}) collective-permute-start(bf16[1,80,1024]{2,1,0:T(8,128)(2,1)S(1)} %get-tuple-element.105), channel_id=1, source_target_pairs={{0,24},{8,0},{16,8},{24,16},{1,25},{9,1},{17,9},{25,17},{2,26},{10... | collective-permute-start | bytes 491528 | tf_op jit(solution)/shard_map/ppermute | solution.py:32
  64.3 2.6 %collective-permute-start.26 = (bf16[1,80,1024]{2,1,0:T(8,128)(2,1)S(1)}, bf16[1,80,1024]{2,1,0:T(8,128)(2,1)S(1)}, u32[]{:S(2)}, u32[]{:S(2)}) collective-permute-start(bf16[1,80,1024]{2,1,0:T(8,128)(2,1)S(1)} %get-tuple-element.104), channel_id=1, source_target_pairs={{0,3},{1,0},{2,1},{3,2},{4,7},{5,4},{6,5},{7,6},{8,11},{9,8},{10,9... | collective-permute-start | bytes 491528 | tf_op jit(solution)/shard_map/ppermute | solution.py:32
  66.8 0.1 collective-permute-done.18
  67.0 2.6 %collective-permute-start.20 = (bf16[1,80,512]{2,1,0:T(8,128)(2,1)S(1)}, bf16[1,80,512]{2,1,0:T(8,128)(2,1)S(1)}, u32[]{:S(2)}, u32[]{:S(2)}) collective-permute-start(bf16[1,80,512]{2,1,0:T(8,128)(2,1)S(1)} %slice.193), channel_id=1, source_target_pairs={{0,24},{8,0},{16,8},{24,16},{1,25},{9,1},{17,9},{25,17},{2,26},{10... | collective-permute-start | bytes 245768 | tf_op jit(solution)/shard_map/ppermute | solution.py:32
  69.7 2.5 %collective-permute-start.28 = (bf16[1,80,512]{2,1,0:T(8,128)(2,1)S(1)}, bf16[1,80,512]{2,1,0:T(8,128)(2,1)S(1)}, u32[]{:S(2)}, u32[]{:S(2)}) collective-permute-start(bf16[1,80,512]{2,1,0:T(8,128)(2,1)S(1)} %slice.197), channel_id=1, source_target_pairs={{0,3},{1,0},{2,1},{3,2},{4,7},{5,4},{6,5},{7,6},{8,11},{9,8},{10,9... | collective-permute-start | bytes 245768 | tf_op jit(solution)/shard_map/ppermute | solution.py:32
  72.2 0.3 collective-permute-done.25
  72.5 0.2 collective-permute-start.27
  72.7 1.5 %collective-permute-done.19 = bf16[1,80,512]{2,1,0:T(8,128)(2,1)S(1)} collective-permute-done((bf16[1,80,512]{2,1,0:T(8,128)(2,1)S(1)}, bf16[1,80,512]{2,1,0:T(8,128)(2,1)S(1)}, u32[]{:S(2)}, u32[]{:S(2)}) %collective-permute-start.19) | collective-permute-done | bytes 81952 | tf_op jit(solution)/shard_map/ppermute | solution.py:32
  74.3 1.9 %collective-permute-start.23 = (bf16[4,80,1024]{2,1,0:T(8,128)(2,1)S(1)}, bf16[4,80,1024]{2,1,0:T(8,128)(2,1)S(1)}, u32[]{:S(2)}, u32[]{:S(2)}) collective-permute-start(bf16[4,80,1024]{2,1,0:T(8,128)(2,1)S(1)} %maximum_maximum_fusion.a0), channel_id=1, source_target_pairs={{0,3},{1,0},{2,1},{3,2},{4,7},{5,4},{6,5},{7,6},{8,11},{9,8},{10,9... | collective-permute-start | bytes 1966088 | tf_op jit(solution)/shard_map/ppermute | solution.py:32
  76.2 1.0 collective-permute-done.27
  77.3 2.0 %collective-permute-start.31 = (bf16[4,80,1024]{2,1,0:T(8,128)(2,1)S(1)}, bf16[4,80,1024]{2,1,0:T(8,128)(2,1)S(1)}, u32[]{:S(2)}, u32[]{:S(2)}) collective-permute-start(bf16[4,80,1024]{2,1,0:T(8,128)(2,1)S(1)} %maximum_maximum_fusion.1.b0), channel_id=1, source_target_pairs={{0,24},{8,0},{16,8},{24,16},{1,25},{9,1},{17,9},{25,17},{2,26},{10... | collective-permute-start | bytes 1966088 | tf_op jit(solution)/shard_map/ppermute | solution.py:32
  79.3 7.7 %collective-permute-done.23.a2 = bf16[4,80,1024]{2,1,0:T(8,128)(2,1)S(1)} collective-permute-done((bf16[4,80,1024]{2,1,0:T(8,128)(2,1)S(1)}, bf16[4,80,1024]{2,1,0:T(8,128)(2,1)S(1)}, u32[]{:S(2)}, u32[]{:S(2)}) %collective-permute-start.23) | collective-permute-done | bytes 655392 | tf_op jit(solution)/shard_map/ppermute | solution.py:32
  87.0 3.4 %collective-permute-start.24 = (bf16[2,80,1024]{2,1,0:T(8,128)(2,1)S(1)}, bf16[2,80,1024]{2,1,0:T(8,128)(2,1)S(1)}, u32[]{:S(2)}, u32[]{:S(2)}) collective-permute-start(bf16[2,80,1024]{2,1,0:T(8,128)(2,1)S(1)} %slice.195), channel_id=1, source_target_pairs={{0,3},{1,0},{2,1},{3,2},{4,7},{5,4},{6,5},{7,6},{8,11},{9,8},{10,9... | collective-permute-start | bytes 983048 | tf_op jit(solution)/shard_map/ppermute | solution.py:32
  90.6 1.7 %collective-permute-start.32 = (bf16[2,80,1024]{2,1,0:T(8,128)(2,1)S(1)}, bf16[2,80,1024]{2,1,0:T(8,128)(2,1)S(1)}, u32[]{:S(2)}, u32[]{:S(2)}) collective-permute-start(bf16[2,80,1024]{2,1,0:T(8,128)(2,1)S(1)} %slice.199), channel_id=1, source_target_pairs={{0,24},{8,0},{16,8},{24,16},{1,25},{9,1},{17,9},{25,17},{2,26},{10... | collective-permute-start | bytes 983048 | tf_op jit(solution)/shard_map/ppermute | solution.py:32
  92.4 3.6 %gram_first.1 = (f32[1024,1024]{1,0:T(8,128)S(1)}, bf16[2,4,4,80,1024]{4,3,2,1,0:T(8,128)(2,1)S(1)}) custom-call(s32[4]{0:T(128)S(1)} %pad_add_fusion.at_ref, bf16[4,80,1024]{2,1,0:T(8,128)(2,1)S(1)} %maximum_maximum_fusion.a0, bf16[4,80,1024]{2,1,0:T(8,128)(2,1)S(1)} %collective-permute-done.21.a1, bf16[4,80,1024]{2,1,0:T(8,128)(2,1)S(1)} %collective-permute-done.23.a2, ...), custom_call_target="tpu_custom_call" | custom-call | flops 2684354560 | bytes 2621440 | tf_op jit(solution)/shard_map/gram_first/pallas_call | solution.py:157
  96.1 2.4 %collective-permute-done.22.a3 = bf16[2,80,1024]{2,1,0:T(8,128)(2,1)S(1)} collective-permute-done((bf16[2,80,1024]{2,1,0:T(8,128)(2,1)S(1)}, bf16[2,80,1024]{2,1,0:T(8,128)(2,1)S(1)}, u32[]{:S(2)}, u32[]{:S(2)}) %collective-permute-start.22) | collective-permute-done | bytes 327712 | tf_op jit(solution)/shard_map/ppermute | solution.py:32
  98.4 2.5 %collective-permute-done.30.b3 = bf16[2,80,1024]{2,1,0:T(8,128)(2,1)S(1)} collective-permute-done((bf16[2,80,1024]{2,1,0:T(8,128)(2,1)S(1)}, bf16[2,80,1024]{2,1,0:T(8,128)(2,1)S(1)}, u32[]{:S(2)}, u32[]{:S(2)}) %collective-permute-start.30) | collective-permute-done | bytes 327712 | tf_op jit(solution)/shard_map/ppermute | solution.py:32
  100.9 2.2 %gram_last.1 = (bf16[1024,1024]{1,0:T(8,128)(2,1)S(1)}, bf16[2,4,4,80,1024]{4,3,2,1,0:T(8,128)(2,1)S(1)}) custom-call(s32[4]{0:T(128)S(1)} %pad_add_fusion.at_ref, bf16[2,80,1024]{2,1,0:T(8,128)(2,1)S(1)} %collective-permute-done.22.a3, bf16[2,80,1024]{2,1,0:T(8,128)(2,1)S(1)} %collective-permute-done.24.a4, ...), custom_call_target="tpu_custom_call" | custom-call | tf_op jit(solution)/shard_map/gram_last/pallas_call | solution.py:187
  103.1 6.5 %collective-permute-start.34 = (bf16[1024,1024]{1,0:T(8,128)(2,1)S(1)}, bf16[1024,1024]{1,0:T(8,128)(2,1)S(1)}, u32[]{:S(2)}, u32[]{:S(2)}) collective-permute-start(bf16[1024,1024]{1,0:T(8,128)(2,1)S(1)} %get-tuple-element.91.own_ref), channel_id=1, source_target_pairs={{0,32},{32,0},{1,33},{33,1},{2,34},{34,2},{3,35},{35,3},{4,36},{36... | collective-permute-start | bytes 6291464 | tf_op jit(solution)/shard_map/ppermute | solution.py:32
  109.6 2.8 %coeff.2 = bf16[400,1024]{1,0:T(8,128)(2,1)S(1)} custom-call(s32[4]{0:T(128)S(1)} %pad_add_fusion.at_ref, bf16[2,1280,1024]{2,1,0:T(8,128)(2,1)S(1)} %bitcast.49, bf16[800,1280]{1,0:T(8,128)(2,1)S(1)} %get-tuple-element.83.pool0_ref, bf16[800,1280]{1,0:T(8,128)(2,1)S(1)} %get-tuple-element.84.pool1_ref), custom_call_target="tpu_custom_call" | custom-call | flops 2097152000 | bytes 4096000 | tf_op jit(solution)/shard_map/coeff/pallas_call | solution.py:216
  112.4 0.1 collective-permute-start.33
  112.6 2.9 %coeff.3 = bf16[400,1024]{1,0:T(8,128)(2,1)S(1)} custom-call(s32[4]{0:T(128)S(1)} %pad_add_fusion.at_ref, bf16[2,1280,1024]{2,1,0:T(8,128)(2,1)S(1)} %bitcast.50, bf16[800,1280]{1,0:T(8,128)(2,1)S(1)} %get-tuple-element.83.pool0_ref, bf16[800,1280]{1,0:T(8,128)(2,1)S(1)} %get-tuple-element.84.pool1_ref), custom_call_target="tpu_custom_call" | custom-call | flops 2097152000 | bytes 4096000 | tf_op jit(solution)/shard_map/coeff/pallas_call | solution.py:216
  115.4 0.3 add_convert_fusion.2.chip_ref
  115.8 1.1 collective-permute-start.35
  116.9 20.3 %schulz.1 = (bf16[1024,1024]{1,0:T(8,128)(2,1)S(1)}, f32[8,128]{1,0:T(8,128)S(1)}) custom-call(bf16[1024,1024]{1,0:T(8,128)(2,1)S(1)} %get-tuple-element.91.own_ref, bf16[1024,1024]{1,0:T(8,128)(2,1)S(1)} %collective-permute-done.34.other_ref), custom_call_target="tpu_custom_call" | custom-call | flops 25769803776 | bytes 8388608 | tf_op jit(solution)/shard_map/schulz/pallas_call | solution.py:276
  137.2 1.9 %third.1.third_ref = bf16[400,1024]{1,0:T(8,128)(2,1)S(1)} custom-call(bf16[400,1024]{1,0:T(8,128)(2,1)S(1)} %add_convert_fusion.2.chip_ref, bf16[400,1024]{1,0:T(8,128)(2,1)S(1)} %collective-permute-done.35.over_ref, bf16[1024,1024]{1,0:T(8,128)(2,1)S(1)} %get-tuple-element.95.z_ref, f32[8,128]{1,0:T(8,128)S(1)} %get-tuple-element.96.frob_ref), custom_call_target="tpu_custom_call" | custom-call | tf_op jit(solution)/shard_map/third/pallas_call | solution.py:301
  139.1 1.1 collective-permute-start.36
  140.2 1.9 %merge_own.1 = (bf16[400,1280]{1,0:T(8,128)(2,1)S(1)}, bf16[1024,1280]{1,0:T(8,128)(2,1)S(1)}) custom-call(s32[4]{0:T(128)S(1)} %pad_add_fusion.at_ref, bf16[400,1024]{1,0:T(8,128)(2,1)S(1)} %third.1.third_ref, bf16[2,1280,1024]{2,1,0:T(8,128)(2,1)S(1)} %bitcast.51), custom_call_target="tpu_custom_call" | custom-call | flops 1048576000 | bytes 2621440 | tf_op jit(solution)/shard_map/merge_own/pallas_call | solution.py:323
  142.1 0.1 collective-permute-done.36.third_ref
  142.2 2.6 %merge.1 = bf16[800,1280]{1,0:T(8,128)(2,1)} custom-call(s32[4]{0:T(128)S(1)} %pad_add_fusion.at_ref, bf16[400,1024]{1,0:T(8,128)(2,1)S(1)} %collective-permute-done.36.third_ref, bf16[1024,1280]{1,0:T(8,128)(2,1)S(1)} %get-tuple-element.97.turned_ref, bf16[400,1280]{1,0:T(8,128)(2,1)S(1)} %get-tuple-element.98.own_ref), custom_call_target="tpu_custom_call" | custom-call | tf_op jit(solution)/shard_map/merge/pallas_call | solution.py:356
  (53 shorter events, 1.2 us)
Async XLA Ops:
  0.1 0.9 copy-start
  11.2 44.1 %collective-permute-start.16 = (bf16[2,800,1280]{2,1,0:T(8,128)(2,1)}, bf16[2,800,1280]{2,1,0:T(8,128)(2,1)S(1)}, u32[]{:S(2)}, u32[]{:S(2)}) collective-permute-start(bf16[2,800,1280]{2,1,0:T(8,128)(2,1)} %get-tuple-element.67), channel_id=1, source_target_pairs={{0,32},{32,0},{1,33},{33,1},{2,34},{34,2},{3,35},{35,3},{4,36},{36... | collective-permute-start | bytes 12288008 | tf_op jit(solution)/shard_map/ppermute | solution.py:32
  12.8 7.4 %collective-permute-start.8 = (bf16[2,4,80,128]{3,2,1,0:T(8,128)(2,1)S(1)}, bf16[2,4,80,128]{3,2,1,0:T(8,128)(2,1)S(1)}, u32[]{:S(2)}, u32[]{:S(2)}) collective-permute-start(bf16[2,4,80,128]{3,2,1,0:T(8,128)(2,1)S(1)} %get-tuple-element.64), channel_id=1, source_target_pairs={{0,3},{1,0},{2,1},{3,2},{4,7},{5,4},{6,5},{7,6},{8,11},{9,8},{10,9... | collective-permute-start | bytes 491528 | tf_op jit(solution)/shard_map/ppermute | solution.py:32
  16.6 10.3 %collective-permute-start = (bf16[2,4,80,128]{3,2,1,0:T(8,128)(2,1)S(1)}, bf16[2,4,80,128]{3,2,1,0:T(8,128)(2,1)S(1)}, u32[]{:S(2)}, u32[]{:S(2)}) collective-permute-start(bf16[2,4,80,128]{3,2,1,0:T(8,128)(2,1)S(1)} %get-tuple-element.57), channel_id=1, source_target_pairs={{0,8},{8,16},{16,24},{24,0},{1,9},{9,17},{17,25},{25,1},{2,10},{10... | collective-permute-start | bytes 491528 | tf_op jit(solution)/shard_map/ppermute | solution.py:32
  17.9 7.6 %collective-permute-start.2 = (bf16[2,4,80,128]{3,2,1,0:T(8,128)(2,1)S(1)}, bf16[2,4,80,128]{3,2,1,0:T(8,128)(2,1)S(1)}, u32[]{:S(2)}, u32[]{:S(2)}) collective-permute-start(bf16[2,4,80,128]{3,2,1,0:T(8,128)(2,1)S(1)} %get-tuple-element.59), channel_id=1, source_target_pairs={{0,24},{8,0},{16,8},{24,16},{1,25},{9,1},{17,9},{25,17},{2,26},{10... | collective-permute-start | bytes 491528 | tf_op jit(solution)/shard_map/ppermute | solution.py:32
  19.3 6.0 %collective-permute-start.6 = (bf16[2,4,80,128]{3,2,1,0:T(8,128)(2,1)S(1)}, bf16[2,4,80,128]{3,2,1,0:T(8,128)(2,1)S(1)}, u32[]{:S(2)}, u32[]{:S(2)}) collective-permute-start(bf16[2,4,80,128]{3,2,1,0:T(8,128)(2,1)S(1)} %get-tuple-element.62), channel_id=1, source_target_pairs={{0,1},{1,2},{2,3},{3,0},{4,5},{5,6},{6,7},{7,4},{8,9},{9,10},{10,1... | collective-permute-start | bytes 491528 | tf_op jit(solution)/shard_map/ppermute | solution.py:32
  20.3 9.6 %collective-permute-start.9 = (bf16[4,4,80,128]{3,2,1,0:T(8,128)(2,1)S(1)}, bf16[4,4,80,128]{3,2,1,0:T(8,128)(2,1)S(1)}, u32[]{:S(2)}, u32[]{:S(2)}) collective-permute-start(bf16[4,4,80,128]{3,2,1,0:T(8,128)(2,1)S(1)} %fusion.5), channel_id=1, source_target_pairs={{0,3},{1,0},{2,1},{3,2},{4,7},{5,4},{6,5},{7,6},{8,11},{9,8},{10,9... | collective-permute-start | bytes 983048 | tf_op jit(solution)/shard_map/ppermute | solution.py:32
  25.4 8.7 %collective-permute-start.7 = (bf16[4,4,80,128]{3,2,1,0:T(8,128)(2,1)S(1)}, bf16[4,4,80,128]{3,2,1,0:T(8,128)(2,1)S(1)}, u32[]{:S(2)}, u32[]{:S(2)}) collective-permute-start(bf16[4,4,80,128]{3,2,1,0:T(8,128)(2,1)S(1)} %fusion.4), channel_id=1, source_target_pairs={{0,1},{1,2},{2,3},{3,0},{4,5},{5,6},{6,7},{7,4},{8,9},{9,10},{10,1... | collective-permute-start | bytes 983048 | tf_op jit(solution)/shard_map/ppermute | solution.py:32
  25.6 8.7 %collective-permute-start.3 = (bf16[4,4,80,128]{3,2,1,0:T(8,128)(2,1)S(1)}, bf16[4,4,80,128]{3,2,1,0:T(8,128)(2,1)S(1)}, u32[]{:S(2)}, u32[]{:S(2)}) collective-permute-start(bf16[4,4,80,128]{3,2,1,0:T(8,128)(2,1)S(1)} %fusion.3), channel_id=1, source_target_pairs={{0,24},{8,0},{16,8},{24,16},{1,25},{9,1},{17,9},{25,17},{2,26},{10... | collective-permute-start | bytes 983048 | tf_op jit(solution)/shard_map/ppermute | solution.py:32
  27.0 8.4 %collective-permute-start.1 = (bf16[4,4,80,128]{3,2,1,0:T(8,128)(2,1)S(1)}, bf16[4,4,80,128]{3,2,1,0:T(8,128)(2,1)S(1)}, u32[]{:S(2)}, u32[]{:S(2)}) collective-permute-start(bf16[4,4,80,128]{3,2,1,0:T(8,128)(2,1)S(1)} %fusion.2), channel_id=1, source_target_pairs={{0,8},{8,16},{16,24},{24,0},{1,9},{9,17},{17,25},{25,1},{2,10},{10... | collective-permute-start | bytes 983048 | tf_op jit(solution)/shard_map/ppermute | solution.py:32
  34.1 21.3 %copy-start.1 = (bf16[2,800,1280]{2,1,0:T(8,128)(2,1)S(1)}, bf16[2,800,1280]{2,1,0:T(8,128)(2,1)}, u32[]{:S(2)}) copy-start(bf16[2,800,1280]{2,1,0:T(8,128)(2,1)} %get-tuple-element.66) | copy-start | bytes 12288004
  34.1 4.2 %collective-permute-start.10 = (bf16[2,4,80,128]{3,2,1,0:T(8,128)(2,1)S(1)}, bf16[2,4,80,128]{3,2,1,0:T(8,128)(2,1)S(1)}, u32[]{:S(2)}, u32[]{:S(2)}) collective-permute-start(bf16[2,4,80,128]{3,2,1,0:T(8,128)(2,1)S(1)} %add_convert_fusion.5), channel_id=1, source_target_pairs={{0,8},{8,0},{16,24},{24,16},{1,9},{9,1},{17,25},{25,17},{2,10},{10... | collective-permute-start | bytes 491528 | tf_op jit(solution)/shard_map/ppermute | solution.py:388
  35.5 4.3 %collective-permute-start.4 = (bf16[2,4,80,128]{3,2,1,0:T(8,128)(2,1)S(1)}, bf16[2,4,80,128]{3,2,1,0:T(8,128)(2,1)S(1)}, u32[]{:S(2)}, u32[]{:S(2)}) collective-permute-start(bf16[2,4,80,128]{3,2,1,0:T(8,128)(2,1)S(1)} %add_convert_fusion.8), channel_id=1, source_target_pairs={{0,1},{1,0},{2,3},{3,2},{4,5},{5,4},{6,7},{7,6},{8,9},{9,8},{10,11... | collective-permute-start | bytes 491528 | tf_op jit(solution)/shard_map/ppermute | solution.py:388
  38.4 4.6 %collective-permute-start.11 = (bf16[4,80,128]{2,1,0:T(8,128)(2,1)S(1)}, bf16[4,80,128]{2,1,0:T(8,128)(2,1)S(1)}, u32[]{:S(2)}, u32[]{:S(2)}) collective-permute-start(bf16[4,80,128]{2,1,0:T(8,128)(2,1)S(1)} %fusion.12), channel_id=1, source_target_pairs={{0,24},{24,0},{8,16},{16,8},{1,25},{25,1},{9,17},{17,9},{2,26},{26... | collective-permute-start | bytes 245768 | tf_op jit(solution)/shard_map/ppermute | solution.py:390
  39.8 4.6 %collective-permute-start.5 = (bf16[4,80,128]{2,1,0:T(8,128)(2,1)S(1)}, bf16[4,80,128]{2,1,0:T(8,128)(2,1)S(1)}, u32[]{:S(2)}, u32[]{:S(2)}) collective-permute-start(bf16[4,80,128]{2,1,0:T(8,128)(2,1)S(1)} %fusion.10), channel_id=1, source_target_pairs={{0,3},{3,0},{1,2},{2,1},{4,7},{7,4},{5,6},{6,5},{8,11},{11,8},{9,1... | collective-permute-start | bytes 245768 | tf_op jit(solution)/shard_map/ppermute | solution.py:390
  44.5 6.3 %collective-permute-start.12 = (bf16[2,80,256]{2,1,0:T(8,128)(2,1)S(1)}, bf16[2,80,256]{2,1,0:T(8,128)(2,1)S(1)}, u32[]{:S(2)}, u32[]{:S(2)}) collective-permute-start(bf16[2,80,256]{2,1,0:T(8,128)(2,1)S(1)} %select_bitcast_fusion), channel_id=1, source_target_pairs={{0,32},{32,0},{1,33},{33,1},{2,34},{34,2},{3,35},{35,3},{4,36},{36... | collective-permute-start | bytes 245768 | tf_op jit(solution)/shard_map/ppermute | solution.py:32
  50.9 6.0 %collective-permute-start.14 = (bf16[2,80,512]{2,1,0:T(8,128)(2,1)S(1)}, bf16[2,80,512]{2,1,0:T(8,128)(2,1)S(1)}, u32[]{:S(2)}, u32[]{:S(2)}) collective-permute-start(bf16[2,80,512]{2,1,0:T(8,128)(2,1)S(1)} %pad_maximum_fusion.2), channel_id=1, source_target_pairs={{0,68},{4,0},{64,4},{68,64},{1,69},{5,1},{65,5},{69,65},{2,70},{6,... | collective-permute-start | bytes 491528 | tf_op jit(solution)/shard_map/ppermute | solution.py:32
  53.7 7.3 %collective-permute-start.13 = (bf16[2,80,512]{2,1,0:T(8,128)(2,1)S(1)}, bf16[2,80,512]{2,1,0:T(8,128)(2,1)S(1)}, u32[]{:S(2)}, u32[]{:S(2)}) collective-permute-start(bf16[2,80,512]{2,1,0:T(8,128)(2,1)S(1)} %pad_maximum_fusion.2), channel_id=1, source_target_pairs={{0,4},{4,64},{64,68},{68,0},{1,5},{5,65},{65,69},{69,1},{2,6},{6,6... | collective-permute-start | bytes 491528 | tf_op jit(solution)/shard_map/ppermute | solution.py:32
  53.7 8.8 %collective-permute-start.15 = (bf16[2,80,512]{2,1,0:T(8,128)(2,1)S(1)}, bf16[2,80,512]{2,1,0:T(8,128)(2,1)S(1)}, u32[]{:S(2)}, u32[]{:S(2)}) collective-permute-start(bf16[2,80,512]{2,1,0:T(8,128)(2,1)S(1)} %pad_maximum_fusion.2), channel_id=1, source_target_pairs={{0,64},{4,68},{64,0},{68,4},{1,65},{5,69},{65,1},{69,5},{2,66},{6,... | collective-permute-start | bytes 491528 | tf_op jit(solution)/shard_map/ppermute | solution.py:32
  62.7 4.2 %collective-permute-start.18 = (bf16[1,80,1024]{2,1,0:T(8,128)(2,1)S(1)}, bf16[1,80,1024]{2,1,0:T(8,128)(2,1)S(1)}, u32[]{:S(2)}, u32[]{:S(2)}) collective-permute-start(bf16[1,80,1024]{2,1,0:T(8,128)(2,1)S(1)} %get-tuple-element.105), channel_id=1, source_target_pairs={{0,24},{8,0},{16,8},{24,16},{1,25},{9,1},{17,9},{25,17},{2,26},{10... | collective-permute-start | bytes 491528 | tf_op jit(solution)/shard_map/ppermute | solution.py:32
  64.2 5.4 %collective-permute-start.17 = (bf16[1,80,1024]{2,1,0:T(8,128)(2,1)S(1)}, bf16[1,80,1024]{2,1,0:T(8,128)(2,1)S(1)}, u32[]{:S(2)}, u32[]{:S(2)}) collective-permute-start(bf16[1,80,1024]{2,1,0:T(8,128)(2,1)S(1)} %get-tuple-element.105), channel_id=1, source_target_pairs={{0,8},{8,16},{16,24},{24,0},{1,9},{9,17},{17,25},{25,1},{2,10},{10... | collective-permute-start | bytes 491528 | tf_op jit(solution)/shard_map/ppermute | solution.py:32
  64.3 5.4 %collective-permute-start.26 = (bf16[1,80,1024]{2,1,0:T(8,128)(2,1)S(1)}, bf16[1,80,1024]{2,1,0:T(8,128)(2,1)S(1)}, u32[]{:S(2)}, u32[]{:S(2)}) collective-permute-start(bf16[1,80,1024]{2,1,0:T(8,128)(2,1)S(1)} %get-tuple-element.104), channel_id=1, source_target_pairs={{0,3},{1,0},{2,1},{3,2},{4,7},{5,4},{6,5},{7,6},{8,11},{9,8},{10,9... | collective-permute-start | bytes 491528 | tf_op jit(solution)/shard_map/ppermute | solution.py:32
  66.8 5.7 %collective-permute-start.25 = (bf16[1,80,1024]{2,1,0:T(8,128)(2,1)S(1)}, bf16[1,80,1024]{2,1,0:T(8,128)(2,1)S(1)}, u32[]{:S(2)}, u32[]{:S(2)}) collective-permute-start(bf16[1,80,1024]{2,1,0:T(8,128)(2,1)S(1)} %get-tuple-element.104), channel_id=1, source_target_pairs={{0,1},{1,2},{2,3},{3,0},{4,5},{5,6},{6,7},{7,4},{8,9},{9,10},{10,1... | collective-permute-start | bytes 491528 | tf_op jit(solution)/shard_map/ppermute | solution.py:32
  67.0 5.7 %collective-permute-start.20 = (bf16[1,80,512]{2,1,0:T(8,128)(2,1)S(1)}, bf16[1,80,512]{2,1,0:T(8,128)(2,1)S(1)}, u32[]{:S(2)}, u32[]{:S(2)}) collective-permute-start(bf16[1,80,512]{2,1,0:T(8,128)(2,1)S(1)} %slice.193), channel_id=1, source_target_pairs={{0,24},{8,0},{16,8},{24,16},{1,25},{9,1},{17,9},{25,17},{2,26},{10... | collective-permute-start | bytes 245768 | tf_op jit(solution)/shard_map/ppermute | solution.py:32
  69.6 4.6 %collective-permute-start.19 = (bf16[1,80,512]{2,1,0:T(8,128)(2,1)S(1)}, bf16[1,80,512]{2,1,0:T(8,128)(2,1)S(1)}, u32[]{:S(2)}, u32[]{:S(2)}) collective-permute-start(bf16[1,80,512]{2,1,0:T(8,128)(2,1)S(1)} %slice.192), channel_id=1, source_target_pairs={{0,8},{8,16},{16,24},{24,0},{1,9},{9,17},{17,25},{25,1},{2,10},{10... | collective-permute-start | bytes 245768 | tf_op jit(solution)/shard_map/ppermute | solution.py:32
  69.7 6.4 %collective-permute-start.28 = (bf16[1,80,512]{2,1,0:T(8,128)(2,1)S(1)}, bf16[1,80,512]{2,1,0:T(8,128)(2,1)S(1)}, u32[]{:S(2)}, u32[]{:S(2)}) collective-permute-start(bf16[1,80,512]{2,1,0:T(8,128)(2,1)S(1)} %slice.197), channel_id=1, source_target_pairs={{0,3},{1,0},{2,1},{3,2},{4,7},{5,4},{6,5},{7,6},{8,11},{9,8},{10,9... | collective-permute-start | bytes 245768 | tf_op jit(solution)/shard_map/ppermute | solution.py:32
  72.5 4.7 %collective-permute-start.27 = (bf16[1,80,512]{2,1,0:T(8,128)(2,1)S(1)}, bf16[1,80,512]{2,1,0:T(8,128)(2,1)S(1)}, u32[]{:S(2)}, u32[]{:S(2)}) collective-permute-start(bf16[1,80,512]{2,1,0:T(8,128)(2,1)S(1)} %slice.196), channel_id=1, source_target_pairs={{0,1},{1,2},{2,3},{3,0},{4,5},{5,6},{6,7},{7,4},{8,9},{9,10},{10,1... | collective-permute-start | bytes 245768 | tf_op jit(solution)/shard_map/ppermute | solution.py:32
  74.3 12.7 %collective-permute-start.23 = (bf16[4,80,1024]{2,1,0:T(8,128)(2,1)S(1)}, bf16[4,80,1024]{2,1,0:T(8,128)(2,1)S(1)}, u32[]{:S(2)}, u32[]{:S(2)}) collective-permute-start(bf16[4,80,1024]{2,1,0:T(8,128)(2,1)S(1)} %maximum_maximum_fusion.a0), channel_id=1, source_target_pairs={{0,3},{1,0},{2,1},{3,2},{4,7},{5,4},{6,5},{7,6},{8,11},{9,8},{10,9... | collective-permute-start | bytes 1966088 | tf_op jit(solution)/shard_map/ppermute | solution.py:32
  76.2 14.2 %collective-permute-start.21 = (bf16[4,80,1024]{2,1,0:T(8,128)(2,1)S(1)}, bf16[4,80,1024]{2,1,0:T(8,128)(2,1)S(1)}, u32[]{:S(2)}, u32[]{:S(2)}) collective-permute-start(bf16[4,80,1024]{2,1,0:T(8,128)(2,1)S(1)} %maximum_maximum_fusion.a0), channel_id=1, source_target_pairs={{0,1},{1,2},{2,3},{3,0},{4,5},{5,6},{6,7},{7,4},{8,9},{9,10},{10,1... | collective-permute-start | bytes 1966088 | tf_op jit(solution)/shard_map/ppermute | solution.py:32
  77.3 13.3 %collective-permute-start.31 = (bf16[4,80,1024]{2,1,0:T(8,128)(2,1)S(1)}, bf16[4,80,1024]{2,1,0:T(8,128)(2,1)S(1)}, u32[]{:S(2)}, u32[]{:S(2)}) collective-permute-start(bf16[4,80,1024]{2,1,0:T(8,128)(2,1)S(1)} %maximum_maximum_fusion.1.b0), channel_id=1, source_target_pairs={{0,24},{8,0},{16,8},{24,16},{1,25},{9,1},{17,9},{25,17},{2,26},{10... | collective-permute-start | bytes 1966088 | tf_op jit(solution)/shard_map/ppermute | solution.py:32
  79.3 13.0 %collective-permute-start.29 = (bf16[4,80,1024]{2,1,0:T(8,128)(2,1)S(1)}, bf16[4,80,1024]{2,1,0:T(8,128)(2,1)S(1)}, u32[]{:S(2)}, u32[]{:S(2)}) collective-permute-start(bf16[4,80,1024]{2,1,0:T(8,128)(2,1)S(1)} %maximum_maximum_fusion.1.b0), channel_id=1, source_target_pairs={{0,8},{8,16},{16,24},{24,0},{1,9},{9,17},{17,25},{25,1},{2,10},{10... | collective-permute-start | bytes 1966088 | tf_op jit(solution)/shard_map/ppermute | solution.py:32
  87.0 9.1 %collective-permute-start.24 = (bf16[2,80,1024]{2,1,0:T(8,128)(2,1)S(1)}, bf16[2,80,1024]{2,1,0:T(8,128)(2,1)S(1)}, u32[]{:S(2)}, u32[]{:S(2)}) collective-permute-start(bf16[2,80,1024]{2,1,0:T(8,128)(2,1)S(1)} %slice.195), channel_id=1, source_target_pairs={{0,3},{1,0},{2,1},{3,2},{4,7},{5,4},{6,5},{7,6},{8,11},{9,8},{10,9... | collective-permute-start | bytes 983048 | tf_op jit(solution)/shard_map/ppermute | solution.py:32
  90.4 8.0 %collective-permute-start.22 = (bf16[2,80,1024]{2,1,0:T(8,128)(2,1)S(1)}, bf16[2,80,1024]{2,1,0:T(8,128)(2,1)S(1)}, u32[]{:S(2)}, u32[]{:S(2)}) collective-permute-start(bf16[2,80,1024]{2,1,0:T(8,128)(2,1)S(1)} %slice.194), channel_id=1, source_target_pairs={{0,1},{1,2},{2,3},{3,0},{4,5},{5,6},{6,7},{7,4},{8,9},{9,10},{10,1... | collective-permute-start | bytes 983048 | tf_op jit(solution)/shard_map/ppermute | solution.py:32
  90.6 7.9 %collective-permute-start.32 = (bf16[2,80,1024]{2,1,0:T(8,128)(2,1)S(1)}, bf16[2,80,1024]{2,1,0:T(8,128)(2,1)S(1)}, u32[]{:S(2)}, u32[]{:S(2)}) collective-permute-start(bf16[2,80,1024]{2,1,0:T(8,128)(2,1)S(1)} %slice.199), channel_id=1, source_target_pairs={{0,24},{8,0},{16,8},{24,16},{1,25},{9,1},{17,9},{25,17},{2,26},{10... | collective-permute-start | bytes 983048 | tf_op jit(solution)/shard_map/ppermute | solution.py:32
  92.3 8.6 %collective-permute-start.30 = (bf16[2,80,1024]{2,1,0:T(8,128)(2,1)S(1)}, bf16[2,80,1024]{2,1,0:T(8,128)(2,1)S(1)}, u32[]{:S(2)}, u32[]{:S(2)}) collective-permute-start(bf16[2,80,1024]{2,1,0:T(8,128)(2,1)S(1)} %slice.198), channel_id=1, source_target_pairs={{0,8},{8,16},{16,24},{24,0},{1,9},{9,17},{17,25},{25,1},{2,10},{10... | collective-permute-start | bytes 983048 | tf_op jit(solution)/shard_map/ppermute | solution.py:32
  103.1 12.3 %collective-permute-start.34 = (bf16[1024,1024]{1,0:T(8,128)(2,1)S(1)}, bf16[1024,1024]{1,0:T(8,128)(2,1)S(1)}, u32[]{:S(2)}, u32[]{:S(2)}) collective-permute-start(bf16[1024,1024]{1,0:T(8,128)(2,1)S(1)} %get-tuple-element.91.own_ref), channel_id=1, source_target_pairs={{0,32},{32,0},{1,33},{33,1},{2,34},{34,2},{3,35},{35,3},{4,36},{36... | collective-permute-start | bytes 6291464 | tf_op jit(solution)/shard_map/ppermute | solution.py:32
  112.4 3.0 %collective-permute-start.33 = (bf16[400,1024]{1,0:T(8,128)(2,1)S(1)}, bf16[400,1024]{1,0:T(8,128)(2,1)S(1)}, u32[]{:S(2)}, u32[]{:S(2)}) collective-permute-start(bf16[400,1024]{1,0:T(8,128)(2,1)S(1)} %coeff.2), channel_id=1, source_target_pairs={{0,32},{32,0},{1,33},{33,1},{2,34},{34,2},{3,35},{35,3},{4,36},{36... | collective-permute-start | bytes 2457608 | tf_op jit(solution)/shard_map/ppermute | solution.py:32
  115.8 21.5 %collective-permute-start.35 = (bf16[400,1024]{1,0:T(8,128)(2,1)S(1)}, bf16[400,1024]{1,0:T(8,128)(2,1)S(1)}, u32[]{:S(2)}, u32[]{:S(2)}) collective-permute-start(bf16[400,1024]{1,0:T(8,128)(2,1)S(1)} %add_convert_fusion.2.chip_ref), channel_id=1, source_target_pairs={{0,64},{64,0},{1,65},{65,1},{2,66},{66,2},{3,67},{67,3},{4,68},{68... | collective-permute-start | bytes 2457608 | tf_op jit(solution)/shard_map/ppermute | solution.py:32
  139.1 3.0 %collective-permute-start.36 = (bf16[400,1024]{1,0:T(8,128)(2,1)S(1)}, bf16[400,1024]{1,0:T(8,128)(2,1)S(1)}, u32[]{:S(2)}, u32[]{:S(2)}) collective-permute-start(bf16[400,1024]{1,0:T(8,128)(2,1)S(1)} %third.1.third_ref), channel_id=1, source_target_pairs={{0,32},{32,0},{1,33},{33,1},{2,34},{34,2},{3,35},{35,3},{4,36},{36... | collective-permute-start | bytes 2457608 | tf_op jit(solution)/shard_map/ppermute | solution.py:32

commit v3 on v2

--- a/solution.py
+++ b/solution.py
@@ -139,17 +139,17 @@
         for j in range(ref.shape[0]):
             inner = (0, -1, 1, 2)[first + j]
             over_x, over_z = (inner, outer) if chunk == 0 else (outer, inner)
-            basis_ref[chunk, lax.rem(x + over_x + 4, 4), lax.rem(z + over_z + 4, 4)] = ref[j]
-
-
-def gram_first_kernel(at_ref, a0, a1, a2, b0, b1, b2, acc_ref, basis_ref, packed_ref):
+            basis_ref[lax.rem(x + over_x + 4, 4), lax.rem(z + over_z + 4, 4)] = ref[j]
+
+
+def gram_first_kernel(at_ref, a0, a1, a2, b0, b1, b2, acc_ref, near_a, near_b, packed_ref):
     pack_rows([a0, a1, a2, b0, b1, b2], packed_ref)
     for rows, columns in upper_blocks(acc_ref.shape[0], GRAM_BLOCK):
         acc_ref[rows, columns] = lax.dot_general(
             packed_ref[:, rows], packed_ref[:, columns], (((0,), (0,)), ((), ())), preferred_element_type=F32
         )
-    near = [(a0, 0, 0, 0), (a1, 0, -1, 0), (a2, 0, 1, 0), (b0, 1, 0, 0), (b1, 1, -1, 0), (b2, 1, 1, 0)]
-    place_rows(at_ref, near, basis_ref)
+    place_rows(at_ref, [(a0, 0, 0, 0), (a1, 0, -1, 0), (a2, 0, 1, 0)], near_a)
+    place_rows(at_ref, [(b0, 1, 0, 0), (b1, 1, -1, 0), (b2, 1, 1, 0)], near_b)
 
 
 def gram_first_call(at, parts):
@@ -157,10 +157,11 @@
     return pl.pallas_call(
         gram_first_kernel,
         in_specs=[pl.BlockSpec(memory_space=pltpu.SMEM)] + [whole()] * 6,
-        out_specs=[whole()] * 2,
+        out_specs=[whole()] * 3,
         out_shape=[
             jax.ShapeDtypeStruct((width, width), F32),
-            jax.ShapeDtypeStruct((2, 4, 4, rows, width), BF),
+            jax.ShapeDtypeStruct((4, 4, rows, width), BF),
+            jax.ShapeDtypeStruct((4, 4, rows, width), BF),
         ],
         scratch_shapes=[pltpu.VMEM((6 * count * rows, width), BF)],
         cost_estimate=pl.CostEstimate(
@@ -171,51 +172,57 @@
     )(at, *parts)
 
 
-def gram_last_kernel(at_ref, a3, a4, b3, b4, acc_ref, near_ref, gram_ref, basis_ref, packed_ref):
-    pack_rows([a3, a4, b3, b4], packed_ref)
+def gram_more_kernel(at_ref, low, high, acc_ref, near_ref, out_ref, basis_ref, packed_ref, *, chunk):
+    pack_rows([low, high], packed_ref)
     for rows, columns in upper_blocks(acc_ref.shape[0], GRAM_BLOCK):
-        value = lax.dot_general(
+        value = acc_ref[rows, columns] + lax.dot_general(
             packed_ref[:, rows], packed_ref[:, columns], (((0,), (0,)), ((), ())), preferred_element_type=F32
         )
-        mirror(gram_ref, rows, (acc_ref[rows, columns] + value).astype(BF), GRAM_BLOCK)
+        if chunk == 0:
+            out_ref[rows, columns] = value
+        else:
+            mirror(out_ref, rows, value.astype(BF), GRAM_BLOCK)
     basis_ref[...] = near_ref[...]
-    place_rows(at_ref, [(a3, 0, 2, 0), (a4, 0, 2, 2), (b3, 1, 2, 0), (b4, 1, 2, 2)], basis_ref)
-
-
-def gram_last_call(at, parts, acc, near):
+    place_rows(at_ref, [(low, chunk, 2, 0), (high, chunk, 2, 2)], basis_ref)
+
+
+def gram_more_call(at, parts, acc, near, chunk):
     count, rows, width = parts[0].shape
     return pl.pallas_call(
-        gram_last_kernel,
-        in_specs=[pl.BlockSpec(memory_space=pltpu.SMEM)] + [whole()] * 6,
+        functools.partial(gram_more_kernel, chunk=chunk),
+        in_specs=[pl.BlockSpec(memory_space=pltpu.SMEM)] + [whole()] * 4,
         out_specs=[whole()] * 2,
         out_shape=[
-            jax.ShapeDtypeStruct((width, width), BF),
+            jax.ShapeDtypeStruct((width, width), BF if chunk else F32),
             jax.ShapeDtypeStruct(near.shape, BF),
         ],
-        scratch_shapes=[pltpu.VMEM((4 * count * rows, width), BF)],
+        scratch_shapes=[pltpu.VMEM((2 * count * rows, width), BF)],
+        cost_estimate=pl.CostEstimate(
+            flops=3 * count * rows * width * width, bytes_accessed=8 * width * width, transcendentals=0
+        ),
         compiler_params=params(24),
-        name="gram_last",
+        name="gram_more",
     )(at, *parts, acc, near)
 
 
-def coeff_kernel(at_ref, basis_ref, pool0_ref, pool1_ref, out_ref, *, own):
+def coeff_kernel(at_ref, basis0_ref, basis1_ref, pool0_ref, pool1_ref, out_ref, *, own):
     half, width = out_ref.shape
     which = at_ref[3] if own else 1 - at_ref[3]
     block = 256
     rows = pl.ds(pl.multiple_of(which * half, 16), half)
     for i in range(0, width, block):
         columns = slice(i, i + block)
-        value = jnp.dot(pool0_ref[rows, :], basis_ref[0, :, columns], preferred_element_type=F32)
-        value = value + jnp.dot(pool1_ref[rows, :], basis_ref[1, :, columns], preferred_element_type=F32)
+        value = jnp.dot(pool0_ref[rows, :], basis0_ref[:, columns], preferred_element_type=F32)
+        value = value + jnp.dot(pool1_ref[rows, :], basis1_ref[:, columns], preferred_element_type=F32)
         out_ref[:, columns] = value.astype(BF)
 
 
 def coeff_call(at, basis, pooled, own):
-    _, depth, width = basis.shape
+    depth, width = basis[0].shape
     rows = pooled[0].shape[0]
     return pl.pallas_call(
         functools.partial(coeff_kernel, own=own),
-        in_specs=[pl.BlockSpec(memory_space=pltpu.SMEM)] + [whole()] * 3,
+        in_specs=[pl.BlockSpec(memory_space=pltpu.SMEM)] + [whole()] * 4,
         out_specs=whole(),
         out_shape=jax.ShapeDtypeStruct((rows // 2, width), BF),
         cost_estimate=pl.CostEstimate(
@@ -223,7 +230,7 @@
         ),
         compiler_params=params(20),
         name="coeff",
-    )(at, basis, *pooled)
+    )(at, *basis, *pooled)
 
 
 def diagonal(shape, first_row, first_col):
@@ -308,10 +315,11 @@
     )(chip_sum, over, z, frob)
 
 
-def merge_own_kernel(at_ref, third_ref, basis_ref, out_ref, turned_ref):
+def merge_own_kernel(at_ref, third_ref, basis0_ref, basis1_ref, out_ref, turned_ref):
     for i in range(0, out_ref.shape[1], MERGE_BLOCK):
         columns = slice(i, i + MERGE_BLOCK)
-        turned_ref[:, columns] = basis_ref[at_ref[2], columns, :].T
+        chunk = jnp.where(at_ref[2] == 0, basis0_ref[columns, :], basis1_ref[columns, :])
+        turned_ref[:, columns] = chunk.T
         out_ref[:, columns] = jnp.dot(
             third_ref[...], turned_ref[:, columns], preferred_element_type=F32
         ).astype(BF)
@@ -319,10 +327,10 @@
 
 def merge_own_call(at, third, basis):
     rows, width = third.shape
-    columns = basis.shape[1]
+    columns = basis[0].shape[0]
     return pl.pallas_call(
         merge_own_kernel,
-        in_specs=[pl.BlockSpec(memory_space=pltpu.SMEM), whole(), whole()],
+        in_specs=[pl.BlockSpec(memory_space=pltpu.SMEM), whole(), whole(), whole()],
         out_specs=[whole(), whole()],
         out_shape=[jax.ShapeDtypeStruct((rows, columns), BF), jax.ShapeDtypeStruct((width, columns), BF)],
         cost_estimate=pl.CostEstimate(
@@ -330,7 +338,7 @@
         ),
         compiler_params=params(),
         name="merge_own",
-    )(at, third, basis)
+    )(at, third, *basis)
 
 
 def merge_kernel(at_ref, third_ref, turned_ref, own_ref, out_any, twin_ref, sem):
@@ -443,11 +451,11 @@
     items = [(jnp.concatenate([*n, f]), axis) for n, f, axis in zip(near, far, ("z", "x"))]
     near, second = ring_gather(items)
     far = second(near)
-    acc, basis = gram_first_call(at, near[0] + near[1])
-    far, acc, basis = lax.optimization_barrier((far, acc, basis))
-    gram_own, basis = gram_last_call(at, far[0] + far[1], acc, basis)
+    acc, near_a, near_b = gram_first_call(at, near[0] + near[1])
+    acc, basis_a = gram_more_call(at, far[0], acc, near_a, 0)
+    gram_own, basis_b = gram_more_call(at, far[1], acc, near_b, 1)
     gram_other = shift(gram_own, "core", 1)
-    basis = basis.reshape(2, width // 4, basis.shape[-1])
+    basis = [part.reshape(width // 4, part.shape[-1]) for part in (basis_a, basis_b)]
     give = coeff_call(at, basis, pooled, False)
     give, pooled = lax.optimization_barrier((give, pooled))
     twin = shift(give, "core", 1)

time: 145 us -> 145 us (level)
  waiting for transfers between devices: 37.7 us -> 36 us
    ppermute x33, waiting for transfers between devices: 33 us -> 31.3 us  [shift(): lax.ppermute(value, axis, [(i, (i + step) % size) for i in range(size)])]
    pallas_call x1 -> x2, Pallas kernels: 2.19 us -> 3.22 us  [gram_more_call(): pl.pallas_call(functools.partial(gram_more_kernel, chunk=chunk), in_specs...]
  transfers between devices with their start and end apart: 37 -> 37, of which waited for: 20 -> 19; matrix products, arithmetic and copies ran while one was open for 1% -> 1% of each run, Pallas kernels for 22% -> 23%
where the time goes in v3:
time: 145 us
  starting transfers between devices  54.8 us (38%)
  Pallas kernels  49.6 us (34%)
  waiting for transfers between devices  36 us (25%)
  other arithmetic  2.52 us (2%)
    ppermute x33, starting transfers between devices, shift(): lax.ppermute(value, axis, [(i, (i + step) % size) for i in range(size)])  50.6 us
    ppermute x33, waiting for transfers between devices, shift(): lax.ppermute(value, axis, [(i, (i + step) % size) for i in range(size)])  31.3 us
    pallas_call x1, Pallas kernels, schulz_call(): pl.pallas_call(schulz_kernel, in_specs=[whole()] * 2, out_specs=[whole()]...  20.3 us
    pallas_call x1, Pallas kernels, sketch_call(): pl.pallas_call(sketch_kernel, in_specs=[pl.BlockSpec(memory_space=pltpu.S...  10.2 us
    pallas_call x2, Pallas kernels, coeff_call(): pl.pallas_call(functools.partial(coeff_kernel, own=own), in_specs=[pl.Blo...  5.66 us
    ppermute x2, starting transfers between devices, halving_reduce(): lax.ppermute(other, axis, [(0, 3), (3, 0), (1, 2), (2, 1)])  4.01 us
    pallas_call x1, Pallas kernels, gram_first_call(): pl.pallas_call(gram_first_kernel, in_specs=[pl.BlockSpec(memory_space=plt...  3.61 us
    pallas_call x2, Pallas kernels, gram_more_call(): pl.pallas_call(functools.partial(gram_more_kernel, chunk=chunk), in_specs...  3.22 us
  transfers between devices with their start and end apart: 37, of which 19 were waited for; matrix products, arithmetic and copies ran while one was open for 1% of the time, Pallas kernels for 23%

profile of v3, /device:TPU:1, one launch (start us, length us, event | category | flops | bytes accessed | tf_op | source)
XLA Modules:
  0.0 144.5 jit_solution(17336391338096262998)
XLA Ops:
  0.1 0.9 copy-done
  1.0 10.2 %sketch.1 = (bf16[4,4,80,128]{3,2,1,0:T(8,128)(2,1)S(1)}, bf16[4,4,80,128]{3,2,1,0:T(8,128)(2,1)S(1)}, bf16[4,4,80,128]{3,2,1,0:T(8,128)(2,1)S(1)}, bf16[2,4,80,...) custom-call(s32[4]{0:T(128)S(1)} %pad_add_fusion.at_ref, ...), custom_call_target="tpu_custom_call" | custom-call | tf_op jit(solution)/shard_map/sketch/pallas_call | solution.py:99
  11.2 1.6 %collective-permute-start.16 = (bf16[2,800,1280]{2,1,0:T(8,128)(2,1)}, bf16[2,800,1280]{2,1,0:T(8,128)(2,1)S(1)}, u32[]{:S(2)}, u32[]{:S(2)}) collective-permute-start(bf16[2,800,1280]{2,1,0:T(8,128)(2,1)} %get-tuple-element.64), channel_id=1, source_target_pairs={{0,32},{32,0},{1,33},{33,1},{2,34},{34,2},{3,35},{35,3},{4,36},{36... | collective-permute-start | bytes 12288008 | tf_op jit(solution)/shard_map/ppermute | solution.py:32
  12.8 3.9 %collective-permute-start.8 = (bf16[2,4,80,128]{3,2,1,0:T(8,128)(2,1)S(1)}, bf16[2,4,80,128]{3,2,1,0:T(8,128)(2,1)S(1)}, u32[]{:S(2)}, u32[]{:S(2)}) collective-permute-start(bf16[2,4,80,128]{3,2,1,0:T(8,128)(2,1)S(1)} %get-tuple-element.61), channel_id=1, source_target_pairs={{0,3},{1,0},{2,1},{3,2},{4,7},{5,4},{6,5},{7,6},{8,11},{9,8},{10,9... | collective-permute-start | bytes 491528 | tf_op jit(solution)/shard_map/ppermute | solution.py:32
  16.7 1.2 collective-permute-start
  17.9 1.5 %collective-permute-start.2 = (bf16[2,4,80,128]{3,2,1,0:T(8,128)(2,1)S(1)}, bf16[2,4,80,128]{3,2,1,0:T(8,128)(2,1)S(1)}, u32[]{:S(2)}, u32[]{:S(2)}) collective-permute-start(bf16[2,4,80,128]{3,2,1,0:T(8,128)(2,1)S(1)} %get-tuple-element.56), channel_id=1, source_target_pairs={{0,24},{8,0},{16,8},{24,16},{1,25},{9,1},{17,9},{25,17},{2,26},{10... | collective-permute-start | bytes 491528 | tf_op jit(solution)/shard_map/ppermute | solution.py:32
  19.3 0.9 collective-permute-done.8
  20.2 0.1 fusion.5
  20.3 3.5 %collective-permute-start.9 = (bf16[4,4,80,128]{3,2,1,0:T(8,128)(2,1)S(1)}, bf16[4,4,80,128]{3,2,1,0:T(8,128)(2,1)S(1)}, u32[]{:S(2)}, u32[]{:S(2)}) collective-permute-start(bf16[4,4,80,128]{3,2,1,0:T(8,128)(2,1)S(1)} %fusion.5), channel_id=1, source_target_pairs={{0,3},{1,0},{2,1},{3,2},{4,7},{5,4},{6,5},{7,6},{8,11},{9,8},{10,9... | collective-permute-start | bytes 983048 | tf_op jit(solution)/shard_map/ppermute | solution.py:32
  23.8 1.6 %collective-permute-done.6 = bf16[2,4,80,128]{3,2,1,0:T(8,128)(2,1)S(1)} collective-permute-done((bf16[2,4,80,128]{3,2,1,0:T(8,128)(2,1)S(1)}, bf16[2,4,80,128]{3,2,1,0:T(8,128)(2,1)S(1)}, u32[]{:S(2)}, u32[]{:S(2)}) %collective-permute-start.6) | collective-permute-done | bytes 163872 | tf_op jit(solution)/shard_map/ppermute | solution.py:32
  25.3 0.1 fusion.4
  25.5 0.1 fusion.3
  25.6 1.3 collective-permute-start.3
  26.9 0.1 fusion.2
  27.0 0.3 collective-permute-start.1
  27.3 2.6 %collective-permute-done.9 = bf16[4,4,80,128]{3,2,1,0:T(8,128)(2,1)S(1)} collective-permute-done((bf16[4,4,80,128]{3,2,1,0:T(8,128)(2,1)S(1)}, bf16[4,4,80,128]{3,2,1,0:T(8,128)(2,1)S(1)}, u32[]{:S(2)}, u32[]{:S(2)}) %collective-permute-start.9) | collective-permute-done | bytes 327712 | tf_op jit(solution)/shard_map/ppermute | solution.py:32
  29.9 4.2 %collective-permute-done.7 = bf16[4,4,80,128]{3,2,1,0:T(8,128)(2,1)S(1)} collective-permute-done((bf16[4,4,80,128]{3,2,1,0:T(8,128)(2,1)S(1)}, bf16[4,4,80,128]{3,2,1,0:T(8,128)(2,1)S(1)}, u32[]{:S(2)}, u32[]{:S(2)}) %collective-permute-start.7) | collective-permute-done | bytes 327712 | tf_op jit(solution)/shard_map/ppermute | solution.py:32
  34.2 0.1 collective-permute-start.10
  34.3 1.1 collective-permute-done.1
  35.5 0.1 collective-permute-start.4
  35.6 2.8 %collective-permute-done.10 = bf16[2,4,80,128]{3,2,1,0:T(8,128)(2,1)S(1)} collective-permute-done((bf16[2,4,80,128]{3,2,1,0:T(8,128)(2,1)S(1)}, bf16[2,4,80,128]{3,2,1,0:T(8,128)(2,1)S(1)}, u32[]{:S(2)}, u32[]{:S(2)}) %collective-permute-start.10) | collective-permute-done | bytes 163872 | tf_op jit(solution)/shard_map/ppermute | solution.py:396
  38.5 1.3 collective-permute-start.11
  39.9 2.7 %collective-permute-start.5 = (bf16[4,80,128]{2,1,0:T(8,128)(2,1)S(1)}, bf16[4,80,128]{2,1,0:T(8,128)(2,1)S(1)}, u32[]{:S(2)}, u32[]{:S(2)}) collective-permute-start(bf16[4,80,128]{2,1,0:T(8,128)(2,1)S(1)} %fusion.10), channel_id=1, source_target_pairs={{0,3},{3,0},{1,2},{2,1},{4,7},{7,4},{5,6},{6,5},{8,11},{11,8},{9,1... | collective-permute-start | bytes 245768 | tf_op jit(solution)/shard_map/ppermute | solution.py:398
  42.5 0.5 collective-permute-done.11
  43.1 1.3 collective-permute-done.5
  44.6 5.4 %collective-permute-start.12 = (bf16[2,80,256]{2,1,0:T(8,128)(2,1)S(1)}, bf16[2,80,256]{2,1,0:T(8,128)(2,1)S(1)}, u32[]{:S(2)}, u32[]{:S(2)}) collective-permute-start(bf16[2,80,256]{2,1,0:T(8,128)(2,1)S(1)} %select_bitcast_fusion), channel_id=1, source_target_pairs={{0,32},{32,0},{1,33},{33,1},{2,34},{34,2},{3,35},{35,3},{4,36},{36... | collective-permute-start | bytes 245768 | tf_op jit(solution)/shard_map/ppermute | solution.py:32
  50.0 0.9 collective-permute-done.12
  50.9 2.8 %collective-permute-start.14 = (bf16[2,80,512]{2,1,0:T(8,128)(2,1)S(1)}, bf16[2,80,512]{2,1,0:T(8,128)(2,1)S(1)}, u32[]{:S(2)}, u32[]{:S(2)}) collective-permute-start(bf16[2,80,512]{2,1,0:T(8,128)(2,1)S(1)} %pad_maximum_fusion.2), channel_id=1, source_target_pairs={{0,68},{4,0},{64,4},{68,64},{1,69},{5,1},{65,5},{69,65},{2,70},{6,... | collective-permute-start | bytes 491528 | tf_op jit(solution)/shard_map/ppermute | solution.py:32
  53.7 1.6 %collective-permute-start.15 = (bf16[2,80,512]{2,1,0:T(8,128)(2,1)S(1)}, bf16[2,80,512]{2,1,0:T(8,128)(2,1)S(1)}, u32[]{:S(2)}, u32[]{:S(2)}) collective-permute-start(bf16[2,80,512]{2,1,0:T(8,128)(2,1)S(1)} %pad_maximum_fusion.2), channel_id=1, source_target_pairs={{0,64},{4,68},{64,0},{68,4},{1,65},{5,69},{65,1},{69,5},{2,66},{6,... | collective-permute-start | bytes 491528 | tf_op jit(solution)/shard_map/ppermute | solution.py:32
  55.4 1.1 fusion.1
  56.5 0.4 collective-permute-done.14
  56.9 4.1 %collective-permute-done.13 = bf16[2,80,512]{2,1,0:T(8,128)(2,1)S(1)} collective-permute-done((bf16[2,80,512]{2,1,0:T(8,128)(2,1)S(1)}, bf16[2,80,512]{2,1,0:T(8,128)(2,1)S(1)}, u32[]{:S(2)}, u32[]{:S(2)}) %collective-permute-start.13) | collective-permute-done | bytes 163872 | tf_op jit(solution)/shard_map/ppermute | solution.py:32
  61.1 1.5 %collective-permute-done.15 = bf16[2,80,512]{2,1,0:T(8,128)(2,1)S(1)} collective-permute-done((bf16[2,80,512]{2,1,0:T(8,128)(2,1)S(1)}, bf16[2,80,512]{2,1,0:T(8,128)(2,1)S(1)}, u32[]{:S(2)}, u32[]{:S(2)}) %collective-permute-start.15) | collective-permute-done | bytes 163872 | tf_op jit(solution)/shard_map/ppermute | solution.py:32
  62.6 0.1 broadcast_select_fusion
  62.8 1.5 %collective-permute-start.18 = (bf16[1,80,1024]{2,1,0:T(8,128)(2,1)S(1)}, bf16[1,80,1024]{2,1,0:T(8,128)(2,1)S(1)}, u32[]{:S(2)}, u32[]{:S(2)}) collective-permute-start(bf16[1,80,1024]{2,1,0:T(8,128)(2,1)S(1)} %get-tuple-element.99), channel_id=1, source_target_pairs={{0,24},{8,0},{16,8},{24,16},{1,25},{9,1},{17,9},{25,17},{2,26},{10... | collective-permute-start | bytes 491528 | tf_op jit(solution)/shard_map/ppermute | solution.py:32
  64.3 2.6 %collective-permute-start.26 = (bf16[1,80,1024]{2,1,0:T(8,128)(2,1)S(1)}, bf16[1,80,1024]{2,1,0:T(8,128)(2,1)S(1)}, u32[]{:S(2)}, u32[]{:S(2)}) collective-permute-start(bf16[1,80,1024]{2,1,0:T(8,128)(2,1)S(1)} %get-tuple-element.98), channel_id=1, source_target_pairs={{0,3},{1,0},{2,1},{3,2},{4,7},{5,4},{6,5},{7,6},{8,11},{9,8},{10,9... | collective-permute-start | bytes 491528 | tf_op jit(solution)/shard_map/ppermute | solution.py:32
  66.9 0.1 collective-permute-done.18
  67.0 2.6 %collective-permute-start.20 = (bf16[1,80,512]{2,1,0:T(8,128)(2,1)S(1)}, bf16[1,80,512]{2,1,0:T(8,128)(2,1)S(1)}, u32[]{:S(2)}, u32[]{:S(2)}) collective-permute-start(bf16[1,80,512]{2,1,0:T(8,128)(2,1)S(1)} %slice.193), channel_id=1, source_target_pairs={{0,24},{8,0},{16,8},{24,16},{1,25},{9,1},{17,9},{25,17},{2,26},{10... | collective-permute-start | bytes 245768 | tf_op jit(solution)/shard_map/ppermute | solution.py:32
  69.7 2.5 %collective-permute-start.28 = (bf16[1,80,512]{2,1,0:T(8,128)(2,1)S(1)}, bf16[1,80,512]{2,1,0:T(8,128)(2,1)S(1)}, u32[]{:S(2)}, u32[]{:S(2)}) collective-permute-start(bf16[1,80,512]{2,1,0:T(8,128)(2,1)S(1)} %slice.197), channel_id=1, source_target_pairs={{0,3},{1,0},{2,1},{3,2},{4,7},{5,4},{6,5},{7,6},{8,11},{9,8},{10,9... | collective-permute-start | bytes 245768 | tf_op jit(solution)/shard_map/ppermute | solution.py:32
  72.2 0.3 collective-permute-done.25
  72.5 0.2 collective-permute-start.27
  72.7 1.5 %collective-permute-done.19 = bf16[1,80,512]{2,1,0:T(8,128)(2,1)S(1)} collective-permute-done((bf16[1,80,512]{2,1,0:T(8,128)(2,1)S(1)}, bf16[1,80,512]{2,1,0:T(8,128)(2,1)S(1)}, u32[]{:S(2)}, u32[]{:S(2)}) %collective-permute-start.19) | collective-permute-done | bytes 81952 | tf_op jit(solution)/shard_map/ppermute | solution.py:32
  74.3 1.9 %collective-permute-start.23 = (bf16[4,80,1024]{2,1,0:T(8,128)(2,1)S(1)}, bf16[4,80,1024]{2,1,0:T(8,128)(2,1)S(1)}, u32[]{:S(2)}, u32[]{:S(2)}) collective-permute-start(bf16[4,80,1024]{2,1,0:T(8,128)(2,1)S(1)} %maximum_maximum_fusion.a0), channel_id=1, source_target_pairs={{0,3},{1,0},{2,1},{3,2},{4,7},{5,4},{6,5},{7,6},{8,11},{9,8},{10,9... | collective-permute-start | bytes 1966088 | tf_op jit(solution)/shard_map/ppermute | solution.py:32
  76.2 1.0 collective-permute-done.27
  77.3 2.0 %collective-permute-start.30 = (bf16[4,80,1024]{2,1,0:T(8,128)(2,1)S(1)}, bf16[4,80,1024]{2,1,0:T(8,128)(2,1)S(1)}, u32[]{:S(2)}, u32[]{:S(2)}) collective-permute-start(bf16[4,80,1024]{2,1,0:T(8,128)(2,1)S(1)} %maximum_maximum_fusion.1.b0), channel_id=1, source_target_pairs={{0,24},{8,0},{16,8},{24,16},{1,25},{9,1},{17,9},{25,17},{2,26},{10... | collective-permute-start | bytes 1966088 | tf_op jit(solution)/shard_map/ppermute | solution.py:32
  79.3 7.7 %collective-permute-done.23.a2 = bf16[4,80,1024]{2,1,0:T(8,128)(2,1)S(1)} collective-permute-done((bf16[4,80,1024]{2,1,0:T(8,128)(2,1)S(1)}, bf16[4,80,1024]{2,1,0:T(8,128)(2,1)S(1)}, u32[]{:S(2)}, u32[]{:S(2)}) %collective-permute-start.23) | collective-permute-done | bytes 655392 | tf_op jit(solution)/shard_map/ppermute | solution.py:32
  87.0 3.4 %collective-permute-start.24 = (bf16[2,80,1024]{2,1,0:T(8,128)(2,1)S(1)}, bf16[2,80,1024]{2,1,0:T(8,128)(2,1)S(1)}, u32[]{:S(2)}, u32[]{:S(2)}) collective-permute-start(bf16[2,80,1024]{2,1,0:T(8,128)(2,1)S(1)} %slice.195), channel_id=1, source_target_pairs={{0,3},{1,0},{2,1},{3,2},{4,7},{5,4},{6,5},{7,6},{8,11},{9,8},{10,9... | collective-permute-start | bytes 983048 | tf_op jit(solution)/shard_map/ppermute | solution.py:32
  90.6 1.7 %collective-permute-start.32 = (bf16[2,80,1024]{2,1,0:T(8,128)(2,1)S(1)}, bf16[2,80,1024]{2,1,0:T(8,128)(2,1)S(1)}, u32[]{:S(2)}, u32[]{:S(2)}) collective-permute-start(bf16[2,80,1024]{2,1,0:T(8,128)(2,1)S(1)} %slice.199), channel_id=1, source_target_pairs={{0,24},{8,0},{16,8},{24,16},{1,25},{9,1},{17,9},{25,17},{2,26},{10... | collective-permute-start | bytes 983048 | tf_op jit(solution)/shard_map/ppermute | solution.py:32
  92.4 3.6 %gram_first.1 = (f32[1024,1024]{1,0:T(8,128)S(1)}, bf16[4,4,80,1024]{3,2,1,0:T(8,128)(2,1)S(1)}, bf16[4,4,80,1024]{3,2,1,0:T(8,128)(2,1)S(1)}) custom-call(s32[4]{0:T(128)S(1)} %pad_add_fusion.at_ref, bf16[4,80,1024]{2,1,0:T(8,128)(2,1)S(1)} %maximum_maximum_fusion.a0, bf16[4,80,1024]{2,1,0:T(8,128)(2,1)S(1)} %collective-permute-done.21.a1, ...), custom_call_target="tpu_custom_call" | custom-call | flops 2684354560 | bytes 2621440 | tf_op jit(solution)/shard_map/gram_first/pallas_call | solution.py:157
  96.1 2.4 %collective-permute-done.22.low = bf16[2,80,1024]{2,1,0:T(8,128)(2,1)S(1)} collective-permute-done((bf16[2,80,1024]{2,1,0:T(8,128)(2,1)S(1)}, bf16[2,80,1024]{2,1,0:T(8,128)(2,1)S(1)}, u32[]{:S(2)}, u32[]{:S(2)}) %collective-permute-start.22) | collective-permute-done | bytes 327712 | tf_op jit(solution)/shard_map/ppermute | solution.py:32
  98.4 1.6 %gram_more.2 = (f32[1024,1024]{1,0:T(8,128)S(1)}, bf16[4,4,80,1024]{3,2,1,0:T(8,128)(2,1)S(1)}) custom-call(s32[4]{0:T(128)S(1)} %pad_add_fusion.at_ref, bf16[2,80,1024]{2,1,0:T(8,128)(2,1)S(1)} %collective-permute-done.22.low, bf16[2,80,1024]{2,1,0:T(8,128)(2,1)S(1)} %collective-permute-done.24.high, f32[1024,1024]{1,0:T(8,128)S(1)} %get-tuple-element.68.acc_ref, ...), custom_call_target="tpu_custom_call" | custom-call | flops 503316480 | bytes 8388608 | tf_op jit(solution)/shard_map/gram_more/pallas_call | solution.py:191
  100.0 0.9 collective-permute-done.31.low
  100.9 1.6 %gram_more.3 = (bf16[1024,1024]{1,0:T(8,128)(2,1)S(1)}, bf16[4,4,80,1024]{3,2,1,0:T(8,128)(2,1)S(1)}) custom-call(s32[4]{0:T(128)S(1)} %pad_add_fusion.at_ref, bf16[2,80,1024]{2,1,0:T(8,128)(2,1)S(1)} %collective-permute-done.31.low, bf16[2,80,1024]{2,1,0:T(8,128)(2,1)S(1)} %collective-permute-done.32.high, f32[1024,1024]{1,0:T(8,128)S(1)} %get-tuple-element.71.acc_ref, ...), custom_call_target="tpu_custom_call" | custom-call | flops 503316480 | bytes 8388608 | tf_op jit(solution)/shard_map/gram_more/pallas_call | solution.py:191
  102.6 6.5 %collective-permute-start.34 = (bf16[1024,1024]{1,0:T(8,128)(2,1)S(1)}, bf16[1024,1024]{1,0:T(8,128)(2,1)S(1)}, u32[]{:S(2)}, u32[]{:S(2)}) collective-permute-start(bf16[1024,1024]{1,0:T(8,128)(2,1)S(1)} %get-tuple-element.85.own_ref), channel_id=1, source_target_pairs={{0,32},{32,0},{1,33},{33,1},{2,34},{34,2},{3,35},{35,3},{4,36},{36... | collective-permute-start | bytes 6291464 | tf_op jit(solution)/shard_map/ppermute | solution.py:32
  109.1 2.8 %coeff.2 = bf16[400,1024]{1,0:T(8,128)(2,1)S(1)} custom-call(s32[4]{0:T(128)S(1)} %pad_add_fusion.at_ref, bf16[1280,1024]{1,0:T(8,128)(2,1)S(1)} %bitcast.50, bf16[1280,1024]{1,0:T(8,128)(2,1)S(1)} %bitcast.53, bf16[800,1280]{1,0:T(8,128)(2,1)S(1)} %get-tuple-element.77.pool0_ref, bf16[800,1280]{1,0:T(8,128)(2,1)S(1)} %get-tuple-element.78.pool1_ref), custom_call_target="tpu_custom_call" | custom-call | flops 2097152000 | bytes 4096000 | tf_op jit(solution)/shard_map/coeff/pallas_call | solution.py:223
  111.9 0.1 collective-permute-start.33
  112.0 2.9 %coeff.3 = bf16[400,1024]{1,0:T(8,128)(2,1)S(1)} custom-call(s32[4]{0:T(128)S(1)} %pad_add_fusion.at_ref, bf16[1280,1024]{1,0:T(8,128)(2,1)S(1)} %bitcast.51, bf16[1280,1024]{1,0:T(8,128)(2,1)S(1)} %bitcast.54, bf16[800,1280]{1,0:T(8,128)(2,1)S(1)} %get-tuple-element.77.pool0_ref, bf16[800,1280]{1,0:T(8,128)(2,1)S(1)} %get-tuple-element.78.pool1_ref), custom_call_target="tpu_custom_call" | custom-call | flops 2097152000 | bytes 4096000 | tf_op jit(solution)/shard_map/coeff/pallas_call | solution.py:223
  114.9 0.3 add_convert_fusion.2.chip_ref
  115.2 1.1 collective-permute-start.35
  116.3 20.3 %schulz.1 = (bf16[1024,1024]{1,0:T(8,128)(2,1)S(1)}, f32[8,128]{1,0:T(8,128)S(1)}) custom-call(bf16[1024,1024]{1,0:T(8,128)(2,1)S(1)} %get-tuple-element.85.own_ref, bf16[1024,1024]{1,0:T(8,128)(2,1)S(1)} %collective-permute-done.34.other_ref), custom_call_target="tpu_custom_call" | custom-call | flops 25769803776 | bytes 8388608 | tf_op jit(solution)/shard_map/schulz/pallas_call | solution.py:283
  136.7 1.9 %third.1.third_ref = bf16[400,1024]{1,0:T(8,128)(2,1)S(1)} custom-call(bf16[400,1024]{1,0:T(8,128)(2,1)S(1)} %add_convert_fusion.2.chip_ref, bf16[400,1024]{1,0:T(8,128)(2,1)S(1)} %collective-permute-done.35.over_ref, bf16[1024,1024]{1,0:T(8,128)(2,1)S(1)} %get-tuple-element.89.z_ref, f32[8,128]{1,0:T(8,128)S(1)} %get-tuple-element.90.frob_ref), custom_call_target="tpu_custom_call" | custom-call | tf_op jit(solution)/shard_map/third/pallas_call | solution.py:308
  138.6 1.1 collective-permute-start.36
  139.7 2.1 %merge_own.1 = (bf16[400,1280]{1,0:T(8,128)(2,1)S(1)}, bf16[1024,1280]{1,0:T(8,128)(2,1)S(1)}) custom-call(s32[4]{0:T(128)S(1)} %pad_add_fusion.at_ref, bf16[400,1024]{1,0:T(8,128)(2,1)S(1)} %third.1.third_ref, bf16[1280,1024]{1,0:T(8,128)(2,1)S(1)} %bitcast.52, bf16[1280,1024]{1,0:T(8,128)(2,1)S(1)} %bitcast.55), custom_call_target="tpu_custom_call" | custom-call | flops 1048576000 | bytes 2621440 | tf_op jit(solution)/shard_map/merge_own/pallas_call | solution.py:331
  141.7 2.6 %merge.1 = bf16[800,1280]{1,0:T(8,128)(2,1)} custom-call(s32[4]{0:T(128)S(1)} %pad_add_fusion.at_ref, bf16[400,1024]{1,0:T(8,128)(2,1)S(1)} %collective-permute-done.36.third_ref, bf16[1024,1280]{1,0:T(8,128)(2,1)S(1)} %get-tuple-element.91.turned_ref, bf16[400,1280]{1,0:T(8,128)(2,1)S(1)} %get-tuple-element.92.own_ref), custom_call_target="tpu_custom_call" | custom-call | tf_op jit(solution)/shard_map/merge/pallas_call | solution.py:364
  (54 shorter events, 1.2 us)
Async XLA Ops:
  0.1 0.9 copy-start
  11.2 44.1 %collective-permute-start.16 = (bf16[2,800,1280]{2,1,0:T(8,128)(2,1)}, bf16[2,800,1280]{2,1,0:T(8,128)(2,1)S(1)}, u32[]{:S(2)}, u32[]{:S(2)}) collective-permute-start(bf16[2,800,1280]{2,1,0:T(8,128)(2,1)} %get-tuple-element.64), channel_id=1, source_target_pairs={{0,32},{32,0},{1,33},{33,1},{2,34},{34,2},{3,35},{35,3},{4,36},{36... | collective-permute-start | bytes 12288008 | tf_op jit(solution)/shard_map/ppermute | solution.py:32
  12.8 7.4 %collective-permute-start.8 = (bf16[2,4,80,128]{3,2,1,0:T(8,128)(2,1)S(1)}, bf16[2,4,80,128]{3,2,1,0:T(8,128)(2,1)S(1)}, u32[]{:S(2)}, u32[]{:S(2)}) collective-permute-start(bf16[2,4,80,128]{3,2,1,0:T(8,128)(2,1)S(1)} %get-tuple-element.61), channel_id=1, source_target_pairs={{0,3},{1,0},{2,1},{3,2},{4,7},{5,4},{6,5},{7,6},{8,11},{9,8},{10,9... | collective-permute-start | bytes 491528 | tf_op jit(solution)/shard_map/ppermute | solution.py:32
  16.7 10.3 %collective-permute-start = (bf16[2,4,80,128]{3,2,1,0:T(8,128)(2,1)S(1)}, bf16[2,4,80,128]{3,2,1,0:T(8,128)(2,1)S(1)}, u32[]{:S(2)}, u32[]{:S(2)}) collective-permute-start(bf16[2,4,80,128]{3,2,1,0:T(8,128)(2,1)S(1)} %get-tuple-element.54), channel_id=1, source_target_pairs={{0,8},{8,16},{16,24},{24,0},{1,9},{9,17},{17,25},{25,1},{2,10},{10... | collective-permute-start | bytes 491528 | tf_op jit(solution)/shard_map/ppermute | solution.py:32
  17.9 7.6 %collective-permute-start.2 = (bf16[2,4,80,128]{3,2,1,0:T(8,128)(2,1)S(1)}, bf16[2,4,80,128]{3,2,1,0:T(8,128)(2,1)S(1)}, u32[]{:S(2)}, u32[]{:S(2)}) collective-permute-start(bf16[2,4,80,128]{3,2,1,0:T(8,128)(2,1)S(1)} %get-tuple-element.56), channel_id=1, source_target_pairs={{0,24},{8,0},{16,8},{24,16},{1,25},{9,1},{17,9},{25,17},{2,26},{10... | collective-permute-start | bytes 491528 | tf_op jit(solution)/shard_map/ppermute | solution.py:32
  19.3 6.0 %collective-permute-start.6 = (bf16[2,4,80,128]{3,2,1,0:T(8,128)(2,1)S(1)}, bf16[2,4,80,128]{3,2,1,0:T(8,128)(2,1)S(1)}, u32[]{:S(2)}, u32[]{:S(2)}) collective-permute-start(bf16[2,4,80,128]{3,2,1,0:T(8,128)(2,1)S(1)} %get-tuple-element.59), channel_id=1, source_target_pairs={{0,1},{1,2},{2,3},{3,0},{4,5},{5,6},{6,7},{7,4},{8,9},{9,10},{10,1... | collective-permute-start | bytes 491528 | tf_op jit(solution)/shard_map/ppermute | solution.py:32
  20.3 9.6 %collective-permute-start.9 = (bf16[4,4,80,128]{3,2,1,0:T(8,128)(2,1)S(1)}, bf16[4,4,80,128]{3,2,1,0:T(8,128)(2,1)S(1)}, u32[]{:S(2)}, u32[]{:S(2)}) collective-permute-start(bf16[4,4,80,128]{3,2,1,0:T(8,128)(2,1)S(1)} %fusion.5), channel_id=1, source_target_pairs={{0,3},{1,0},{2,1},{3,2},{4,7},{5,4},{6,5},{7,6},{8,11},{9,8},{10,9... | collective-permute-start | bytes 983048 | tf_op jit(solution)/shard_map/ppermute | solution.py:32
  25.4 8.7 %collective-permute-start.7 = (bf16[4,4,80,128]{3,2,1,0:T(8,128)(2,1)S(1)}, bf16[4,4,80,128]{3,2,1,0:T(8,128)(2,1)S(1)}, u32[]{:S(2)}, u32[]{:S(2)}) collective-permute-start(bf16[4,4,80,128]{3,2,1,0:T(8,128)(2,1)S(1)} %fusion.4), channel_id=1, source_target_pairs={{0,1},{1,2},{2,3},{3,0},{4,5},{5,6},{6,7},{7,4},{8,9},{9,10},{10,1... | collective-permute-start | bytes 983048 | tf_op jit(solution)/shard_map/ppermute | solution.py:32
  25.6 8.7 %collective-permute-start.3 = (bf16[4,4,80,128]{3,2,1,0:T(8,128)(2,1)S(1)}, bf16[4,4,80,128]{3,2,1,0:T(8,128)(2,1)S(1)}, u32[]{:S(2)}, u32[]{:S(2)}) collective-permute-start(bf16[4,4,80,128]{3,2,1,0:T(8,128)(2,1)S(1)} %fusion.3), channel_id=1, source_target_pairs={{0,24},{8,0},{16,8},{24,16},{1,25},{9,1},{17,9},{25,17},{2,26},{10... | collective-permute-start | bytes 983048 | tf_op jit(solution)/shard_map/ppermute | solution.py:32
  27.0 8.4 %collective-permute-start.1 = (bf16[4,4,80,128]{3,2,1,0:T(8,128)(2,1)S(1)}, bf16[4,4,80,128]{3,2,1,0:T(8,128)(2,1)S(1)}, u32[]{:S(2)}, u32[]{:S(2)}) collective-permute-start(bf16[4,4,80,128]{3,2,1,0:T(8,128)(2,1)S(1)} %fusion.2), channel_id=1, source_target_pairs={{0,8},{8,16},{16,24},{24,0},{1,9},{9,17},{17,25},{25,1},{2,10},{10... | collective-permute-start | bytes 983048 | tf_op jit(solution)/shard_map/ppermute | solution.py:32
  34.1 21.3 %copy-start.1 = (bf16[2,800,1280]{2,1,0:T(8,128)(2,1)S(1)}, bf16[2,800,1280]{2,1,0:T(8,128)(2,1)}, u32[]{:S(2)}) copy-start(bf16[2,800,1280]{2,1,0:T(8,128)(2,1)} %get-tuple-element.63) | copy-start | bytes 12288004
  34.2 4.2 %collective-permute-start.10 = (bf16[2,4,80,128]{3,2,1,0:T(8,128)(2,1)S(1)}, bf16[2,4,80,128]{3,2,1,0:T(8,128)(2,1)S(1)}, u32[]{:S(2)}, u32[]{:S(2)}) collective-permute-start(bf16[2,4,80,128]{3,2,1,0:T(8,128)(2,1)S(1)} %add_convert_fusion.5), channel_id=1, source_target_pairs={{0,8},{8,0},{16,24},{24,16},{1,9},{9,1},{17,25},{25,17},{2,10},{10... | collective-permute-start | bytes 491528 | tf_op jit(solution)/shard_map/ppermute | solution.py:396
  35.5 4.3 %collective-permute-start.4 = (bf16[2,4,80,128]{3,2,1,0:T(8,128)(2,1)S(1)}, bf16[2,4,80,128]{3,2,1,0:T(8,128)(2,1)S(1)}, u32[]{:S(2)}, u32[]{:S(2)}) collective-permute-start(bf16[2,4,80,128]{3,2,1,0:T(8,128)(2,1)S(1)} %add_convert_fusion.8), channel_id=1, source_target_pairs={{0,1},{1,0},{2,3},{3,2},{4,5},{5,4},{6,7},{7,6},{8,9},{9,8},{10,11... | collective-permute-start | bytes 491528 | tf_op jit(solution)/shard_map/ppermute | solution.py:396
  38.5 4.6 %collective-permute-start.11 = (bf16[4,80,128]{2,1,0:T(8,128)(2,1)S(1)}, bf16[4,80,128]{2,1,0:T(8,128)(2,1)S(1)}, u32[]{:S(2)}, u32[]{:S(2)}) collective-permute-start(bf16[4,80,128]{2,1,0:T(8,128)(2,1)S(1)} %fusion.12), channel_id=1, source_target_pairs={{0,24},{24,0},{8,16},{16,8},{1,25},{25,1},{9,17},{17,9},{2,26},{26... | collective-permute-start | bytes 245768 | tf_op jit(solution)/shard_map/ppermute | solution.py:398
  39.9 4.6 %collective-permute-start.5 = (bf16[4,80,128]{2,1,0:T(8,128)(2,1)S(1)}, bf16[4,80,128]{2,1,0:T(8,128)(2,1)S(1)}, u32[]{:S(2)}, u32[]{:S(2)}) collective-permute-start(bf16[4,80,128]{2,1,0:T(8,128)(2,1)S(1)} %fusion.10), channel_id=1, source_target_pairs={{0,3},{3,0},{1,2},{2,1},{4,7},{7,4},{5,6},{6,5},{8,11},{11,8},{9,1... | collective-permute-start | bytes 245768 | tf_op jit(solution)/shard_map/ppermute | solution.py:398
  44.6 6.3 %collective-permute-start.12 = (bf16[2,80,256]{2,1,0:T(8,128)(2,1)S(1)}, bf16[2,80,256]{2,1,0:T(8,128)(2,1)S(1)}, u32[]{:S(2)}, u32[]{:S(2)}) collective-permute-start(bf16[2,80,256]{2,1,0:T(8,128)(2,1)S(1)} %select_bitcast_fusion), channel_id=1, source_target_pairs={{0,32},{32,0},{1,33},{33,1},{2,34},{34,2},{3,35},{35,3},{4,36},{36... | collective-permute-start | bytes 245768 | tf_op jit(solution)/shard_map/ppermute | solution.py:32
  50.9 6.0 %collective-permute-start.14 = (bf16[2,80,512]{2,1,0:T(8,128)(2,1)S(1)}, bf16[2,80,512]{2,1,0:T(8,128)(2,1)S(1)}, u32[]{:S(2)}, u32[]{:S(2)}) collective-permute-start(bf16[2,80,512]{2,1,0:T(8,128)(2,1)S(1)} %pad_maximum_fusion.2), channel_id=1, source_target_pairs={{0,68},{4,0},{64,4},{68,64},{1,69},{5,1},{65,5},{69,65},{2,70},{6,... | collective-permute-start | bytes 491528 | tf_op jit(solution)/shard_map/ppermute | solution.py:32
  53.7 7.3 %collective-permute-start.13 = (bf16[2,80,512]{2,1,0:T(8,128)(2,1)S(1)}, bf16[2,80,512]{2,1,0:T(8,128)(2,1)S(1)}, u32[]{:S(2)}, u32[]{:S(2)}) collective-permute-start(bf16[2,80,512]{2,1,0:T(8,128)(2,1)S(1)} %pad_maximum_fusion.2), channel_id=1, source_target_pairs={{0,4},{4,64},{64,68},{68,0},{1,5},{5,65},{65,69},{69,1},{2,6},{6,6... | collective-permute-start | bytes 491528 | tf_op jit(solution)/shard_map/ppermute | solution.py:32
  53.7 8.8 %collective-permute-start.15 = (bf16[2,80,512]{2,1,0:T(8,128)(2,1)S(1)}, bf16[2,80,512]{2,1,0:T(8,128)(2,1)S(1)}, u32[]{:S(2)}, u32[]{:S(2)}) collective-permute-start(bf16[2,80,512]{2,1,0:T(8,128)(2,1)S(1)} %pad_maximum_fusion.2), channel_id=1, source_target_pairs={{0,64},{4,68},{64,0},{68,4},{1,65},{5,69},{65,1},{69,5},{2,66},{6,... | collective-permute-start | bytes 491528 | tf_op jit(solution)/shard_map/ppermute | solution.py:32
  62.8 4.2 %collective-permute-start.18 = (bf16[1,80,1024]{2,1,0:T(8,128)(2,1)S(1)}, bf16[1,80,1024]{2,1,0:T(8,128)(2,1)S(1)}, u32[]{:S(2)}, u32[]{:S(2)}) collective-permute-start(bf16[1,80,1024]{2,1,0:T(8,128)(2,1)S(1)} %get-tuple-element.99), channel_id=1, source_target_pairs={{0,24},{8,0},{16,8},{24,16},{1,25},{9,1},{17,9},{25,17},{2,26},{10... | collective-permute-start | bytes 491528 | tf_op jit(solution)/shard_map/ppermute | solution.py:32
  64.2 5.4 %collective-permute-start.17 = (bf16[1,80,1024]{2,1,0:T(8,128)(2,1)S(1)}, bf16[1,80,1024]{2,1,0:T(8,128)(2,1)S(1)}, u32[]{:S(2)}, u32[]{:S(2)}) collective-permute-start(bf16[1,80,1024]{2,1,0:T(8,128)(2,1)S(1)} %get-tuple-element.99), channel_id=1, source_target_pairs={{0,8},{8,16},{16,24},{24,0},{1,9},{9,17},{17,25},{25,1},{2,10},{10... | collective-permute-start | bytes 491528 | tf_op jit(solution)/shard_map/ppermute | solution.py:32
  64.3 5.4 %collective-permute-start.26 = (bf16[1,80,1024]{2,1,0:T(8,128)(2,1)S(1)}, bf16[1,80,1024]{2,1,0:T(8,128)(2,1)S(1)}, u32[]{:S(2)}, u32[]{:S(2)}) collective-permute-start(bf16[1,80,1024]{2,1,0:T(8,128)(2,1)S(1)} %get-tuple-element.98), channel_id=1, source_target_pairs={{0,3},{1,0},{2,1},{3,2},{4,7},{5,4},{6,5},{7,6},{8,11},{9,8},{10,9... | collective-permute-start | bytes 491528 | tf_op jit(solution)/shard_map/ppermute | solution.py:32
  66.9 5.7 %collective-permute-start.25 = (bf16[1,80,1024]{2,1,0:T(8,128)(2,1)S(1)}, bf16[1,80,1024]{2,1,0:T(8,128)(2,1)S(1)}, u32[]{:S(2)}, u32[]{:S(2)}) collective-permute-start(bf16[1,80,1024]{2,1,0:T(8,128)(2,1)S(1)} %get-tuple-element.98), channel_id=1, source_target_pairs={{0,1},{1,2},{2,3},{3,0},{4,5},{5,6},{6,7},{7,4},{8,9},{9,10},{10,1... | collective-permute-start | bytes 491528 | tf_op jit(solution)/shard_map/ppermute | solution.py:32
  67.0 5.7 %collective-permute-start.20 = (bf16[1,80,512]{2,1,0:T(8,128)(2,1)S(1)}, bf16[1,80,512]{2,1,0:T(8,128)(2,1)S(1)}, u32[]{:S(2)}, u32[]{:S(2)}) collective-permute-start(bf16[1,80,512]{2,1,0:T(8,128)(2,1)S(1)} %slice.193), channel_id=1, source_target_pairs={{0,24},{8,0},{16,8},{24,16},{1,25},{9,1},{17,9},{25,17},{2,26},{10... | collective-permute-start | bytes 245768 | tf_op jit(solution)/shard_map/ppermute | solution.py:32
  69.6 4.6 %collective-permute-start.19 = (bf16[1,80,512]{2,1,0:T(8,128)(2,1)S(1)}, bf16[1,80,512]{2,1,0:T(8,128)(2,1)S(1)}, u32[]{:S(2)}, u32[]{:S(2)}) collective-permute-start(bf16[1,80,512]{2,1,0:T(8,128)(2,1)S(1)} %slice.192), channel_id=1, source_target_pairs={{0,8},{8,16},{16,24},{24,0},{1,9},{9,17},{17,25},{25,1},{2,10},{10... | collective-permute-start | bytes 245768 | tf_op jit(solution)/shard_map/ppermute | solution.py:32
  69.7 6.4 %collective-permute-start.28 = (bf16[1,80,512]{2,1,0:T(8,128)(2,1)S(1)}, bf16[1,80,512]{2,1,0:T(8,128)(2,1)S(1)}, u32[]{:S(2)}, u32[]{:S(2)}) collective-permute-start(bf16[1,80,512]{2,1,0:T(8,128)(2,1)S(1)} %slice.197), channel_id=1, source_target_pairs={{0,3},{1,0},{2,1},{3,2},{4,7},{5,4},{6,5},{7,6},{8,11},{9,8},{10,9... | collective-permute-start | bytes 245768 | tf_op jit(solution)/shard_map/ppermute | solution.py:32
  72.5 4.7 %collective-permute-start.27 = (bf16[1,80,512]{2,1,0:T(8,128)(2,1)S(1)}, bf16[1,80,512]{2,1,0:T(8,128)(2,1)S(1)}, u32[]{:S(2)}, u32[]{:S(2)}) collective-permute-start(bf16[1,80,512]{2,1,0:T(8,128)(2,1)S(1)} %slice.196), channel_id=1, source_target_pairs={{0,1},{1,2},{2,3},{3,0},{4,5},{5,6},{6,7},{7,4},{8,9},{9,10},{10,1... | collective-permute-start | bytes 245768 | tf_op jit(solution)/shard_map/ppermute | solution.py:32
  74.3 12.7 %collective-permute-start.23 = (bf16[4,80,1024]{2,1,0:T(8,128)(2,1)S(1)}, bf16[4,80,1024]{2,1,0:T(8,128)(2,1)S(1)}, u32[]{:S(2)}, u32[]{:S(2)}) collective-permute-start(bf16[4,80,1024]{2,1,0:T(8,128)(2,1)S(1)} %maximum_maximum_fusion.a0), channel_id=1, source_target_pairs={{0,3},{1,0},{2,1},{3,2},{4,7},{5,4},{6,5},{7,6},{8,11},{9,8},{10,9... | collective-permute-start | bytes 1966088 | tf_op jit(solution)/shard_map/ppermute | solution.py:32
  76.2 14.2 %collective-permute-start.21 = (bf16[4,80,1024]{2,1,0:T(8,128)(2,1)S(1)}, bf16[4,80,1024]{2,1,0:T(8,128)(2,1)S(1)}, u32[]{:S(2)}, u32[]{:S(2)}) collective-permute-start(bf16[4,80,1024]{2,1,0:T(8,128)(2,1)S(1)} %maximum_maximum_fusion.a0), channel_id=1, source_target_pairs={{0,1},{1,2},{2,3},{3,0},{4,5},{5,6},{6,7},{7,4},{8,9},{9,10},{10,1... | collective-permute-start | bytes 1966088 | tf_op jit(solution)/shard_map/ppermute | solution.py:32
  77.3 13.3 %collective-permute-start.30 = (bf16[4,80,1024]{2,1,0:T(8,128)(2,1)S(1)}, bf16[4,80,1024]{2,1,0:T(8,128)(2,1)S(1)}, u32[]{:S(2)}, u32[]{:S(2)}) collective-permute-start(bf16[4,80,1024]{2,1,0:T(8,128)(2,1)S(1)} %maximum_maximum_fusion.1.b0), channel_id=1, source_target_pairs={{0,24},{8,0},{16,8},{24,16},{1,25},{9,1},{17,9},{25,17},{2,26},{10... | collective-permute-start | bytes 1966088 | tf_op jit(solution)/shard_map/ppermute | solution.py:32
  79.3 13.0 %collective-permute-start.29 = (bf16[4,80,1024]{2,1,0:T(8,128)(2,1)S(1)}, bf16[4,80,1024]{2,1,0:T(8,128)(2,1)S(1)}, u32[]{:S(2)}, u32[]{:S(2)}) collective-permute-start(bf16[4,80,1024]{2,1,0:T(8,128)(2,1)S(1)} %maximum_maximum_fusion.1.b0), channel_id=1, source_target_pairs={{0,8},{8,16},{16,24},{24,0},{1,9},{9,17},{17,25},{25,1},{2,10},{10... | collective-permute-start | bytes 1966088 | tf_op jit(solution)/shard_map/ppermute | solution.py:32
  87.0 9.1 %collective-permute-start.24 = (bf16[2,80,1024]{2,1,0:T(8,128)(2,1)S(1)}, bf16[2,80,1024]{2,1,0:T(8,128)(2,1)S(1)}, u32[]{:S(2)}, u32[]{:S(2)}) collective-permute-start(bf16[2,80,1024]{2,1,0:T(8,128)(2,1)S(1)} %slice.195), channel_id=1, source_target_pairs={{0,3},{1,0},{2,1},{3,2},{4,7},{5,4},{6,5},{7,6},{8,11},{9,8},{10,9... | collective-permute-start | bytes 983048 | tf_op jit(solution)/shard_map/ppermute | solution.py:32
  90.4 8.0 %collective-permute-start.22 = (bf16[2,80,1024]{2,1,0:T(8,128)(2,1)S(1)}, bf16[2,80,1024]{2,1,0:T(8,128)(2,1)S(1)}, u32[]{:S(2)}, u32[]{:S(2)}) collective-permute-start(bf16[2,80,1024]{2,1,0:T(8,128)(2,1)S(1)} %slice.194), channel_id=1, source_target_pairs={{0,1},{1,2},{2,3},{3,0},{4,5},{5,6},{6,7},{7,4},{8,9},{9,10},{10,1... | collective-permute-start | bytes 983048 | tf_op jit(solution)/shard_map/ppermute | solution.py:32
  90.6 9.5 %collective-permute-start.32 = (bf16[2,80,1024]{2,1,0:T(8,128)(2,1)S(1)}, bf16[2,80,1024]{2,1,0:T(8,128)(2,1)S(1)}, u32[]{:S(2)}, u32[]{:S(2)}) collective-permute-start(bf16[2,80,1024]{2,1,0:T(8,128)(2,1)S(1)} %slice.199), channel_id=1, source_target_pairs={{0,24},{8,0},{16,8},{24,16},{1,25},{9,1},{17,9},{25,17},{2,26},{10... | collective-permute-start | bytes 983048 | tf_op jit(solution)/shard_map/ppermute | solution.py:32
  92.3 8.6 %collective-permute-start.31 = (bf16[2,80,1024]{2,1,0:T(8,128)(2,1)S(1)}, bf16[2,80,1024]{2,1,0:T(8,128)(2,1)S(1)}, u32[]{:S(2)}, u32[]{:S(2)}) collective-permute-start(bf16[2,80,1024]{2,1,0:T(8,128)(2,1)S(1)} %slice.198), channel_id=1, source_target_pairs={{0,8},{8,16},{16,24},{24,0},{1,9},{9,17},{17,25},{25,1},{2,10},{10... | collective-permute-start | bytes 983048 | tf_op jit(solution)/shard_map/ppermute | solution.py:32
  102.6 12.3 %collective-permute-start.34 = (bf16[1024,1024]{1,0:T(8,128)(2,1)S(1)}, bf16[1024,1024]{1,0:T(8,128)(2,1)S(1)}, u32[]{:S(2)}, u32[]{:S(2)}) collective-permute-start(bf16[1024,1024]{1,0:T(8,128)(2,1)S(1)} %get-tuple-element.85.own_ref), channel_id=1, source_target_pairs={{0,32},{32,0},{1,33},{33,1},{2,34},{34,2},{3,35},{35,3},{4,36},{36... | collective-permute-start | bytes 6291464 | tf_op jit(solution)/shard_map/ppermute | solution.py:32
  111.9 3.0 %collective-permute-start.33 = (bf16[400,1024]{1,0:T(8,128)(2,1)S(1)}, bf16[400,1024]{1,0:T(8,128)(2,1)S(1)}, u32[]{:S(2)}, u32[]{:S(2)}) collective-permute-start(bf16[400,1024]{1,0:T(8,128)(2,1)S(1)} %coeff.2), channel_id=1, source_target_pairs={{0,32},{32,0},{1,33},{33,1},{2,34},{34,2},{3,35},{35,3},{4,36},{36... | collective-permute-start | bytes 2457608 | tf_op jit(solution)/shard_map/ppermute | solution.py:32
  115.2 21.5 %collective-permute-start.35 = (bf16[400,1024]{1,0:T(8,128)(2,1)S(1)}, bf16[400,1024]{1,0:T(8,128)(2,1)S(1)}, u32[]{:S(2)}, u32[]{:S(2)}) collective-permute-start(bf16[400,1024]{1,0:T(8,128)(2,1)S(1)} %add_convert_fusion.2.chip_ref), channel_id=1, source_target_pairs={{0,64},{64,0},{1,65},{65,1},{2,66},{66,2},{3,67},{67,3},{4,68},{68... | collective-permute-start | bytes 2457608 | tf_op jit(solution)/shard_map/ppermute | solution.py:32
  138.6 3.1 %collective-permute-start.36 = (bf16[400,1024]{1,0:T(8,128)(2,1)S(1)}, bf16[400,1024]{1,0:T(8,128)(2,1)S(1)}, u32[]{:S(2)}, u32[]{:S(2)}) collective-permute-start(bf16[400,1024]{1,0:T(8,128)(2,1)S(1)} %third.1.third_ref), channel_id=1, source_target_pairs={{0,32},{32,0},{1,33},{33,1},{2,34},{34,2},{3,35},{35,3},{4,36},{36... | collective-permute-start | bytes 2457608 | tf_op jit(solution)/shard_map/ppermute | solution.py:32
